TPU v7x, 32 devices: a whole 2x2x4 slice. The times are simulated.
32 devices in a mesh: dp: 4 (over y, x), gx: 2 (over core), gy: 4 (over z).
Axes of the slice: x: 2, y: 2, z: 4, core: 2. Of those that a mesh axis runs over, the one named last changes fastest.
Arguments:
- inputs: bfloat16 [2, 4096, 2048], P(None, ('dp', 'gy'), 'gx'), may hold values from -6 to 6
- cotangent: bfloat16 [2, 4096, 2048], P(None, ('dp', 'gy'), 'gx'), may hold values from -6 to 6
- segments: int32 [2, 4096], P(None, 'dp'), may hold values from 0 to 3, as said below
- attention_gain: float32 [2, 2048], replicated, may hold values from 0.5 to 1.5
- query_weight: bfloat16 [2, 2048, 2048], P(None, 'gx', 'gy'), may hold values from -0.046875 to 0.046875
- key_weight: bfloat16 [2, 2048, 2048], P(None, 'gx', 'gy'), may hold values from -0.046875 to 0.046875
- value_weight: bfloat16 [2, 2048, 2048], P(None, 'gx', 'gy'), may hold values from -0.125 to 0.125
- mixing_weight: bfloat16 [2, 2048, 2048], P(None, 'gy', 'gx'), may hold values from -1 to 1
- relative_bias: float32 [2, 32, 32], replicated, may hold values from -6 to 6
- dense_gain: float32 [2, 2048], replicated, may hold values from 0.5 to 1.5
- gate_weight: bfloat16 [2, 2048, 5120], P(None, 'gx', 'gy'), may hold values from -0.125 to 0.125
- up_weight: bfloat16 [2, 2048, 5120], P(None, 'gx', 'gy'), may hold values from -0.125 to 0.125
- down_weight: bfloat16 [2, 5120, 2048], P(None, 'gy', 'gx'), may hold values from -0.078125 to 0.078125
Outputs:
- output: float32 [2, 4096, 2048], P(None, ('dp', 'gy'), 'gx')
- grad_inputs: float32 [2, 4096, 2048], P(None, ('dp', 'gy'), 'gx')
- grad_attention: float32 [2, 2048], replicated
- grad_query: float32 [2, 2048, 2048], P(None, 'gx', 'gy')
- grad_key: float32 [2, 2048, 2048], P(None, 'gx', 'gy')
- grad_value: float32 [2, 2048, 2048], P(None, 'gx', 'gy')
- grad_mixing: float32 [2, 2048, 2048], P(None, 'gy', 'gx')
- grad_relative: float32 [2, 32, 32], replicated
- grad_dense: float32 [2, 2048], replicated
- grad_gate: float32 [2, 2048, 5120], P(None, 'gx', 'gy')
- grad_up: float32 [2, 2048, 5120], P(None, 'gx', 'gy')
- grad_down: float32 [2, 5120, 2048], P(None, 'gy', 'gx')
Inputs may be any that keep to these rules, and one draw needn't show every extreme that they name: `segments`: within each sequence of 1024 tokens the numbers are 1, 2 and 3 for three documents in order, never falling, each document of 65 tokens or more, and the sequence ends in 1 to 128 padding tokens numbered 0.
All inputs are finite; a program needn't handle non-finite values.
Results may differ from a plain program's by a relative error of at most 0.023.
Values may be sent and summed in bfloat16 or wider, within the bound.
No kernel may reach another device: no remote copies, remote signals or barrier semaphores. Data moves between devices by JAX's collectives and lax.ppermute only.
A program may use at most 512 MiB of HBM per device.

v0:
```python
import jax
import jax.numpy as jnp
from jax import lax
from jax.sharding import PartitionSpec as P

D = 2048
H = 32
DH = 64
NB = 32
LAYERS = 2
MICRO = 2
LEN = 1024


THRESHOLDS = (12, 16, 23, 32, 46, 64, 91)
HIGH = lax.Precision.HIGHEST


def bucket_of(offset):
    distance = jnp.abs(offset)
    beyond = 8 + sum(((distance >= threshold).astype(jnp.int32) for threshold in THRESHOLDS))
    within = jnp.where(distance < 8, distance, beyond)
    return jnp.where(offset > 0, 16, 0) + within


def row_total(values):
    return lax.psum(values, "gx")


def token_gather(values):
    return lax.all_gather(values, "gy", axis=0, tiled=True)


def token_reduce(values):
    return lax.psum_scatter(values, "gy", scatter_dimension=0, tiled=True)


def head_reduce(values):
    return lax.psum_scatter(values, "gx", scatter_dimension=2, tiled=True)


def head_gather(values):
    return lax.all_gather(values, "gx", axis=2, tiled=True)


def hidden_reduce(values):
    return lax.psum_scatter(values, "gx", scatter_dimension=2, tiled=True)


def hidden_gather(values):
    return lax.all_gather(values, "gx", axis=2, tiled=True)


def project(acts, weights):
    return jnp.einsum("td,ndf->ntf", acts, weights, preferred_element_type=jnp.float32)


def project_back(grads, weights):
    return jnp.einsum("ntf,ndf->td", grads, weights, preferred_element_type=jnp.float32)


def weight_grad(acts, grads):
    return jnp.einsum("td,ntf->ndf", acts, grads, preferred_element_type=jnp.float32)


def smooth_gate(gate_in, up_in):
    return jax.nn.gelu(gate_in, approximate=True) * up_in


def norm_scale(hidden):
    total = row_total(jnp.sum(hidden * hidden, axis=1))
    return lax.rsqrt(total / D + 1e-06)


def norm_back(grad_norm, hidden, scale, gain):
    weighted = grad_norm * gain
    inner = row_total(jnp.sum(weighted * hidden, axis=1))
    cubed = scale * scale * scale * inner / D
    grad_hidden = scale[:, None] * weighted - hidden * cubed[:, None]
    gain_grad = jnp.sum(grad_norm * hidden * scale[:, None], axis=0)
    return (grad_hidden, gain_grad)


def offset_table(length):
    offset = jnp.arange(2 * length, dtype=jnp.int32) - (length - 1)
    buckets = bucket_of(offset)
    return (buckets[:, None] == jnp.arange(NB, dtype=jnp.int32)[None, :]).astype(jnp.float32)


def toeplitz(vector, length):
    heads = vector.shape[0]
    wide = jnp.broadcast_to(vector[:, None, :], (heads, length, 2 * length)).reshape(heads, -1)
    wide = wide[:, : length * (2 * length - 1)].reshape(heads, length, 2 * length - 1)
    return wide[:, :, length - 1 :]


def diagonal_sums(matrix, length):
    heads = matrix.shape[0]
    padded = jnp.pad(matrix, ((0, 0), (0, 0), (length - 1, 0))).reshape(heads, -1)
    padded = jnp.pad(padded, ((0, 0), (0, length))).reshape(heads, length, 2 * length)
    return jnp.sum(padded, axis=1)


def pair_mask(segment, length):
    same = (segment[:, :, None] == segment[:, None, :]) & (segment[:, None, :] != 0)
    places = jnp.arange(length, dtype=jnp.int32)
    return (same | (places[:, None] == places[None, :])[None])[:, None]


def split_heads(stacked, length, heads):
    count = stacked.shape[1] // length
    width = stacked.shape[2] // heads
    shaped = stacked.reshape(3, count, length, heads, width).transpose(0, 1, 3, 2, 4)
    return (shaped[0], shaped[1], shaped[2])


def scores_of(query, key_in, biases, allowed):
    raw = (
        jnp.einsum("shqd,shkd->shqk", query, key_in, preferred_element_type=jnp.float32)
        + biases[None]
    )
    return jnp.where(allowed, raw, -1000000000.0)


def attend(stacked, segment, biases, length):
    heads = biases.shape[0]
    query, key_in, value = split_heads(stacked, length, heads)
    allowed = pair_mask(segment.reshape(-1, length), length)
    scores = scores_of(query, key_in, biases, allowed)
    highest = jnp.max(scores, axis=-1, keepdims=True)
    expo = jnp.exp(scores - highest)
    total = jnp.sum(expo, axis=-1, keepdims=True)
    probs = (expo / total).astype(jnp.bfloat16)
    mixed_heads = jnp.einsum("shqk,shkd->shqd", probs, value, preferred_element_type=jnp.float32)
    mixed_heads = mixed_heads.astype(jnp.bfloat16).transpose(0, 2, 1, 3)
    mixed_heads = mixed_heads.reshape(stacked.shape[1], stacked.shape[2])
    return (mixed_heads, highest + jnp.log(total))


def attend_back(stacked, segment, biases, log_total, grad_mixed, length):
    heads = biases.shape[0]
    query, key_in, value = split_heads(stacked, length, heads)
    allowed = pair_mask(segment.reshape(-1, length), length)
    probs = jnp.exp(scores_of(query, key_in, biases, allowed) - log_total)
    count = stacked.shape[1] // length
    grad_out = grad_mixed.reshape(count, length, heads, -1).transpose(0, 2, 1, 3)
    grad_probs = jnp.einsum("shqd,shkd->shqk", grad_out, value, preferred_element_type=jnp.float32)
    grad_value = jnp.einsum(
        "shqk,shqd->shkd", probs.astype(jnp.bfloat16), grad_out, preferred_element_type=jnp.float32
    )
    delta_rows = jnp.sum(probs * grad_probs, axis=-1, keepdims=True)
    grad_scores = (probs * (grad_probs - delta_rows)).astype(jnp.bfloat16)
    grad_query = jnp.einsum(
        "shqk,shkd->shqd", grad_scores, key_in, preferred_element_type=jnp.float32
    )
    grad_key = jnp.einsum("shqk,shqd->shkd", grad_scores, query, preferred_element_type=jnp.float32)
    grads = jnp.stack((grad_query, grad_key, grad_value)).astype(jnp.bfloat16)
    grads = grads.transpose(0, 1, 3, 2, 4).reshape(stacked.shape)
    return (grads, jnp.sum(grad_scores, axis=0, dtype=jnp.float32))


def body(
    inputs,
    cotangent,
    segments,
    attention_gain,
    query_weight,
    key_weight,
    value_weight,
    mixing_weight,
    relative_bias,
    dense_gain,
    gate_weight,
    up_weight,
    down_weight,
):
    n_gx = lax.axis_size("gx")
    gx_index = lax.axis_index("gx")
    gy_index = lax.axis_index("gy")
    row_count = inputs.shape[1]
    col_count = inputs.shape[2]
    col_start = gx_index * col_count
    heads_dev = query_weight.shape[2] // (n_gx * DH)
    head_start = (gy_index * n_gx + gx_index) * heads_dev
    table_rows = offset_table(LEN)
    attn_weights = []
    dense_weights = []
    bias_mats = []
    for layer_index in range(LAYERS):
        attn_weights.append(
            jnp.stack(
                (query_weight[layer_index], key_weight[layer_index], value_weight[layer_index])
            )
        )
        dense_weights.append(jnp.stack((gate_weight[layer_index], up_weight[layer_index])))
        table_dev = lax.dynamic_slice_in_dim(relative_bias[layer_index], head_start, heads_dev, 1)
        vector = jnp.dot(table_rows, table_dev, precision=HIGH).T
        bias_mats.append(toeplitz(vector, LEN))
    attn_acc = [jnp.zeros(item.shape, jnp.float32) for item in attn_weights]
    dense_acc = [jnp.zeros(item.shape, jnp.float32) for item in dense_weights]
    mixing_acc = [jnp.zeros(mixing_weight.shape[1:], jnp.float32) for item in attn_weights]
    down_acc = [jnp.zeros(down_weight.shape[1:], jnp.float32) for item in attn_weights]
    gain_attn_acc = [jnp.zeros((col_count,), jnp.float32) for item in attn_weights]
    gain_dense_acc = [jnp.zeros((col_count,), jnp.float32) for item in attn_weights]
    offset_acc = [jnp.zeros((heads_dev, 2 * LEN), jnp.float32) for item in attn_weights]
    outputs = []
    input_grads = []
    for micro_index in range(MICRO):
        seg_all = segments[micro_index]
        row_segs = lax.dynamic_slice_in_dim(seg_all, gy_index * row_count, row_count)
        keep_rows = (row_segs != 0).astype(jnp.float32)[:, None]
        hidden = inputs[micro_index].astype(jnp.float32)
        saved = []
        for layer_index in range(LAYERS):
            gain_attn = lax.dynamic_slice_in_dim(attention_gain[layer_index], col_start, col_count)
            gain_dense = lax.dynamic_slice_in_dim(dense_gain[layer_index], col_start, col_count)
            scale_attn = norm_scale(hidden)
            normed = (hidden * scale_attn[:, None] * gain_attn).astype(jnp.bfloat16)
            normed_all = token_gather(normed)
            stacked = head_reduce(project(normed_all, attn_weights[layer_index])).astype(
                jnp.bfloat16
            )
            mixed_heads, log_total = attend(stacked, seg_all, bias_mats[layer_index], LEN)
            mixed_all = head_gather(mixed_heads[None])[0]
            branch = token_reduce(
                jnp.dot(mixed_all, mixing_weight[layer_index], preferred_element_type=jnp.float32)
            )
            hidden_mid = hidden + branch
            scale_dense = norm_scale(hidden_mid)
            dense_in = (hidden_mid * scale_dense[:, None] * gain_dense).astype(jnp.bfloat16)
            dense_all = token_gather(dense_in)
            gate_up = hidden_reduce(project(dense_all, dense_weights[layer_index]))
            activated = smooth_gate(gate_up[0], gate_up[1]).astype(jnp.bfloat16)
            active_all = hidden_gather(activated[None])[0]
            dense_out = token_reduce(
                jnp.dot(active_all, down_weight[layer_index], preferred_element_type=jnp.float32)
            )
            hidden_next = hidden_mid + dense_out
            saved.append(
                (
                    hidden,
                    scale_attn,
                    normed_all,
                    stacked,
                    log_total,
                    mixed_all,
                    hidden_mid,
                    scale_dense,
                    dense_all,
                    gate_up,
                    active_all,
                )
            )
            hidden = hidden_next
        outputs.append(hidden * keep_rows)
        grad_hidden = cotangent[micro_index].astype(jnp.float32) * keep_rows
        for layer_index in reversed(range(LAYERS)):
            (
                hidden,
                scale_attn,
                normed_all,
                stacked,
                log_total,
                mixed_all,
                hidden_mid,
                scale_dense,
                dense_all,
                gate_up,
                active_all,
            ) = saved[layer_index]
            gain_attn = lax.dynamic_slice_in_dim(attention_gain[layer_index], col_start, col_count)
            gain_dense = lax.dynamic_slice_in_dim(dense_gain[layer_index], col_start, col_count)
            grad_branch = token_gather(grad_hidden.astype(jnp.bfloat16))
            down_acc[layer_index] = down_acc[layer_index] + jnp.einsum(
                "tf,td->fd", active_all, grad_branch, preferred_element_type=jnp.float32
            )
            grad_active = jnp.einsum(
                "td,fd->tf",
                grad_branch,
                down_weight[layer_index],
                preferred_element_type=jnp.float32,
            )
            grad_active = hidden_reduce(grad_active[None])[0]
            unused, pullback = jax.vjp(smooth_gate, gate_up[0], gate_up[1])
            grad_gate, grad_up = pullback(grad_active)
            grad_pair = jnp.stack((grad_gate, grad_up)).astype(jnp.bfloat16)
            grad_pair_all = hidden_gather(grad_pair)
            dense_acc[layer_index] = dense_acc[layer_index] + weight_grad(dense_all, grad_pair_all)
            grad_dense_in = token_reduce(project_back(grad_pair_all, dense_weights[layer_index]))
            grad_norm_mid, gain_part = norm_back(grad_dense_in, hidden_mid, scale_dense, gain_dense)
            gain_dense_acc[layer_index] = gain_dense_acc[layer_index] + gain_part
            grad_mid = grad_hidden + grad_norm_mid
            grad_attn_out = token_gather(grad_mid.astype(jnp.bfloat16))
            mixing_acc[layer_index] = mixing_acc[layer_index] + jnp.einsum(
                "tc,td->cd", mixed_all, grad_attn_out, preferred_element_type=jnp.float32
            )
            grad_mixed = jnp.einsum(
                "td,cd->tc",
                grad_attn_out,
                mixing_weight[layer_index],
                preferred_element_type=jnp.float32,
            )
            grad_mixed = head_reduce(grad_mixed[None])[0].astype(jnp.bfloat16)
            grad_stacked, score_total = attend_back(
                stacked, seg_all, bias_mats[layer_index], log_total, grad_mixed, LEN
            )
            offset_acc[layer_index] = offset_acc[layer_index] + diagonal_sums(score_total, LEN)
            grad_stacked_all = head_gather(grad_stacked)
            attn_acc[layer_index] = attn_acc[layer_index] + weight_grad(
                normed_all, grad_stacked_all
            )
            grad_normed = token_reduce(project_back(grad_stacked_all, attn_weights[layer_index]))
            grad_norm_in, gain_part = norm_back(grad_normed, hidden, scale_attn, gain_attn)
            gain_attn_acc[layer_index] = gain_attn_acc[layer_index] + gain_part
            grad_hidden = grad_mid + grad_norm_in
        input_grads.append(grad_hidden)
    attn_grads = jnp.stack(attn_acc)
    dense_grads = jnp.stack(dense_acc)
    summed = lax.psum(
        (
            attn_grads[:, 0],
            attn_grads[:, 1],
            attn_grads[:, 2],
            jnp.stack(mixing_acc),
            dense_grads[:, 0],
            dense_grads[:, 1],
            jnp.stack(down_acc),
        ),
        "dp",
    )
    bucket_grads = jnp.einsum("ob,lho->lbh", table_rows, jnp.stack(offset_acc), precision=HIGH)
    bias_full = lax.dynamic_update_slice_in_dim(
        jnp.zeros((LAYERS, NB, H), jnp.float32), bucket_grads, head_start, 2
    )
    attn_gain_full = lax.dynamic_update_slice_in_dim(
        jnp.zeros((LAYERS, D), jnp.float32), jnp.stack(gain_attn_acc), col_start, 1
    )
    dense_gain_full = lax.dynamic_update_slice_in_dim(
        jnp.zeros((LAYERS, D), jnp.float32), jnp.stack(gain_dense_acc), col_start, 1
    )
    small = lax.psum((attn_gain_full, dense_gain_full, bias_full), ("dp", "gx", "gy"))
    return (
        jnp.stack(outputs),
        jnp.stack(input_grads),
        small[0],
        summed[0],
        summed[1],
        summed[2],
        summed[3],
        small[2],
        small[1],
        summed[4],
        summed[5],
        summed[6],
    )


def solution(mesh):
    placed = (
        P(None, ("dp", "gy"), "gx"),
        P(None, ("dp", "gy"), "gx"),
        P(None, "dp"),
        P(),
        P(None, "gx", "gy"),
        P(None, "gx", "gy"),
        P(None, "gx", "gy"),
        P(None, "gy", "gx"),
        P(),
        P(),
        P(None, "gx", "gy"),
        P(None, "gx", "gy"),
        P(None, "gy", "gx"),
    )
    return jax.shard_map(
        body,
        mesh=mesh,
        in_specs=placed,
        out_specs=(
            P(None, ("dp", "gy"), "gx"),
            P(None, ("dp", "gy"), "gx"),
            P(),
            P(None, "gx", "gy"),
            P(None, "gx", "gy"),
            P(None, "gx", "gy"),
            P(None, "gy", "gx"),
            P(),
            P(),
            P(None, "gx", "gy"),
            P(None, "gx", "gy"),
            P(None, "gy", "gx"),
        ),
        check_vma=False,
    )
```

profile of v0, /device:TPU:0, one launch (start us, length us, event | category | flops | bytes accessed | tf_op | source)
XLA Modules:
  0.0 4443.3 jit_solution(563244002540466702)
XLA Ops:
  193.8 94.4 %reshape.1131 = f32[8384512]{0:T(1024)} reshape(f32[4,2096128]{1,0:T(4,128)} %slice.331) | data formatting | bytes 67076096
  288.3 49.7 %reshape.1060 = f32[4,1024,2047]{2,1,0:T(8,128)} reshape(f32[8384512]{0:T(1024)} %reshape.1131) | data formatting | bytes 67076096 | tf_op jit(solution)/shard_map/reshape | solution.py:93
  446.8 75.0 %reduce-scatter.51.cloned.1.call-done = f32[256,1024]{1,0:T(8,128)} async-done(((f32[1024,1024]{1,0:T(8,128)}), f32[256,1024]{1,0:T(8,128)}) %reduce-scatter.51.cloned.1.call-update) | async-done | bytes 1048592 | tf_op jit(solution)/shard_map/reduce_scatter | solution.py:35
  521.8 80.3 %reduce-scatter.35.cloned.1.call-done = f32[256,1024]{1,0:T(8,128)} async-done(((f32[1024,1024]{1,0:T(8,128)}), f32[256,1024]{1,0:T(8,128)}) %reduce-scatter.35.cloned.1.call-update) | async-done | bytes 1048592 | tf_op jit(solution)/shard_map/reduce_scatter | solution.py:35
  782.7 72.5 %reduce-scatter.55.cloned.1.call-done = f32[256,1024]{1,0:T(8,128)} async-done(((f32[1024,1024]{1,0:T(8,128)}), f32[256,1024]{1,0:T(8,128)}) %reduce-scatter.55.cloned.1.call-update) | async-done | bytes 1048592 | tf_op jit(solution)/shard_map/reduce_scatter | solution.py:35
  856.6 78.7 %reduce-scatter.39.cloned.1.call-done = f32[256,1024]{1,0:T(8,128)} async-done(((f32[1024,1024]{1,0:T(8,128)}), f32[256,1024]{1,0:T(8,128)}) %reduce-scatter.39.cloned.1.call-update) | async-done | bytes 1048592 | tf_op jit(solution)/shard_map/reduce_scatter | solution.py:35
  1116.0 94.5 %reshape.1133 = f32[8384512]{0:T(1024)} reshape(f32[4,2096128]{1,0:T(4,128)} %slice.338) | data formatting | bytes 67076096
  1210.5 49.7 %reshape.1066 = f32[4,1024,2047]{2,1,0:T(8,128)} reshape(f32[8384512]{0:T(1024)} %reshape.1133) | data formatting | bytes 67076096 | tf_op jit(solution)/shard_map/reshape | solution.py:93
  1365.9 73.8 %reduce-scatter.59.cloned.1.call-done = f32[256,1024]{1,0:T(8,128)} async-done(((f32[1024,1024]{1,0:T(8,128)}), f32[256,1024]{1,0:T(8,128)}) %reduce-scatter.59.cloned.1.call-update) | async-done | bytes 1048592 | tf_op jit(solution)/shard_map/reduce_scatter | solution.py:35
  1441.1 78.7 %reduce-scatter.43.cloned.1.call-done = f32[256,1024]{1,0:T(8,128)} async-done(((f32[1024,1024]{1,0:T(8,128)}), f32[256,1024]{1,0:T(8,128)}) %reduce-scatter.43.cloned.1.call-update) | async-done | bytes 1048592 | tf_op jit(solution)/shard_map/reduce_scatter | solution.py:35
  1525.2 43.3 all-gather.65.cloned.1.call-done
  1687.9 77.3 %reduce-scatter.67.cloned.1.call-done = f32[256,1024]{1,0:T(8,128)} async-done(((f32[1024,1024]{1,0:T(8,128)}), f32[256,1024]{1,0:T(8,128)}) %reduce-scatter.67.cloned.1.call-update) | async-done | bytes 1048592 | tf_op jit(solution)/shard_map/reduce_scatter | solution.py:35
  1768.4 45.4 %all-gather.81.cloned.1.call-done = bf16[1024,1024]{1,0:T(8,128)(2,1)} async-done(((bf16[256,1024]{1,0:T(8,128)(2,1)}), bf16[1024,1024]{1,0:T(8,128)(2,1)}) %all-gather.81.cloned.1.call-update) | async-done | bytes 2097168 | tf_op jit(solution)/shard_map/all_gather | solution.py:31
  1958.9 73.4 %reduce-scatter.83.cloned.1.call-done = f32[256,1024]{1,0:T(8,128)} async-done(((f32[1024,1024]{1,0:T(8,128)}), f32[256,1024]{1,0:T(8,128)}) %reduce-scatter.83.cloned.1.call-update) | async-done | bytes 1048592 | tf_op jit(solution)/shard_map/reduce_scatter | solution.py:35
  2036.8 75.5 %reduce-scatter.47.cloned.1.call-done = f32[256,1024]{1,0:T(8,128)} async-done(((f32[1024,1024]{1,0:T(8,128)}), f32[256,1024]{1,0:T(8,128)}) %reduce-scatter.47.cloned.1.call-update) | async-done | bytes 1048592 | tf_op jit(solution)/shard_map/reduce_scatter | solution.py:35
  2112.3 80.3 %reduce-scatter.63.cloned.1.call-done = f32[256,1024]{1,0:T(8,128)} async-done(((f32[1024,1024]{1,0:T(8,128)}), f32[256,1024]{1,0:T(8,128)}) %reduce-scatter.63.cloned.1.call-update) | async-done | bytes 1048592 | tf_op jit(solution)/shard_map/reduce_scatter | solution.py:35
  2198.7 45.8 %all-gather.69.cloned.1.call-done = bf16[1024,1024]{1,0:T(8,128)(2,1)} async-done(((bf16[256,1024]{1,0:T(8,128)(2,1)}), bf16[1024,1024]{1,0:T(8,128)(2,1)}) %all-gather.69.cloned.1.call-update) | async-done | bytes 2097168 | tf_op jit(solution)/shard_map/all_gather | solution.py:31
  2425.6 73.0 %reduce-scatter.71.cloned.1.call-done = f32[256,1024]{1,0:T(8,128)} async-done(((f32[1024,1024]{1,0:T(8,128)}), f32[256,1024]{1,0:T(8,128)}) %reduce-scatter.71.cloned.1.call-update) | async-done | bytes 1048592 | tf_op jit(solution)/shard_map/reduce_scatter | solution.py:35
  2498.6 80.1 %reduce-scatter.87.cloned.1.call-done = f32[256,1024]{1,0:T(8,128)} async-done(((f32[1024,1024]{1,0:T(8,128)}), f32[256,1024]{1,0:T(8,128)}) %reduce-scatter.87.cloned.1.call-update) | async-done | bytes 1048592 | tf_op jit(solution)/shard_map/reduce_scatter | solution.py:35
  2588.7 45.8 %all-gather.89.cloned.1.call-done = bf16[1024,1024]{1,0:T(8,128)(2,1)} async-done(((bf16[256,1024]{1,0:T(8,128)(2,1)}), bf16[1024,1024]{1,0:T(8,128)(2,1)}) %all-gather.89.cloned.1.call-update) | async-done | bytes 2097168 | tf_op jit(solution)/shard_map/all_gather | solution.py:31
  2779.2 51.6 %reduce-scatter.91.cloned.1.call-done = f32[256,1024]{1,0:T(8,128)} async-done(((f32[1024,1024]{1,0:T(8,128)}), f32[256,1024]{1,0:T(8,128)}) %reduce-scatter.91.cloned.1.call-update) | async-done | bytes 1048592 | tf_op jit(solution)/shard_map/reduce_scatter | solution.py:35
  2830.7 80.3 %reduce-scatter.75.cloned.1.call-done = f32[256,1024]{1,0:T(8,128)} async-done(((f32[1024,1024]{1,0:T(8,128)}), f32[256,1024]{1,0:T(8,128)}) %reduce-scatter.75.cloned.1.call-update) | async-done | bytes 1048592 | tf_op jit(solution)/shard_map/reduce_scatter | solution.py:35
  3613.7 42.9 all-reduce.8
  3660.3 722.3 %all-reduce.20.cloned.1.call-done = (f32[2,1024,512]{1,2,0:T(8,128)}, f32[2,1024,512]{1,2,0:T(8,128)}, f32[2,1024,512]{1,2,0:T(8,128)}, f32[2,512,1024]{2,1,0:T(...) async-done(((f32[2,1024,512]{1,2,0:T(8,128)}, f32[2,1024,512]{1,2,0:T(8,128)}, f32[2,1024,512]{1,2,0:T(8,128)}, ...) | async-done | bytes 48234512 | tf_op jit(solution)/shard_map/psum | solution.py:319
  (792 shorter events, 2141.7 us)
Async XLA Ops:
  16.8 354.5 %reduce-scatter.49.cloned.1.call-start = ((), (), s32[]{:S(2)}) async-start(), calls=%async_computation.49 | async-start | bytes 9437184 | tf_op jit(solution)/shard_map/reduce_scatter | solution.py:39
  73.1 328.8 %reduce-scatter.33.cloned.1.call-start = ((), (), s32[]{:S(2)}) async-start(), calls=%async_computation.33 | async-start | bytes 9437184 | tf_op jit(solution)/shard_map/reduce_scatter | solution.py:39
  118.4 314.2 %all-gather.51.cloned.1.call-start = ((), (), s32[]{:S(2)}) async-start(), calls=%async_computation.50 | async-start | bytes 1572864 | tf_op jit(solution)/shard_map/all_gather | solution.py:43
  445.5 209.3 %all-gather.53.cloned.1.call-start = ((), (), s32[]{:S(2)}) async-start(), calls=%async_computation.52 | async-start | bytes 2621440 | tf_op jit(solution)/shard_map/all_gather | solution.py:31
  767.5 167.8 %reduce-scatter.39.cloned.1.call-start = ((), (), s32[]{:S(2)}) async-start(), calls=%async_computation.39 | async-start | bytes 5242880 | tf_op jit(solution)/shard_map/reduce_scatter | solution.py:35
  782.0 205.7 %all-gather.57.cloned.1.call-start = ((), (), s32[]{:S(2)}) async-start(), calls=%async_computation.56 | async-start | bytes 2621440 | tf_op jit(solution)/shard_map/all_gather | solution.py:31
  941.6 348.2 %reduce-scatter.57.cloned.1.call-start = ((), (), s32[]{:S(2)}) async-start(), calls=%async_computation.57 | async-start | bytes 9437184 | tf_op jit(solution)/shard_map/reduce_scatter | solution.py:39
  995.8 307.7 %reduce-scatter.41.cloned.1.call-start = ((), (), s32[]{:S(2)}) async-start(), calls=%async_computation.41 | async-start | bytes 9437184 | tf_op jit(solution)/shard_map/reduce_scatter | solution.py:39
  1041.3 308.6 %all-gather.59.cloned.1.call-start = ((), (), s32[]{:S(2)}) async-start(), calls=%async_computation.58 | async-start | bytes 1572864 | tf_op jit(solution)/shard_map/all_gather | solution.py:43
  1363.4 205.0 %all-gather.65.cloned.1.call-start = ((), (), s32[]{:S(2)}) async-start(), calls=%async_computation.64 | async-start | bytes 2621440 | tf_op jit(solution)/shard_map/all_gather | solution.py:31
  1365.9 249.3 %all-gather.45.cloned.1.call-start = ((), (), s32[]{:S(2)}) async-start(), calls=%async_computation.44 | async-start | bytes 2621440 | tf_op jit(solution)/shard_map/all_gather | solution.py:31
  1687.8 172.8 %all-gather.61.cloned.1.call-start = ((), (), s32[]{:S(2)}) async-start(), calls=%async_computation.60 | async-start | bytes 2621440 | tf_op jit(solution)/shard_map/all_gather | solution.py:31
  1932.6 179.7 %reduce-scatter.47.cloned.1.call-start = ((), (), s32[]{:S(2)}) async-start(), calls=%async_computation.47 | async-start | bytes 5242880 | tf_op jit(solution)/shard_map/reduce_scatter | solution.py:35
  1944.3 248.3 %reduce-scatter.63.cloned.1.call-start = ((), (), s32[]{:S(2)}) async-start(), calls=%async_computation.63 | async-start | bytes 5242880 | tf_op jit(solution)/shard_map/reduce_scatter | solution.py:35
  1958.9 285.7 %all-gather.69.cloned.1.call-start = ((), (), s32[]{:S(2)}) async-start(), calls=%async_computation.68 | async-start | bytes 2621440 | tf_op jit(solution)/shard_map/all_gather | solution.py:31
  2413.0 165.8 %reduce-scatter.87.cloned.1.call-start = ((), (), s32[]{:S(2)}) async-start(), calls=%async_computation.87 | async-start | bytes 5242880 | tf_op jit(solution)/shard_map/reduce_scatter | solution.py:35
  2425.6 208.9 %all-gather.89.cloned.1.call-start = ((), (), s32[]{:S(2)}) async-start(), calls=%async_computation.88 | async-start | bytes 2621440 | tf_op jit(solution)/shard_map/all_gather | solution.py:31
  2741.0 170.0 %reduce-scatter.75.cloned.1.call-start = ((), (), s32[]{:S(2)}) async-start(), calls=%async_computation.75 | async-start | bytes 5242880 | tf_op jit(solution)/shard_map/reduce_scatter | solution.py:35
  2759.6 358.5 %all-gather.77.cloned.1.call-start = ((), (), s32[]{:S(2)}) async-start(), calls=%async_computation.76 | async-start | bytes 2621440 | tf_op jit(solution)/shard_map/all_gather | solution.py:31
  2920.2 237.7 %all-gather.93.cloned.1.call-start = ((), (), s32[]{:S(2)}) async-start(), calls=%async_computation.92 | async-start | bytes 2621440 | tf_op jit(solution)/shard_map/all_gather | solution.py:31
  3215.1 221.7 %all-gather.95.cloned.1.call-start = ((), (), s32[]{:S(2)}) async-start(), calls=%async_computation.94 | async-start | bytes 4718592 | tf_op jit(solution)/shard_map/all_gather | solution.py:43
  3266.1 342.6 %reduce-scatter.79.cloned.1.call-start = ((), (), s32[]{:S(2)}) async-start(), calls=%async_computation.79 | async-start | bytes 5242880 | tf_op jit(solution)/shard_map/reduce_scatter | solution.py:35
  3298.2 310.5 %reduce-scatter.95.cloned.1.call-start = ((), (), s32[]{:S(2)}) async-start(), calls=%async_computation.95 | async-start | bytes 5242880 | tf_op jit(solution)/shard_map/reduce_scatter | solution.py:35
  3443.6 939.0 %all-reduce.20.cloned.1.call-start = ((), (), s32[]{:S(2)}) async-start(), calls=%async_computation.96 | async-start | bytes 96468992 | tf_op jit(solution)/shard_map/psum | solution.py:319
  (219 other events, 9385.5 us)
Sparse Core Ops, SparseCore 0:
  16.1 48.5 all-gather.48
  443.8 77.9 reduce-scatter.50
  524.8 77.2 reduce-scatter.34
  608.4 46.4 all-gather.52
  777.2 77.9 reduce-scatter.54
  858.0 77.2 reduce-scatter.38
  941.2 46.4 all-gather.56
  1361.7 77.9 reduce-scatter.58
  1442.5 77.2 reduce-scatter.42
  1687.2 77.9 reduce-scatter.66
  1767.3 46.4 all-gather.80
  1954.3 77.9 reduce-scatter.82
  2035.0 77.2 reduce-scatter.46
  2115.3 77.2 reduce-scatter.62
  2198.0 46.4 all-gather.68
  2420.6 77.9 reduce-scatter.70
  2501.5 77.2 reduce-scatter.86
  2588.0 46.4 all-gather.88
  2752.8 77.9 reduce-scatter.90
  2833.7 77.2 reduce-scatter.74
  2920.3 46.4 all-gather.76
  3298.3 77.2 reduce-scatter.78
  3443.7 77.2 reduce-scatter.94
  3550.9 831.6 all-reduce.19
  (41 shorter events, 829.2 us)
where the time goes:
time: 4460 us; the launch traced here: 4440 us
  waiting for transfers between devices  2530 us (57%)
  local copies, waits for them, and re-layouts  942 us (21%)
  matrix products  553 us (12%)
  other arithmetic  337 us (8%)
  blocking collectives  62.7 us (1%)
    reduce_scatter x16, waiting for transfers between devices, token_reduce(): return lax.psum_scatter(values, 'gy', scatter_dimension=0, tiled=True)  1050 us
    psum x1, waiting for transfers between devices, body(): lax.psum((attn_grads[:, 0], attn_grads[:, 1], attn_grads[:, 2], jnp.stack...  722 us
    unnamed x389, local copies, waits for them, and re-layouts  598 us
    all_gather x16, waiting for transfers between devices, token_gather(): return lax.all_gather(values, 'gy', axis=0, tiled=True)  550 us
    reshape x2, local copies, waits for them, and re-layouts, toeplitz(): wide[:, :length * (2 * length - 1)].reshape(heads, length, 2 * length - 1)  99.4 us
    reduce_scatter x8, waiting for transfers between devices, hidden_reduce(): return lax.psum_scatter(values, 'gx', scatter_dimension=2, tiled=True)  97 us
  transfers between devices with their start and end apart: 65, of which 49 were waited for; matrix products, arithmetic and copies ran while one was open for 37% of the time, Pallas kernels for 0%

commit v1 on v0

v1 whole, which is shorter than its diff:
```python
import functools

import jax
import jax.numpy as jnp
from jax import lax
from jax.experimental import pallas as pl
from jax.experimental.pallas import tpu as pltpu
from jax.sharding import PartitionSpec as P

D = 2048
H = 32
DH = 64
NB = 32
LAYERS = 2
MICRO = 2
LEN = 1024
TILE = 256
NEAR = 5
NEG = -1000000000.0
HIGH = lax.Precision.HIGHEST


def head_mask(hp, h, rows):
    lane = lax.broadcasted_iota(jnp.int32, (rows, hp*DH), 1)
    return (lane >= h*DH) & (lane < (h+1)*DH)

def pick(values, hp, h):
    if hp == 1:
        return values
    return jnp.where(head_mask(hp, h, values.shape[0]), values, jnp.zeros_like(values))

def nt(a,b): return lax.dot_general(a,b,(((1,),(1,)),((),())),preferred_element_type=jnp.float32)
def tn(a,b): return lax.dot_general(a,b,(((0,),(0,)),((),())),preferred_element_type=jnp.float32)
def nn(a,b): return lax.dot_general(a,b,(((1,),(0,)),((),())),preferred_element_type=jnp.float32)

def build_bias(hp, w_ref, bias):
    for h in range(hp):
        for d in range(NEAR):
            wide = jnp.broadcast_to(w_ref[h, d:d+1, :], (TILE, 2*TILE))
            wide = pltpu.roll(wide, 0, 1, stride=1, stride_axis=0)
            bias[h, d] = wide[:, :TILE]

def fwd_kernel(hp, span, segr, segc, q_ref, k_ref, v_ref, w_ref, o_ref, lse_ref, bias, s_ref):
    iq = pl.program_id(1)
    @pl.when(iq == 0)
    def _():
        build_bias(hp, w_ref, bias)
    lo = span[0, iq]; hi = span[1, iq]
    q = q_ref[...]
    row_seg = segr[...]
    outs = []
    lse_ref[...] = jnp.zeros_like(lse_ref)
    for h in range(hp):
        qh = pick(q, hp, h)
        def first(kc, high):
            rows = pl.ds(pl.multiple_of(kc*TILE, TILE), TILE)
            s = nt(k_ref[rows, :], qh) + bias[h, jnp.clip(kc-iq+2, 0, NEAR-1)]
            s = jnp.where(segc[rows, :] == row_seg, s, NEG)
            s_ref[rows, :] = s
            return jnp.maximum(high, jnp.max(s, axis=0, keepdims=True))
        high = lax.fori_loop(lo, hi, first, jnp.full((1, TILE), NEG, jnp.float32))
        def second(kc, carry):
            total, acc = carry
            rows = pl.ds(pl.multiple_of(kc*TILE, TILE), TILE)
            e = jnp.exp(s_ref[rows, :] - high)
            total = total + jnp.sum(e, axis=0, keepdims=True)
            acc = acc + tn(v_ref[rows, :], e.astype(jnp.bfloat16))
            return total, acc
        total, acc = lax.fori_loop(lo, hi, second, (jnp.zeros((1, TILE), jnp.float32), jnp.zeros((hp*DH, TILE), jnp.float32)))
        outs.append((acc / total)[h*DH:(h+1)*DH, :])
        lse_ref[0, h:h+1, :] = high + jnp.log(total)
    out = jnp.concatenate(outs, axis=0) if hp > 1 else outs[0]
    o_ref[...] = out.T.astype(o_ref.dtype)

def bwd_kernel(hp, span, segr, segc, q_ref, k_ref, v_ref, w_ref, o_ref, lse_ref, go_ref, gq_ref, gk_ref, gv_ref, gb_ref, bias, gbias, gk_acc, gv_acc):
    iq = pl.program_id(1)
    @pl.when(iq == 0)
    def _():
        build_bias(hp, w_ref, bias)
        gbias[...] = jnp.zeros_like(gbias)
        gk_acc[...] = jnp.zeros_like(gk_acc)
        gv_acc[...] = jnp.zeros_like(gv_acc)
    lo = span[0, iq]; hi = span[1, iq]
    q = q_ref[...]
    go = go_ref[...]
    row_seg = segr[...]
    prod = (o_ref[...].astype(jnp.float32) * go.astype(jnp.float32)).T
    outs = []
    for h in range(hp):
        qh = pick(q, hp, h)
        goh = pick(go, hp, h)
        lse = lse_ref[0, h:h+1, :]
        delta = jnp.sum(prod[h*DH:(h+1)*DH, :], axis=0, keepdims=True)
        def step(kc, acc):
            rows = pl.ds(pl.multiple_of(kc*TILE, TILE), TILE)
            near = jnp.clip(kc-iq+2, 0, NEAR-1)
            k = k_ref[rows, :]
            s = nt(k, qh) + bias[h, near]
            s = jnp.where(segc[rows, :] == row_seg, s, NEG)
            p = jnp.exp(s - lse)
            gp = nt(v_ref[rows, :], goh)
            gs = (p * (gp - delta)).astype(jnp.bfloat16)
            gv_acc[rows, :] += nn(p.astype(jnp.bfloat16), goh)
            gk_acc[rows, :] += nn(gs, qh)
            gbias[h, near] += gs.astype(jnp.float32)
            return acc + tn(k, gs)
        acc = lax.fori_loop(lo, hi, step, jnp.zeros((hp*DH, TILE), jnp.float32))
        outs.append(acc[h*DH:(h+1)*DH, :])
    out = jnp.concatenate(outs, axis=0) if hp > 1 else outs[0]
    gq_ref[...] = out.T.astype(gq_ref.dtype)
    @pl.when(iq == pl.num_programs(1) - 1)
    def _():
        gk_ref[...] = gk_acc[...].astype(gk_ref.dtype)
        gv_ref[...] = gv_acc[...].astype(gv_ref.dtype)
        gb_ref[...] = jnp.zeros_like(gb_ref)
        down = lax.broadcasted_iota(jnp.int32, (TILE, TILE), 0)
        across = lax.broadcasted_iota(jnp.int32, (TILE, TILE), 1)
        flip = (down + across == TILE - 1).astype(jnp.float32)
        for h in range(hp):
            for d in range(NEAR):
                tile = gbias[h, d]
                if 0 < d < NEAR - 1:
                    tile = lax.dot_general(flip, tile, (((1,), (0,)), ((), ())), precision=lax.Precision.HIGHEST, preferred_element_type=jnp.float32)
                wide = jnp.concatenate([tile, jnp.zeros_like(tile)], axis=1)
                if 0 < d < NEAR - 1:
                    wide = pltpu.roll(wide, 0, 1, stride=1, stride_axis=0)
                gb_ref[h, d:d+1, :] = jnp.sum(wide, axis=0, keepdims=True)

def parts_of(qkv, heads, hp):
    width = hp*DH; pairs = heads//hp
    if width % 128 == 0:
        return [(qkv, n*pairs) for n in range(3)]
    step = heads*DH
    return [(qkv[:, n*step:(n+1)*step], 0) for n in range(3)]

def attend(qkv, span, segr, segc, w):
    heads = w.shape[0]; hp = 2 if heads % 2 == 0 else 1
    width = hp*DH; pairs = heads//hp; steps = LEN//TILE
    (qa,q0),(ka,k0),(va,v0) = parts_of(qkv, heads, hp)
    grid = pltpu.PrefetchScalarGridSpec(
        num_scalar_prefetch=1, grid=(pairs, steps),
        in_specs=[
            pl.BlockSpec((1, TILE), lambda p, i, s: (0, i)),
            pl.BlockSpec((LEN, 1), lambda p, i, s: (0, 0)),
            pl.BlockSpec((TILE, width), lambda p, i, s: (i, q0+p)),
            pl.BlockSpec((LEN, width), lambda p, i, s: (0, k0+p)),
            pl.BlockSpec((LEN, width), lambda p, i, s: (0, v0+p)),
            pl.BlockSpec((hp, NEAR, 2*TILE), lambda p, i, s: (p, 0, 0)),
        ],
        out_specs=[
            pl.BlockSpec((TILE, width), lambda p, i, s: (i, p)),
            pl.BlockSpec((1, 8, TILE), lambda p, i, s: (p, 0, i)),
        ],
        scratch_shapes=[pltpu.VMEM((hp, NEAR, TILE, TILE), jnp.float32), pltpu.VMEM((LEN, TILE), jnp.float32)],
    )
    return pl.pallas_call(
        functools.partial(fwd_kernel, hp), grid_spec=grid,
        out_shape=[jax.ShapeDtypeStruct((LEN, heads*DH), jnp.bfloat16), jax.ShapeDtypeStruct((pairs, 8, LEN), jnp.float32)],
        compiler_params=pltpu.CompilerParams(vmem_limit_bytes=32*1024*1024),
        cost_estimate=pl.CostEstimate(flops=heads*LEN*LEN*DH*16, bytes_accessed=LEN*heads*DH*8, transcendentals=heads*LEN*LEN),
    )(span, segr, segc, qa, ka, va, w)

def attend_back(qkv, span, segr, segc, w, o, lse, go):
    heads = w.shape[0]; hp = 2 if heads % 2 == 0 else 1
    width = hp*DH; pairs = heads//hp; steps = LEN//TILE
    (qa,q0),(ka,k0),(va,v0) = parts_of(qkv, heads, hp)
    grid = pltpu.PrefetchScalarGridSpec(
        num_scalar_prefetch=1, grid=(pairs, steps),
        in_specs=[
            pl.BlockSpec((1, TILE), lambda p, i, s: (0, i)),
            pl.BlockSpec((LEN, 1), lambda p, i, s: (0, 0)),
            pl.BlockSpec((TILE, width), lambda p, i, s: (i, q0+p)),
            pl.BlockSpec((LEN, width), lambda p, i, s: (0, k0+p)),
            pl.BlockSpec((LEN, width), lambda p, i, s: (0, v0+p)),
            pl.BlockSpec((hp, NEAR, 2*TILE), lambda p, i, s: (p, 0, 0)),
            pl.BlockSpec((TILE, width), lambda p, i, s: (i, p)),
            pl.BlockSpec((1, 8, TILE), lambda p, i, s: (p, 0, i)),
            pl.BlockSpec((TILE, width), lambda p, i, s: (i, p)),
        ],
        out_specs=[
            pl.BlockSpec((TILE, width), lambda p, i, s: (i, p)),
            pl.BlockSpec((LEN, width), lambda p, i, s: (0, p)),
            pl.BlockSpec((LEN, width), lambda p, i, s: (0, p)),
            pl.BlockSpec((hp, 8, 2*TILE), lambda p, i, s: (p, 0, 0)),
        ],
        scratch_shapes=[pltpu.VMEM((hp, NEAR, TILE, TILE), jnp.float32)]*2 + [pltpu.VMEM((LEN, width), jnp.float32)]*2,
    )
    flat = jax.ShapeDtypeStruct((LEN, heads*DH), jnp.bfloat16)
    return pl.pallas_call(
        functools.partial(bwd_kernel, hp), grid_spec=grid,
        out_shape=[flat, flat, flat, jax.ShapeDtypeStruct((heads, 8, 2*TILE), jnp.float32)],
        compiler_params=pltpu.CompilerParams(vmem_limit_bytes=32*1024*1024),
        cost_estimate=pl.CostEstimate(flops=heads*LEN*LEN*DH*40, bytes_accessed=LEN*heads*DH*16, transcendentals=heads*LEN*LEN),
    )(span, segr, segc, qa, ka, va, w, o, lse, go)

THRESHOLDS = (12, 16, 23, 32, 46, 64, 91)
def bucket_of(offset):
    distance = jnp.abs(offset)
    beyond = 8 + sum(((distance >= threshold).astype(jnp.int32) for threshold in THRESHOLDS))
    within = jnp.where(distance < 8, distance, beyond)
    return jnp.where(offset > 0, 16, 0) + within

def near_table(back):
    place = jnp.arange(2*TILE, dtype=jnp.int32)
    turn = place - (TILE - 1) if back else jnp.where(place < TILE, place, place - 2*TILE)
    offset = TILE*(jnp.arange(NEAR, dtype=jnp.int32) - 2)[:, None] - turn[None, :]
    return (bucket_of(offset)[:, :, None] == jnp.arange(NB, dtype=jnp.int32)).astype(jnp.float32)

def segment_views(segment):
    places = jnp.arange(LEN, dtype=jnp.int32)
    own = jnp.where(segment == 0, 4 + places, segment)
    order = jnp.where(segment == 0, 4, segment).reshape(-1, TILE)
    low, high = order[:, 0], order[:, -1]
    lo = jnp.sum((high[None, :] < low[:, None]).astype(jnp.int32), axis=1)
    hi = jnp.sum((low[None, :] <= high[:, None]).astype(jnp.int32), axis=1)
    return jnp.stack((lo, hi)), own[None, :], own[:, None]


def core_swap(values):
    return lax.ppermute(values, "gx", [(0, 1), (1, 0)])


def token_gather(values):
    return lax.all_gather(values, "gy", axis=0, tiled=True)


def token_reduce(values):
    return lax.psum_scatter(values, "gy", scatter_dimension=0, tiled=True)


def dot(left, right, dims):
    return lax.dot_general(left, right, (dims, ((), ())), preferred_element_type=jnp.float32)


def row_norm(hidden):
    part = jnp.sum(hidden * hidden, axis=1)
    return lax.rsqrt((part + core_swap(part)) / D + 1e-06)


def norm_back(grad_norm, hidden, scale, gain):
    weighted = grad_norm * gain
    part = jnp.sum(weighted * hidden, axis=1)
    inner = part + core_swap(part)
    cubed = scale * scale * scale * inner / D
    grad_hidden = scale[:, None] * weighted - hidden * cubed[:, None]
    gain_grad = jnp.sum(grad_norm * hidden * scale[:, None], axis=0)
    return grad_hidden, gain_grad


def halves(weights, axis, core):
    width = weights.shape[axis] // 2
    own = lax.dynamic_slice_in_dim(weights, core * width, width, axis)
    other = lax.dynamic_slice_in_dim(weights, (1 - core) * width, width, axis)
    return own, other


def in_order(own, other, axis, core):
    return jnp.where(
        core == 0,
        jnp.concatenate((own, other), axis),
        jnp.concatenate((other, own), axis),
    )


def take_half(values, which):
    rows = values.shape[0] // 2
    return lax.dynamic_slice_in_dim(values, which * rows, rows, 0)


def batch_sum(values, place, bits):
    size = lax.axis_size("dp")
    kept = values
    trail = []
    for bit in bits:
        swap = [(i, i ^ bit) for i in range(size)]
        mine = jnp.where((place & bit) != 0, 1, 0)
        come = lax.ppermute(take_half(kept, 1 - mine), "dp", swap)
        kept = (take_half(kept, mine).astype(jnp.float32) + come.astype(jnp.float32)).astype(
            jnp.bfloat16
        )
        trail.append((swap, mine))
    for swap, mine in reversed(trail):
        kept = in_order(kept, lax.ppermute(kept, "dp", swap), 0, mine)
    return kept


def batch_sums(values, place):
    size = lax.axis_size("dp")
    bits = [1 << n for n in range(size.bit_length() - 1)]
    rows = values.shape[0] // 2
    return jnp.concatenate(
        (
            batch_sum(values[:rows], place, bits),
            batch_sum(values[rows:], place, bits[::-1]),
        ),
        0,
    )


def small_sum(values):
    for axis in ("gx", "gy", "dp"):
        size = lax.axis_size(axis)
        bit = 1
        while bit < size:
            values = values + lax.ppermute(values, axis, [(i, i ^ bit) for i in range(size)])
            bit *= 2
    return values


def body(
    inputs,
    cotangent,
    segments,
    attention_gain,
    query_weight,
    key_weight,
    value_weight,
    mixing_weight,
    relative_bias,
    dense_gain,
    gate_weight,
    up_weight,
    down_weight,
):
    core = lax.axis_index("gx")
    block = lax.axis_index("gy")
    place = lax.axis_index("dp")
    row_count = inputs.shape[1]
    col_count = inputs.shape[2]
    col_start = core * col_count
    heads_dev = query_weight.shape[2] // (2 * DH)
    head_start = (block * 2 + core) * heads_dev
    hidden_dev = gate_weight.shape[2] // 2
    bf16 = jnp.bfloat16
    ahead = near_table(False)
    behind = near_table(True)
    layers = []
    for layer in range(LAYERS):
        qs = halves(query_weight[layer], 1, core)
        ks = halves(key_weight[layer], 1, core)
        vs = halves(value_weight[layer], 1, core)
        gs = halves(gate_weight[layer], 1, core)
        us = halves(up_weight[layer], 1, core)
        table = lax.dynamic_slice_in_dim(relative_bias[layer], head_start, heads_dev, 1)
        layers.append(
            dict(
                qkv=[jnp.concatenate((qs[n], ks[n], vs[n]), 1) for n in range(2)],
                gu=[jnp.concatenate((gs[n], us[n]), 1) for n in range(2)],
                mix=halves(mixing_weight[layer], 0, core),
                down=halves(down_weight[layer], 0, core),
                bias=jnp.einsum("dcb,bh->hdc", ahead, table, precision=HIGH),
                gain1=lax.dynamic_slice_in_dim(attention_gain[layer], col_start, col_count),
                gain2=lax.dynamic_slice_in_dim(dense_gain[layer], col_start, col_count),
            )
        )
    acc = [dict() for _ in range(LAYERS)]

    def add(layer, name, value):
        have = acc[layer].get(name)
        acc[layer][name] = value if have is None else have + value

    NN = ((1,), (0,))
    NT = ((1,), (1,))
    TN = ((0,), (0,))
    micros = []
    for micro in range(MICRO):
        seg_all = segments[micro]
        row_segs = lax.dynamic_slice_in_dim(seg_all, block * row_count, row_count)
        keep = (row_segs != 0).astype(jnp.float32)[:, None]
        views = segment_views(seg_all)
        hidden = inputs[micro].astype(jnp.float32)
        saved = []
        for layer in range(LAYERS):
            w = layers[layer]
            scale1 = row_norm(hidden)
            normed = token_gather((hidden * scale1[:, None] * w["gain1"]).astype(bf16))
            come = core_swap(dot(normed, w["qkv"][1], NN).astype(bf16))
            qkv = (dot(normed, w["qkv"][0], NN) + come.astype(jnp.float32)).astype(bf16)
            mixed, lse = attend(qkv, *views, w["bias"])
            mixed_other = core_swap(mixed)
            branch = dot(mixed, w["mix"][0], NN) + dot(mixed_other, w["mix"][1], NN)
            middle = hidden + token_reduce(branch.astype(bf16)).astype(jnp.float32)
            scale2 = row_norm(middle)
            dense = token_gather((middle * scale2[:, None] * w["gain2"]).astype(bf16))
            come = core_swap(dot(dense, w["gu"][1], NN).astype(bf16))
            gate_up = dot(dense, w["gu"][0], NN) + come.astype(jnp.float32)
            active = (
                jax.nn.gelu(gate_up[:, :hidden_dev], approximate=True) * gate_up[:, hidden_dev:]
            ).astype(bf16)
            active_other = core_swap(active)
            out = dot(active, w["down"][0], NN) + dot(active_other, w["down"][1], NN)
            last = middle + token_reduce(out.astype(bf16)).astype(jnp.float32)
            saved.append(
                (
                    hidden,
                    scale1,
                    normed,
                    qkv,
                    lse,
                    mixed,
                    mixed_other,
                    middle,
                    scale2,
                    dense,
                    gate_up.astype(bf16),
                    active,
                    active_other,
                )
            )
            hidden = last
        micros.append((keep, views, saved, hidden))
    outputs = [hidden * keep for keep, _, _, hidden in micros]
    grads = [cotangent[n].astype(jnp.float32) * micros[n][0] for n in range(MICRO)]
    results = [None] * LAYERS
    for layer in reversed(range(LAYERS)):
        w = layers[layer]
        for micro in range(MICRO):
            keep, views, saved, _ = micros[micro]
            (
                hidden,
                scale1,
                normed,
                qkv,
                lse,
                mixed,
                mixed_other,
                middle,
                scale2,
                dense,
                gate_up,
                active,
                active_other,
            ) = saved[layer]
            grad = grads[micro]
            grad_out = token_gather(grad.astype(bf16))
            come = core_swap(dot(grad_out, w["down"][1], NT).astype(bf16))
            grad_active = dot(grad_out, w["down"][0], NT) + come.astype(jnp.float32)
            gate = gate_up[:, :hidden_dev].astype(jnp.float32)
            up = gate_up[:, hidden_dev:].astype(jnp.float32)
            _, pull = jax.vjp(lambda a, b: jax.nn.gelu(a, approximate=True) * b, gate, up)
            pair = jnp.concatenate(pull(grad_active), 1).astype(bf16)
            pair_other = core_swap(pair)
            grad_dense = dot(pair, w["gu"][0], NT) + dot(pair_other, w["gu"][1], NT)
            grad_dense = token_reduce(grad_dense.astype(bf16)).astype(jnp.float32)
            add(layer, "down0", dot(active, grad_out, TN))
            add(layer, "down1", dot(active_other, grad_out, TN))
            add(layer, "gu0", dot(dense, pair, TN))
            add(layer, "gu1", dot(dense, pair_other, TN))
            grad_norm, gain_part = norm_back(grad_dense, middle, scale2, w["gain2"])
            add(layer, "gain2", gain_part)
            grad_mid = grad + grad_norm
            grad_out = token_gather(grad_mid.astype(bf16))
            come = core_swap(dot(grad_out, w["mix"][1], NT).astype(bf16))
            grad_mixed = (dot(grad_out, w["mix"][0], NT) + come.astype(jnp.float32)).astype(bf16)
            gq, gk, gv, gb = attend_back(qkv, *views, w["bias"], mixed, lse, grad_mixed)
            add(layer, "bias", gb)
            triple = jnp.concatenate((gq, gk, gv), 1)
            triple_other = core_swap(triple)
            grad_normed = dot(triple, w["qkv"][0], NT) + dot(triple_other, w["qkv"][1], NT)
            grad_normed = token_reduce(grad_normed.astype(bf16)).astype(jnp.float32)
            add(layer, "mix0", dot(mixed, grad_out, TN))
            add(layer, "mix1", dot(mixed_other, grad_out, TN))
            add(layer, "qkv0", dot(normed, triple, TN))
            add(layer, "qkv1", dot(normed, triple_other, TN))
            grad_norm, gain_part = norm_back(grad_normed, hidden, scale1, w["gain1"])
            add(layer, "gain1", gain_part)
            grads[micro] = grad_mid + grad_norm
        have = acc[layer]
        for name in ("down", "gu", "mix", "qkv"):
            have[name] = [
                batch_sums(have[name + str(n)].astype(bf16), place).astype(jnp.float32)
                for n in range(2)
            ]

    def columns(name, count):
        result = [[] for _ in range(count)]
        for layer in range(LAYERS):
            own, other = acc[layer][name]
            width = own.shape[1] // count
            for n in range(count):
                cut = slice(n * width, (n + 1) * width)
                result[n].append(in_order(own[:, cut], other[:, cut], 1, core))
        return [jnp.stack(item) for item in result]

    grad_query, grad_key, grad_value = columns("qkv", 3)
    grad_gate, grad_up = columns("gu", 2)
    grad_mixing = jnp.stack([in_order(*acc[n]["mix"], 0, core) for n in range(LAYERS)])
    grad_down = jnp.stack([in_order(*acc[n]["down"], 0, core) for n in range(LAYERS)])
    gain = jnp.stack([acc[n][name] for name in ("gain1", "gain2") for n in range(LAYERS)])
    gain = lax.dynamic_update_slice_in_dim(
        jnp.zeros((2 * LAYERS, D), jnp.float32), gain, col_start, 1
    )
    bias = jnp.stack([acc[n]["bias"][:, :NEAR] for n in range(LAYERS)])
    bias = jnp.einsum("lhdc,dcb->lbh", bias, behind, precision=HIGH)
    bias = lax.dynamic_update_slice_in_dim(
        jnp.zeros((LAYERS, NB, H), jnp.float32), bias, head_start, 2
    )
    small = small_sum(jnp.concatenate((gain.reshape(-1, 128), bias.reshape(-1, 128)), 0))
    split = gain.size // 128
    gain = small[:split].reshape(gain.shape)
    bias = small[split:].reshape(bias.shape)
    return (
        jnp.stack(outputs),
        jnp.stack(grads),
        gain[:LAYERS],
        grad_query,
        grad_key,
        grad_value,
        grad_mixing,
        bias,
        gain[LAYERS:],
        grad_gate,
        grad_up,
        grad_down,
    )


def solution(mesh):
    tokens = P(None, ("dp", "gy"), "gx")
    wide = P(None, "gx", "gy")
    tall = P(None, "gy", "gx")
    return jax.shard_map(
        body,
        mesh=mesh,
        in_specs=(
            tokens,
            tokens,
            P(None, "dp"),
            P(),
            wide,
            wide,
            wide,
            tall,
            P(),
            P(),
            wide,
            wide,
            tall,
        ),
        out_specs=(tokens, tokens, P(), wide, wide, wide, tall, P(), P(), wide, wide, tall),
        check_vma=False,
    )
```

time: 4460 us -> 1900 us (0.43)
  waiting for transfers between devices: 2530 us -> 891 us
  local copies, waits for them, and re-layouts: 942 us -> 91.6 us
  matrix products: 553 us -> 309 us
  Pallas kernels: 0 us -> 217 us
  starting transfers between devices: 6.21 us -> 169 us
  other arithmetic: 337 us -> 197 us
  blocking collectives: 62.7 us -> 0 us
    reduce_scatter x16, waiting for transfers between devices: 1050 us -> 229 us  [token_reduce(): return lax.psum_scatter(values, 'gy', scatter_dimension=0, tiled=True)]
    psum x1 -> x0, waiting for transfers between devices: 722 us -> none  [body(): lax.psum((attn_grads[:, 0], attn_grads[:, 1], attn_grads[:, 2], jnp.stack...]
    unnamed x389 -> x553, local copies, waits for them, and re-layouts: 598 us -> 29.3 us
    ppermute x0 -> x181, waiting for transfers between devices: none -> 264 us  [the longest x64 134 us: batch_sum(): come = lax.ppermute(take_half(kept, 1 - mine), 'dp', swap)]
    dot_general x75 -> x99, matrix products: 553 us -> 309 us  [the longest x96 308 us: dot(): lax.dot_general(left, right, (dims, ((), ())), preferred_element_type=jnp...]
    pallas_call x0 -> x8, Pallas kernels: none -> 217 us  [the longest x4 124 us: attend_back(): pl.pallas_call(functools.partial(bwd_kernel, hp), grid_spec=grid, out_sha...]
    reshape x10 -> x3, local copies, waits for them, and re-layouts: 194 us -> 0.78 us  [the longest x1 0.69 us: body(): bias = small[split:].reshape(bias.shape)]
    ppermute x0 -> x181, starting transfers between devices: none -> 164 us  [the longest x64 84.1 us: batch_sum(): come = lax.ppermute(take_half(kept, 1 - mine), 'dp', swap)]
  transfers between devices with their start and end apart: 65 -> 213, of which waited for: 49 -> 123; matrix products, arithmetic and copies ran while one was open for 37% -> 28% of each run, Pallas kernels for 0% -> 10%
where the time goes in v1:
time: 1900 us; the launch traced here: 1890 us
  waiting for transfers between devices  891 us (47%)
  matrix products  309 us (16%)
  Pallas kernels  217 us (11%)
  other arithmetic  197 us (10%)
  starting transfers between devices  169 us (9%)
  local copies, waits for them, and re-layouts  91.6 us (5%)
  between operations  19.6 us (1%)
    all_gather x16, waiting for transfers between devices, token_gather(): return lax.all_gather(values, 'gy', axis=0, tiled=True)  396 us
    dot_general x96, matrix products, dot(): lax.dot_general(left, right, (dims, ((), ())), preferred_element_type=jnp...  308 us
    reduce_scatter x16, waiting for transfers between devices, token_reduce(): return lax.psum_scatter(values, 'gy', scatter_dimension=0, tiled=True)  229 us
    ppermute x64, waiting for transfers between devices, batch_sum(): come = lax.ppermute(take_half(kept, 1 - mine), 'dp', swap)  134 us
    pallas_call x4, Pallas kernels, attend_back(): pl.pallas_call(functools.partial(bwd_kernel, hp), grid_spec=grid, out_sha...  124 us
    pallas_call x4, Pallas kernels, attend(): pl.pallas_call(functools.partial(fwd_kernel, hp), grid_spec=grid, out_sha...  92.8 us
    ppermute x64, waiting for transfers between devices, batch_sum(): kept = in_order(kept, lax.ppermute(kept, 'dp', swap), 0, mine)  86.4 us
    ppermute x64, starting transfers between devices, batch_sum(): come = lax.ppermute(take_half(kept, 1 - mine), 'dp', swap)  84.1 us
  transfers between devices with their start and end apart: 213, of which 123 were waited for; matrix products, arithmetic and copies ran while one was open for 28% of the time, Pallas kernels for 10%

profile of v1, /device:TPU:0, one launch (start us, length us, event | category | flops | bytes accessed | tf_op | source)
XLA Modules:
  0.0 1894.2 jit_solution(3153298477414553686)
XLA Ops:
  20.6 41.0 %all-gather.25.cloned.1.call-done = bf16[1024,1024]{1,0:T(8,128)(2,1)} async-done(((bf16[256,1024]{1,0:T(8,128)(2,1)}), bf16[1024,1024]{1,0:T(8,128)(2,1)}) %all-gather.25.cloned.1.call-update) | async-done | bytes 2097168 | tf_op jit(solution)/shard_map/all_gather | solution.py:224
  73.8 23.2 %shard_map.222 = (bf16[1024,256]{1,0:T(8,128)(2,1)S(1)}, f32[2,8,1024]{2,1,0:T(8,128)S(1)}) custom-call(s32[2,4]{1,0:T(2,128)S(1)} %pad_add_fusion.1.span, s32[1,1024]{1,0:T(1,128)S(1)} %get-tuple-element.231.segr, s32[1024,1]{1,0:T(8,128)S(1)} %compare_select_fusion.segc, bf16[1024,768]{1,0:T(8,128)(2,1)S(1)} %add_convert_fusion.25.q_ref.k_ref.v_ref, ...), custom_call_target="tpu_custom_call" | custom-call | flops 4294967296 | bytes 2097152 | tf_op jit(solution)/shard_map/pallas_call | solution.py:156
  124.5 23.2 %shard_map.220 = (bf16[1024,256]{1,0:T(8,128)(2,1)S(1)}, f32[2,8,1024]{2,1,0:T(8,128)S(1)}) custom-call(s32[2,4]{1,0:T(2,128)S(1)} %pad_add_fusion.span, s32[1,1024]{1,0:T(1,128)S(1)} %get-tuple-element.227.segr, s32[1024,1]{1,0:T(8,128)S(1)} %compare_select_fusion.1.segc, bf16[1024,768]{1,0:T(8,128)(2,1)S(1)} %add_convert_fusion.27.q_ref.k_ref.v_ref, ...), custom_call_target="tpu_custom_call" | custom-call | flops 4294967296 | bytes 2097152 | tf_op jit(solution)/shard_map/pallas_call | solution.py:156
  157.4 46.0 %reduce-scatter.17.cloned.1.call-done = bf16[256,1024]{1,0:T(8,128)(2,1)} async-done(((bf16[1024,1024]{1,0:T(8,128)(2,1)}), bf16[256,1024]{1,0:T(8,128)(2,1)}) %reduce-scatter.17.cloned.1.call-update) | async-done | bytes 524304 | tf_op jit(solution)/shard_map/reduce_scatter | solution.py:228
  219.4 34.0 %all-gather.27.cloned.1.call-done = bf16[1024,1024]{1,0:T(8,128)(2,1)} async-done(((bf16[256,1024]{1,0:T(8,128)(2,1)}), bf16[1024,1024]{1,0:T(8,128)(2,1)}) %all-gather.27.cloned.1.call-update) | async-done | bytes 2097168 | tf_op jit(solution)/shard_map/all_gather | solution.py:224
  275.5 29.6 %all-gather.19.cloned.1.call-done = bf16[1024,1024]{1,0:T(8,128)(2,1)} async-done(((bf16[256,1024]{1,0:T(8,128)(2,1)}), bf16[1024,1024]{1,0:T(8,128)(2,1)}) %all-gather.19.cloned.1.call-update) | async-done | bytes 2097168 | tf_op jit(solution)/shard_map/all_gather | solution.py:224
  343.3 24.6 %reduce-scatter.27.cloned.1.call-done = bf16[256,1024]{1,0:T(8,128)(2,1)} async-done(((bf16[1024,1024]{1,0:T(8,128)(2,1)}), bf16[256,1024]{1,0:T(8,128)(2,1)}) %reduce-scatter.27.cloned.1.call-update) | async-done | bytes 524304 | tf_op jit(solution)/shard_map/reduce_scatter | solution.py:228
  367.9 46.2 %reduce-scatter.19.cloned.1.call-done = bf16[256,1024]{1,0:T(8,128)(2,1)} async-done(((bf16[1024,1024]{1,0:T(8,128)(2,1)}), bf16[256,1024]{1,0:T(8,128)(2,1)}) %reduce-scatter.19.cloned.1.call-update) | async-done | bytes 524304 | tf_op jit(solution)/shard_map/reduce_scatter | solution.py:228
  422.7 41.6 %all-gather.29.cloned.1.call-done = bf16[1024,1024]{1,0:T(8,128)(2,1)} async-done(((bf16[256,1024]{1,0:T(8,128)(2,1)}), bf16[1024,1024]{1,0:T(8,128)(2,1)}) %all-gather.29.cloned.1.call-update) | async-done | bytes 2097168 | tf_op jit(solution)/shard_map/all_gather | solution.py:224
  477.3 23.2 %shard_map.223 = (bf16[1024,256]{1,0:T(8,128)(2,1)S(1)}, f32[2,8,1024]{2,1,0:T(8,128)S(1)}) custom-call(s32[2,4]{1,0:T(2,128)S(1)} %pad_add_fusion.1.span, s32[1,1024]{1,0:T(1,128)S(1)} %get-tuple-element.231.segr, s32[1024,1]{1,0:T(8,128)S(1)} %compare_select_fusion.segc, bf16[1024,768]{1,0:T(8,128)(2,1)S(1)} %add_convert_fusion.24.q_ref.k_ref.v_ref, ...), custom_call_target="tpu_custom_call" | custom-call | flops 4294967296 | bytes 2097152 | tf_op jit(solution)/shard_map/pallas_call | solution.py:156
  524.6 23.2 %shard_map.221 = (bf16[1024,256]{1,0:T(8,128)(2,1)S(1)}, f32[2,8,1024]{2,1,0:T(8,128)S(1)}) custom-call(s32[2,4]{1,0:T(2,128)S(1)} %pad_add_fusion.span, s32[1,1024]{1,0:T(1,128)S(1)} %get-tuple-element.227.segr, s32[1024,1]{1,0:T(8,128)S(1)} %compare_select_fusion.1.segc, bf16[1024,768]{1,0:T(8,128)(2,1)S(1)} %add_convert_fusion.26.q_ref.k_ref.v_ref, ...), custom_call_target="tpu_custom_call" | custom-call | flops 4294967296 | bytes 2097152 | tf_op jit(solution)/shard_map/pallas_call | solution.py:156
  561.9 43.9 %reduce-scatter.21.cloned.1.call-done = bf16[256,1024]{1,0:T(8,128)(2,1)} async-done(((bf16[1024,1024]{1,0:T(8,128)(2,1)}), bf16[256,1024]{1,0:T(8,128)(2,1)}) %reduce-scatter.21.cloned.1.call-update) | async-done | bytes 524304 | tf_op jit(solution)/shard_map/reduce_scatter | solution.py:228
  618.5 36.4 %all-gather.31.cloned.1.call-done = bf16[1024,1024]{1,0:T(8,128)(2,1)} async-done(((bf16[256,1024]{1,0:T(8,128)(2,1)}), bf16[1024,1024]{1,0:T(8,128)(2,1)}) %all-gather.31.cloned.1.call-update) | async-done | bytes 2097168 | tf_op jit(solution)/shard_map/all_gather | solution.py:224
  661.8 39.8 %all-gather.41.cloned.1.call-done = bf16[1024,1024]{1,0:T(8,128)(2,1)} async-done(((bf16[256,1024]{1,0:T(8,128)(2,1)}), bf16[1024,1024]{1,0:T(8,128)(2,1)}) %all-gather.41.cloned.1.call-update) | async-done | bytes 2097168 | tf_op jit(solution)/shard_map/all_gather | solution.py:224
  706.1 41.6 %all-gather.23.cloned.1.call-done = bf16[1024,1024]{1,0:T(8,128)(2,1)} async-done(((bf16[256,1024]{1,0:T(8,128)(2,1)}), bf16[1024,1024]{1,0:T(8,128)(2,1)}) %all-gather.23.cloned.1.call-update) | async-done | bytes 2097168 | tf_op jit(solution)/shard_map/all_gather | solution.py:224
  754.4 40.0 %all-gather.33.cloned.1.call-done = bf16[1024,1024]{1,0:T(8,128)(2,1)} async-done(((bf16[256,1024]{1,0:T(8,128)(2,1)}), bf16[1024,1024]{1,0:T(8,128)(2,1)}) %all-gather.33.cloned.1.call-update) | async-done | bytes 2097168 | tf_op jit(solution)/shard_map/all_gather | solution.py:224
  989.4 29.9 %reduce-scatter.23.cloned.1.call-done = bf16[256,1024]{1,0:T(8,128)(2,1)} async-done(((bf16[1024,1024]{1,0:T(8,128)(2,1)}), bf16[256,1024]{1,0:T(8,128)(2,1)}) %reduce-scatter.23.cloned.1.call-update) | async-done | bytes 524304 | tf_op jit(solution)/shard_map/reduce_scatter | solution.py:228
  1091.2 24.8 %all-gather.43.cloned.1.call-done = bf16[1024,1024]{1,0:T(8,128)(2,1)} async-done(((bf16[256,1024]{1,0:T(8,128)(2,1)}), bf16[1024,1024]{1,0:T(8,128)(2,1)}) %all-gather.43.cloned.1.call-update) | async-done | bytes 2097168 | tf_op jit(solution)/shard_map/all_gather | solution.py:224
  1120.8 31.4 %shard_map.224 = (bf16[1024,256]{1,0:T(8,128)(2,1)S(1)}, bf16[1024,256]{1,0:T(8,128)(2,1)S(1)}, bf16[1024,256]{1,0:T(8,128)(2,1)S(1)}, f32[4,8,512]{2,1,0:T(8,128)S(1)}) custom-call(s32[2,4]{1,0:T(2,128)S(1)} %pad_add_fusion.span, s32[1,1024]{1,0:T(1,128)S(1)} %get-tuple-element.227.segr, s32[1024,1]{1,0:T(8,128)S(1)} %compare_select_fusion.1.segc, ...), custom_call_target="tpu_custom_call" | custom-call | flops 10737418240 | bytes 4194304 | tf_op jit(solution)/shard_map/pallas_call | solution.py:189
  1168.5 31.2 %shard_map.226 = (bf16[1024,256]{1,0:T(8,128)(2,1)S(1)}, bf16[1024,256]{1,0:T(8,128)(2,1)S(1)}, bf16[1024,256]{1,0:T(8,128)(2,1)S(1)}, f32[4,8,512]{2,1,0:T(8,128)S(1)}) custom-call(s32[2,4]{1,0:T(2,128)S(1)} %copy-done.21, s32[1,1024]{1,0:T(1,128)S(1)} %copy-done.17, s32[1024,1]{1,0:T(8,128)S(1)} %copy-done.9, bf16[1024,768]{1,0:T(8,128)(2,1)S(1)} %copy-done.29, ...), custom_call_target="tpu_custom_call" | custom-call | flops 10737418240 | bytes 4194304 | tf_op jit(solution)/shard_map/pallas_call | solution.py:189
  1338.6 24.4 %all-gather.37.cloned.1.call-done = bf16[1024,1024]{1,0:T(8,128)(2,1)} async-done(((bf16[256,1024]{1,0:T(8,128)(2,1)}), bf16[1024,1024]{1,0:T(8,128)(2,1)}) %all-gather.37.cloned.1.call-update) | async-done | bytes 2097168 | tf_op jit(solution)/shard_map/all_gather | solution.py:224
  1621.6 24.4 %all-gather.39.cloned.1.call-done = bf16[1024,1024]{1,0:T(8,128)(2,1)} async-done(((bf16[256,1024]{1,0:T(8,128)(2,1)}), bf16[1024,1024]{1,0:T(8,128)(2,1)}) %all-gather.39.cloned.1.call-update) | async-done | bytes 2097168 | tf_op jit(solution)/shard_map/all_gather | solution.py:224
  1685.8 30.9 %shard_map.225 = (bf16[1024,256]{1,0:T(8,128)(2,1)S(1)}, bf16[1024,256]{1,0:T(8,128)(2,1)S(1)}, bf16[1024,256]{1,0:T(8,128)(2,1)S(1)}, f32[4,8,512]{2,1,0:T(8,128)S(1)}) custom-call(s32[2,4]{1,0:T(2,128)S(1)} %copy-done.23, s32[1,1024]{1,0:T(1,128)S(1)} %copy-done.19, s32[1024,1]{1,0:T(8,128)S(1)} %copy-done.11, bf16[1024,768]{1,0:T(8,128)(2,1)S(1)} %copy-done.27, ...), custom_call_target="tpu_custom_call" | custom-call | flops 10737418240 | bytes 4194304 | tf_op jit(solution)/shard_map/pallas_call | solution.py:189
  1718.9 30.7 %shard_map.227 = (bf16[1024,256]{1,0:T(8,128)(2,1)S(1)}, bf16[1024,256]{1,0:T(8,128)(2,1)S(1)}, bf16[1024,256]{1,0:T(8,128)(2,1)S(1)}, f32[4,8,512]{2,1,0:T(8,128)S(1)}) custom-call(s32[2,4]{1,0:T(2,128)S(1)} %copy-done.21, s32[1,1024]{1,0:T(1,128)S(1)} %copy-done.17, s32[1024,1]{1,0:T(8,128)S(1)} %copy-done.9, bf16[1024,768]{1,0:T(8,128)(2,1)S(1)} %copy-done.25, ...), custom_call_target="tpu_custom_call" | custom-call | flops 10737418240 | bytes 4194304 | tf_op jit(solution)/shard_map/pallas_call | solution.py:189
  (1465 shorter events, 1089.4 us)
Async XLA Ops:
  13.0 98.9 %all-gather.17.cloned.1.call-start = ((), (), s32[]{:S(2)}) async-start(), calls=%async_computation.16 | async-start | bytes 2621440 | tf_op jit(solution)/shard_map/all_gather | solution.py:224
  102.6 100.9 %reduce-scatter.17.cloned.1.call-start = ((), (), s32[]{:S(2)}) async-start(), calls=%async_computation.17 | async-start | bytes 2621440 | tf_op jit(solution)/shard_map/reduce_scatter | solution.py:228
  153.4 100.0 %all-gather.27.cloned.1.call-start = ((), (), s32[]{:S(2)}) async-start(), calls=%async_computation.26 | async-start | bytes 2621440 | tf_op jit(solution)/shard_map/all_gather | solution.py:224
  260.1 107.7 %reduce-scatter.27.cloned.1.call-start = ((), (), s32[]{:S(2)}) async-start(), calls=%async_computation.27 | async-start | bytes 2621440 | tf_op jit(solution)/shard_map/reduce_scatter | solution.py:228
  343.2 121.0 %all-gather.29.cloned.1.call-start = ((), (), s32[]{:S(2)}) async-start(), calls=%async_computation.28 | async-start | bytes 2621440 | tf_op jit(solution)/shard_map/all_gather | solution.py:224
  505.4 100.3 %reduce-scatter.21.cloned.1.call-start = ((), (), s32[]{:S(2)}) async-start(), calls=%async_computation.21 | async-start | bytes 2621440 | tf_op jit(solution)/shard_map/reduce_scatter | solution.py:228
  552.7 102.3 %all-gather.31.cloned.1.call-start = ((), (), s32[]{:S(2)}) async-start(), calls=%async_computation.30 | async-start | bytes 2621440 | tf_op jit(solution)/shard_map/all_gather | solution.py:224
  612.7 135.0 %all-gather.23.cloned.1.call-start = ((), (), s32[]{:S(2)}) async-start(), calls=%async_computation.22 | async-start | bytes 2621440 | tf_op jit(solution)/shard_map/all_gather | solution.py:224
  613.3 181.1 %all-gather.33.cloned.1.call-start = ((), (), s32[]{:S(2)}) async-start(), calls=%async_computation.32 | async-start | bytes 2621440 | tf_op jit(solution)/shard_map/all_gather | solution.py:224
  613.9 368.8 %reduce-scatter.41.cloned.1.call-start = ((), (), s32[]{:S(2)}) async-start(), calls=%async_computation.41 | async-start | bytes 2621440 | tf_op jit(solution)/shard_map/reduce_scatter | solution.py:228
  661.8 136.3 %collective-permute-start.22 = (bf16[1024,1280]{1,0:T(8,128)(2,1)}, bf16[1024,1280]{1,0:T(8,128)(2,1)}, u32[]{:S(2)}, u32[]{:S(2)}) collective-permute-start(bf16[1024,1280]{1,0:T(8,128)(2,1)} %convolution_convert_fusion), channel_id=1, source_target_pairs={{0,4},{4,0},{1,5},{5,1},{2,6},{6,2},{3,7},{7,3},{8,12},{12,8},{9,1... | collective-permute-start | bytes 7864328 | tf_op jit(solution)/shard_map/ppermute | solution.py:220
  706.1 99.2 %collective-permute-start.36 = (bf16[1024,640]{1,0:T(8,128)(2,1)}, bf16[1024,640]{1,0:T(8,128)(2,1)}, u32[]{:S(2)}, u32[]{:S(2)}) collective-permute-start(bf16[1024,640]{1,0:T(8,128)(2,1)} %convolution_convert_fusion.9), channel_id=1, source_target_pairs={{0,4},{4,0},{1,5},{5,1},{2,6},{6,2},{3,7},{7,3},{8,12},{12,8},{9,1... | collective-permute-start | bytes 3932168 | tf_op jit(solution)/shard_map/ppermute | solution.py:220
  804.8 103.7 %collective-permute-start.23 = (bf16[1024,640]{1,0:T(8,128)(2,1)}, bf16[1024,640]{1,0:T(8,128)(2,1)}, u32[]{:S(2)}, u32[]{:S(2)}) collective-permute-start(bf16[1024,640]{1,0:T(8,128)(2,1)} %fusion.51), channel_id=1, source_target_pairs={{0,4},{4,0},{1,5},{5,1},{2,6},{6,2},{3,7},{7,3},{8,12},{12,8},{9,1... | collective-permute-start | bytes 3932168 | tf_op jit(solution)/shard_map/ppermute | solution.py:220
  820.2 114.4 %collective-permute-start.11 = (bf16[1024,640]{1,0:T(8,128)(2,1)}, bf16[1024,640]{1,0:T(8,128)(2,1)}, u32[]{:S(2)}, u32[]{:S(2)}) collective-permute-start(bf16[1024,640]{1,0:T(8,128)(2,1)} %fusion.33), channel_id=1, source_target_pairs={{0,4},{4,0},{1,5},{5,1},{2,6},{6,2},{3,7},{7,3},{8,12},{12,8},{9,1... | collective-permute-start | bytes 3932168 | tf_op jit(solution)/shard_map/ppermute | solution.py:220
  838.8 143.9 %reduce-scatter.33.cloned.1.call-start = ((), (), s32[]{:S(2)}) async-start(), calls=%async_computation.33 | async-start | bytes 2621440 | tf_op jit(solution)/shard_map/reduce_scatter | solution.py:228
  866.2 123.2 %reduce-scatter.31.cloned.1.call-start = ((), (), s32[]{:S(2)}) async-start(), calls=%async_computation.31 | async-start | bytes 2621440 | tf_op jit(solution)/shard_map/reduce_scatter | solution.py:228
  917.6 101.8 %reduce-scatter.23.cloned.1.call-start = ((), (), s32[]{:S(2)}) async-start(), calls=%async_computation.23 | async-start | bytes 2621440 | tf_op jit(solution)/shard_map/reduce_scatter | solution.py:228
  949.0 139.0 %all-gather.35.cloned.1.call-start = ((), (), s32[]{:S(2)}) async-start(), calls=%async_computation.34 | async-start | bytes 2621440 | tf_op jit(solution)/shard_map/all_gather | solution.py:224
  1062.6 189.4 %reduce-scatter.35.cloned.1.call-start = ((), (), s32[]{:S(2)}) async-start(), calls=%async_computation.35 | async-start | bytes 2621440 | tf_op jit(solution)/shard_map/reduce_scatter | solution.py:228
  1221.3 112.3 %all-gather.45.cloned.1.call-start = ((), (), s32[]{:S(2)}) async-start(), calls=%async_computation.44 | async-start | bytes 2621440 | tf_op jit(solution)/shard_map/all_gather | solution.py:224
  1302.5 229.7 %reduce-scatter.37.cloned.1.call-start = ((), (), s32[]{:S(2)}) async-start(), calls=%async_computation.37 | async-start | bytes 2621440 | tf_op jit(solution)/shard_map/reduce_scatter | solution.py:228
  1496.7 121.6 %all-gather.47.cloned.1.call-start = ((), (), s32[]{:S(2)}) async-start(), calls=%async_computation.46 | async-start | bytes 2621440 | tf_op jit(solution)/shard_map/all_gather | solution.py:224
  1592.4 268.2 %reduce-scatter.39.cloned.1.call-start = ((), (), s32[]{:S(2)}) async-start(), calls=%async_computation.39 | async-start | bytes 2621440 | tf_op jit(solution)/shard_map/reduce_scatter | solution.py:228
  1756.6 104.0 %reduce-scatter.47.cloned.1.call-start = ((), (), s32[]{:S(2)}) async-start(), calls=%async_computation.47 | async-start | bytes 2621440 | tf_op jit(solution)/shard_map/reduce_scatter | solution.py:228
  (461 other events, 10581.4 us)
Sparse Core Ops, SparseCore 0:
  13.1 48.4 all-gather.24
  66.7 45.2 all-gather.16
  160.2 43.1 reduce-scatter.16
  208.1 45.2 all-gather.26
  260.3 44.7 all-gather.18
  370.8 43.1 reduce-scatter.18
  418.9 45.2 all-gather.28
  469.4 44.7 all-gather.20
  562.6 43.1 reduce-scatter.20
  609.7 45.2 all-gather.30
  656.9 44.6 all-gather.40
  703.0 44.6 all-gather.22
  749.7 44.6 all-gather.32
  884.6 43.1 reduce-scatter.32
  930.1 43.1 reduce-scatter.30
  976.1 43.1 reduce-scatter.22
  1024.4 45.2 all-gather.34
  1071.3 44.6 all-gather.42
  1272.4 44.3 all-gather.44
  1318.2 44.6 all-gather.36
  1505.6 43.1 reduce-scatter.44
  1555.6 44.3 all-gather.46
  1601.3 44.6 all-gather.38
  1756.7 48.7 reduce-scatter.38
  (8 shorter events, 338.6 us)

commit v2 on v1

v2 whole, which is shorter than its diff:
```python
import functools

import jax
import jax.numpy as jnp
from jax import lax
from jax.experimental import pallas as pl
from jax.experimental.pallas import tpu as pltpu
from jax.sharding import PartitionSpec as P

D = 2048
H = 32
DH = 64
NB = 32
LAYERS = 2
MICRO = 2
LEN = 1024
TILE = 256
NEAR = 5
NEG = -1000000000.0
HIGH = lax.Precision.HIGHEST
ROWS = 256
GELU_A = 0.7978845608028654
GELU_B = 0.044715


def lanes_of(head, heads):
    wide = min(2, heads) * DH
    start = head * DH // wide * wide
    return slice(start, start + wide)


def pick(values, head, heads):
    values = values[:, lanes_of(head, heads)]
    if heads == 1:
        return values
    lane = lax.broadcasted_iota(jnp.int32, values.shape, 1)
    return jnp.where((lane // DH) == head % 2, values, jnp.zeros_like(values))


def join(rows, heads):
    if heads == 1:
        return rows[0]
    return jnp.concatenate([rows[h][h % 2 * DH : h % 2 * DH + DH] for h in range(heads)], 0)


def nt(a, b):
    return lax.dot_general(a, b, (((1,), (1,)), ((), ())), preferred_element_type=jnp.float32)


def nn(a, b):
    return lax.dot_general(a, b, (((1,), (0,)), ((), ())), preferred_element_type=jnp.float32)


def build_bias(heads, w_ref, bias):
    for h in range(heads):
        for d in range(NEAR):
            wide = jnp.broadcast_to(w_ref[h, d : d + 1, :], (TILE, 2 * TILE))
            if 0 < d < NEAR - 1:
                wide = pltpu.roll(wide, 0, 1, stride=1, stride_axis=0)
            bias[h, d] = wide[:, :TILE]


def fwd_kernel(heads, span, segr, segc, q_ref, k_ref, v_ref, w_ref, o_ref, lse_ref, bias, turned):
    iq = pl.program_id(0)

    @pl.when(iq == 0)
    def _():
        build_bias(heads, w_ref, bias)
        turned[...] = v_ref[...].T

    q = q_ref[...]
    row_seg = segr[...]
    queries = [pick(q, h, heads) for h in range(heads)]
    wide = min(2, heads) * DH

    def step(kc, carry):
        rows = pl.ds(pl.multiple_of(kc * TILE, TILE), TILE)
        near = jnp.clip(kc - iq + 2, 0, NEAR - 1)
        allowed = segc[rows, :] == row_seg
        k = k_ref[rows, :]
        out = []
        for h in range(heads):
            high, total, acc = carry[h]
            s = nt(k[:, lanes_of(h, heads)], queries[h]) + bias[h, near]
            s = jnp.where(allowed, s, NEG)
            top = jnp.maximum(high, jnp.max(s, axis=0, keepdims=True))
            scale = jnp.exp(high - top)
            e = jnp.exp(s - top)
            total = total * scale + jnp.sum(e, axis=0, keepdims=True)
            acc = acc * scale + nn(turned[lanes_of(h, heads), rows], e.astype(jnp.bfloat16))
            out.append((top, total, acc))
        return tuple(out)

    start = (
        jnp.full((1, TILE), 2 * NEG, jnp.float32),
        jnp.zeros((1, TILE), jnp.float32),
        jnp.zeros((wide, TILE), jnp.float32),
    )
    done = lax.fori_loop(span[0, iq], span[1, iq], step, (start,) * heads)
    lse_ref[...] = jnp.zeros_like(lse_ref)
    for h in range(heads):
        lse_ref[h : h + 1, :] = done[h][0] + jnp.log(done[h][1])
    out = join([acc / total for _, total, acc in done], heads)
    o_ref[...] = out.T.astype(o_ref.dtype)


def bwd_kernel(
    heads,
    span,
    segr,
    segc,
    q_ref,
    k_ref,
    v_ref,
    w_ref,
    o_ref,
    lse_ref,
    go_ref,
    gq_ref,
    gk_ref,
    gv_ref,
    gb_ref,
    bias,
    gbias,
    gk_acc,
    gv_acc,
    turned,
):
    iq = pl.program_id(0)

    @pl.when(iq == 0)
    def _():
        build_bias(heads, w_ref, bias)
        turned[...] = k_ref[...].T
        gbias[...] = jnp.zeros_like(gbias)
        gk_acc[...] = jnp.zeros_like(gk_acc)
        gv_acc[...] = jnp.zeros_like(gv_acc)

    q = q_ref[...]
    go = go_ref[...]
    row_seg = segr[...]
    prod = (o_ref[...].astype(jnp.float32) * go.astype(jnp.float32)).T
    queries = [pick(q, h, heads) for h in range(heads)]
    outs = [pick(go, h, heads) for h in range(heads)]
    lse = [lse_ref[h : h + 1, :] for h in range(heads)]
    delta = [
        jnp.sum(prod[h * DH : (h + 1) * DH, :], axis=0, keepdims=True) for h in range(heads)
    ]
    wide = min(2, heads) * DH

    def step(kc, carry):
        rows = pl.ds(pl.multiple_of(kc * TILE, TILE), TILE)
        near = jnp.clip(kc - iq + 2, 0, NEAR - 1)
        allowed = segc[rows, :] == row_seg
        k = k_ref[rows, :]
        v = v_ref[rows, :]
        result = []
        for h in range(heads):
            lanes = lanes_of(h, heads)
            s = nt(k[:, lanes], queries[h]) + bias[h, near]
            s = jnp.where(allowed, s, NEG)
            p = jnp.exp(s - lse[h])
            gp = nt(v[:, lanes], outs[h])
            gs = (p * (gp - delta[h])).astype(jnp.bfloat16)
            gv_acc[rows, lanes] += nn(p.astype(jnp.bfloat16), outs[h])
            gk_acc[rows, lanes] += nn(gs, queries[h])
            gbias[h, near] += gs.astype(jnp.float32)
            result.append(carry[h] + nn(turned[lanes, rows], gs))
        return tuple(result)

    start = (jnp.zeros((wide, TILE), jnp.float32),) * heads
    done = lax.fori_loop(span[0, iq], span[1, iq], step, start)
    gq_ref[...] = join(done, heads).T.astype(gq_ref.dtype)

    @pl.when(iq == pl.num_programs(0) - 1)
    def _():
        gk_ref[...] = gk_acc[...].astype(gk_ref.dtype)
        gv_ref[...] = gv_acc[...].astype(gv_ref.dtype)
        gb_ref[...] = jnp.zeros_like(gb_ref)
        down = lax.broadcasted_iota(jnp.int32, (TILE, TILE), 0)
        across = lax.broadcasted_iota(jnp.int32, (TILE, TILE), 1)
        flip = (down + across == TILE - 1).astype(jnp.float32)
        for h in range(heads):
            for d in range(NEAR):
                tile = gbias[h, d]
                if 0 < d < NEAR - 1:
                    tile = lax.dot_general(
                        flip,
                        tile,
                        (((1,), (0,)), ((), ())),
                        precision=HIGH,
                        preferred_element_type=jnp.float32,
                    )
                wide = jnp.concatenate([tile, jnp.zeros_like(tile)], axis=1)
                if 0 < d < NEAR - 1:
                    wide = pltpu.roll(wide, 0, 1, stride=1, stride_axis=0)
                gb_ref[h, d : d + 1, :] = jnp.sum(wide, axis=0, keepdims=True)


def parts_of(qkv, width):
    if width % 128 == 0:
        return [(qkv, n) for n in range(3)]
    return [(qkv[:, n * width : (n + 1) * width], 0) for n in range(3)]


def seen_specs(qkv, heads):
    width = heads * DH
    (qa, q0), (ka, k0), (va, v0) = parts_of(qkv, width)
    specs = [
        pl.BlockSpec((1, TILE), lambda i, s: (0, i)),
        pl.BlockSpec((LEN, 1), lambda i, s: (0, 0)),
        pl.BlockSpec((TILE, width), lambda i, s: (i, q0)),
        pl.BlockSpec((LEN, width), lambda i, s: (0, k0)),
        pl.BlockSpec((LEN, width), lambda i, s: (0, v0)),
        pl.BlockSpec((heads, NEAR, 2 * TILE), lambda i, s: (0, 0, 0)),
    ]
    return specs, (qa, ka, va)


def attend(qkv, span, segr, segc, w):
    heads = w.shape[0]
    width = heads * DH
    specs, parts = seen_specs(qkv, heads)
    tile = pl.BlockSpec((TILE, width), lambda i, s: (i, 0))
    sums = pl.BlockSpec((8, TILE), lambda i, s: (0, i))
    grid = pltpu.PrefetchScalarGridSpec(
        num_scalar_prefetch=1,
        grid=(LEN // TILE,),
        in_specs=specs,
        out_specs=[tile, sums],
        scratch_shapes=[
            pltpu.VMEM((heads, NEAR, TILE, TILE), jnp.float32),
            pltpu.VMEM((width, LEN), jnp.bfloat16),
        ],
    )
    return pl.pallas_call(
        functools.partial(fwd_kernel, heads),
        grid_spec=grid,
        out_shape=[
            jax.ShapeDtypeStruct((LEN, width), jnp.bfloat16),
            jax.ShapeDtypeStruct((8, LEN), jnp.float32),
        ],
        compiler_params=pltpu.CompilerParams(vmem_limit_bytes=40 * 1024 * 1024),
        cost_estimate=pl.CostEstimate(flops=0, bytes_accessed=0, transcendentals=0),
    )(span, segr, segc, *parts, w)


def attend_back(qkv, span, segr, segc, w, o, lse, go):
    heads = w.shape[0]
    width = heads * DH
    specs, parts = seen_specs(qkv, heads)
    tile = pl.BlockSpec((TILE, width), lambda i, s: (i, 0))
    sums = pl.BlockSpec((8, TILE), lambda i, s: (0, i))
    whole = pl.BlockSpec((LEN, width), lambda i, s: (0, 0))
    grid = pltpu.PrefetchScalarGridSpec(
        num_scalar_prefetch=1,
        grid=(LEN // TILE,),
        in_specs=specs + [tile, sums, tile],
        out_specs=[tile, whole, whole, pl.BlockSpec((heads, 8, 2 * TILE), lambda i, s: (0, 0, 0))],
        scratch_shapes=[pltpu.VMEM((heads, NEAR, TILE, TILE), jnp.float32)] * 2
        + [pltpu.VMEM((LEN, width), jnp.float32)] * 2
        + [pltpu.VMEM((width, LEN), jnp.bfloat16)],
    )
    flat = jax.ShapeDtypeStruct((LEN, width), jnp.bfloat16)
    return pl.pallas_call(
        functools.partial(bwd_kernel, heads),
        grid_spec=grid,
        out_shape=[flat, flat, flat, jax.ShapeDtypeStruct((heads, 8, 2 * TILE), jnp.float32)],
        compiler_params=pltpu.CompilerParams(vmem_limit_bytes=40 * 1024 * 1024),
        cost_estimate=pl.CostEstimate(flops=0, bytes_accessed=0, transcendentals=0),
    )(span, segr, segc, *parts, w, o, lse, go)


THRESHOLDS = (12, 16, 23, 32, 46, 64, 91)
def bucket_of(offset):
    distance = jnp.abs(offset)
    beyond = 8 + sum(((distance >= threshold).astype(jnp.int32) for threshold in THRESHOLDS))
    within = jnp.where(distance < 8, distance, beyond)
    return jnp.where(offset > 0, 16, 0) + within

def near_table(back):
    place = jnp.arange(2*TILE, dtype=jnp.int32)
    turn = place - (TILE - 1) if back else jnp.where(place < TILE, place, place - 2*TILE)
    offset = TILE*(jnp.arange(NEAR, dtype=jnp.int32) - 2)[:, None] - turn[None, :]
    return (bucket_of(offset)[:, :, None] == jnp.arange(NB, dtype=jnp.int32)).astype(jnp.float32)

def segment_views(segment):
    places = jnp.arange(LEN, dtype=jnp.int32)
    own = jnp.where(segment == 0, 4 + places, segment)
    order = jnp.where(segment == 0, 4, segment).reshape(-1, TILE)
    low, high = order[:, 0], order[:, -1]
    lo = jnp.sum((high[None, :] < low[:, None]).astype(jnp.int32), axis=1)
    hi = jnp.sum((low[None, :] <= high[:, None]).astype(jnp.int32), axis=1)
    return jnp.stack((lo, hi)), own[None, :], own[:, None]


NN = ((1,), (0,))
NT = ((1,), (1,))
TN = ((0,), (0,))
BF = jnp.bfloat16
F32 = jnp.float32


def core_swap(values):
    return lax.ppermute(values, "gx", [(0, 1), (1, 0)])


def token_gather(values):
    return lax.all_gather(values, "gy", axis=0, tiled=True)


def token_reduce(values):
    return lax.psum_scatter(values, "gy", scatter_dimension=0, tiled=True).astype(F32)


def shifted(values, step):
    size = lax.axis_size("gy")
    return lax.ppermute(values, "gy", [(n, (n + step) % size) for n in range(size)])


def dot(left, right, dims):
    return lax.dot_general(left, right, (dims, ((), ())), preferred_element_type=F32)


def rows_kernel(dims, count, extras, finish, *refs):
    total = None
    for n in range(count):
        part = dot(refs[n][...], refs[count + n][...], dims)
        total = part if total is None else total + part
    inner = 2 * count + extras
    finish(total, [ref[...] for ref in refs[2 * count : inner]], refs[inner:])


def keep_rounded(total, extras, outs):
    outs[0][...] = total.astype(BF)


def add_rounded(total, extras, outs):
    outs[0][...] = (total + extras[0].astype(F32)).astype(BF)


def gelu_parts(gate):
    inner = GELU_A * (gate + GELU_B * gate * gate * gate)
    half = 0.5 * (1.0 + jnp.tanh(inner))
    return half, gate * half


def gate_rounded(total, extras, outs):
    total = total + extras[0].astype(F32)
    width = total.shape[1] // 2
    gate, up = total[:, :width], total[:, width:]
    outs[0][...] = total.astype(BF)
    outs[1][...] = (gelu_parts(gate)[1] * up).astype(BF)


def gate_back_rounded(total, extras, outs):
    grad = total + extras[0].astype(F32)
    width = grad.shape[1]
    gate = extras[1][:, :width].astype(F32)
    up = extras[1][:, width:].astype(F32)
    half, value = gelu_parts(gate)
    slope = half + 2.0 * gate * half * (1.0 - half) * GELU_A * (1.0 + 3.0 * GELU_B * gate * gate)
    outs[0][:, :width] = (grad * up * slope).astype(BF)
    outs[0][:, width:] = (grad * value).astype(BF)


def rows_dot(parts, weights, dims, finish=keep_rounded, extras=(), widths=None):
    rows = parts[0].shape[0]
    if widths is None:
        widths = (weights[0].shape[1 - dims[1][0]],)
    outs = [jax.ShapeDtypeStruct((rows, width), BF) for width in widths]
    if not all(item.shape[1] % 128 == 0 for item in (*parts, *weights, *extras, *outs)):
        return plain_dot(parts, weights, dims, finish, extras, outs)
    tall = min(rows, ROWS)

    def sliced(item):
        return pl.BlockSpec((tall, item.shape[1]), lambda i: (i, 0))

    def whole(item):
        return pl.BlockSpec(item.shape, lambda i: (0, 0))

    result = pl.pallas_call(
        functools.partial(rows_kernel, dims, len(parts), len(extras), finish),
        grid=(rows // tall,),
        in_specs=[sliced(item) for item in parts]
        + [whole(item) for item in weights]
        + [sliced(item) for item in extras],
        out_specs=[sliced(item) for item in outs],
        out_shape=outs,
        compiler_params=pltpu.CompilerParams(vmem_limit_bytes=40 * 1024 * 1024),
        cost_estimate=pl.CostEstimate(flops=0, bytes_accessed=0, transcendentals=0),
    )(*parts, *weights, *extras)
    return result[0] if len(outs) == 1 else result


class Holder:
    def __init__(self, shape):
        self.value = jnp.zeros(shape.shape, shape.dtype)

    def __setitem__(self, place, value):
        self.value = value if place is Ellipsis else self.value.at[place].set(value)


def plain_dot(parts, weights, dims, finish, extras, outs):
    total = sum(dot(part, weight, dims) for part, weight in zip(parts, weights))
    held = [Holder(item) for item in outs]
    finish(total, extras, held)
    return held[0].value if len(held) == 1 else [item.value for item in held]


def row_norm(hidden):
    part = jnp.sum(hidden * hidden, axis=1)
    return lax.rsqrt((part + core_swap(part)) / D + 1e-06)


def norm_back(grad_norm, hidden, scale, gain):
    weighted = grad_norm * gain
    part = jnp.sum(weighted * hidden, axis=1)
    inner = part + core_swap(part)
    cubed = scale * scale * scale * inner / D
    grad_hidden = scale[:, None] * weighted - hidden * cubed[:, None]
    gain_grad = jnp.sum(grad_norm * hidden * scale[:, None], axis=0)
    return grad_hidden, gain_grad


def halves(weights, axis, core):
    width = weights.shape[axis] // 2
    own = lax.dynamic_slice_in_dim(weights, core * width, width, axis)
    other = lax.dynamic_slice_in_dim(weights, (1 - core) * width, width, axis)
    return own, other


def in_order(own, other, core, axis):
    return jnp.where(
        core == 0,
        jnp.concatenate((own, other), axis),
        jnp.concatenate((other, own), axis),
    )


def paired(*weights):
    cut = [jnp.split(item, 2, axis=1) for item in weights]
    return jnp.concatenate([item[n] for n in range(2) for item in cut], 1)


def unpaired(values, count):
    cut = jnp.split(values, 2 * count, axis=1)
    return [jnp.concatenate((cut[n], cut[count + n]), 1) for n in range(count)]


def link_swap(values, bits):
    size = lax.axis_size("dp")
    pairs = [(n * 2 + c, (n ^ bits[c]) * 2 + c) for n in range(size) for c in range(2)]
    return lax.ppermute(values, ("dp", "gx"), pairs)


def take_half(values, which):
    rows = values.shape[0] // 2
    return lax.dynamic_slice_in_dim(values, which * rows, rows, 0)


def stack_half(own, other, which):
    return jnp.where(
        which == 0,
        jnp.concatenate((own, other), 0),
        jnp.concatenate((other, own), 0),
    )


def batch_steps(place, core):
    size = lax.axis_size("dp")
    bits = [1 << n for n in range(size.bit_length() - 1)]
    steps = []
    for first, second in zip(bits, bits[::-1]):
        bit = jnp.where(core == 0, first, second)
        steps.append(((first, second), jnp.where((place & bit) != 0, 1, 0)))
    return steps


def settle_kernel(core_cut, count, place, own_ref, other_ref, *refs):
    outs = refs[-count:]
    half = pl.program_id(0)

    def store(values, core):
        width = values.shape[1] // (2 * count)
        for n in range(count):
            for part in range(2):
                start = (part * count + n) * width
                spot = (part ^ core) * width
                outs[n][0, :, spot : spot + width] = values[:, start : start + width].astype(F32)

    for source, ref in enumerate((own_ref, other_ref)):

        @pl.when((half ^ place[0]) == source)
        def _():
            if not core_cut:
                outs[0][0] = ref[...].astype(F32)
            for core in range(2 if core_cut else 0):

                @pl.when(place[1] == core)
                def _():
                    store(ref[...], core)


def settle(own, other, flag, core, layer, base, core_cut, targets, shapes):
    rows, width = own.shape
    whole = pl.BlockSpec((rows, width), lambda i, s: (0, 0))
    grid = pltpu.PrefetchScalarGridSpec(
        num_scalar_prefetch=1,
        grid=(2,),
        in_specs=[whole, whole] + [pl.BlockSpec(memory_space=pl.ANY)] * len(targets),
        out_specs=[
            pl.BlockSpec((1, rows, item.shape[2]), lambda i, s: (layer, base + i, 0))
            for item in shapes
        ],
    )
    return pl.pallas_call(
        functools.partial(settle_kernel, core_cut, len(shapes)),
        grid_spec=grid,
        out_shape=shapes,
        input_output_aliases={3 + n: n for n in range(len(targets))},
        compiler_params=pltpu.CompilerParams(vmem_limit_bytes=40 * 1024 * 1024),
        cost_estimate=pl.CostEstimate(flops=0, bytes_accessed=0, transcendentals=0),
    )(jnp.stack((flag, core)).astype(jnp.int32), own, other, *targets)


def axis_sum(values, axis):
    size = lax.axis_size(axis)

    def swapped(item, bits):
        return lax.ppermute(item, axis, [(n, n ^ bits) for n in range(size)])

    if size == 4:
        one, two, three = (swapped(values, bits) for bits in (1, 2, 3))
        return (values + one) + (two + three)
    bit = 1
    while bit < size:
        values = values + swapped(values, bit)
        bit *= 2
    return values


class Order:
    def __init__(self):
        self.last = None

    def enter(self, *values):
        if self.last is None:
            return values
        return lax.optimization_barrier((*values, self.last))[:-1]

    def leave(self, value):
        self.last = value


def body(
    inputs,
    cotangent,
    segments,
    attention_gain,
    query_weight,
    key_weight,
    value_weight,
    mixing_weight,
    relative_bias,
    dense_gain,
    gate_weight,
    up_weight,
    down_weight,
):
    core = lax.axis_index("gx")
    block = lax.axis_index("gy")
    place = lax.axis_index("dp")
    row_count = inputs.shape[1]
    col_count = inputs.shape[2]
    col_start = core * col_count
    heads_dev = query_weight.shape[2] // (2 * DH)
    head_start = (block * 2 + core) * heads_dev
    hidden_dev = gate_weight.shape[2] // 2
    ahead = near_table(False)
    behind = near_table(True)
    steps = batch_steps(place, core)
    order = Order()
    later = []
    flows = []
    summed = []
    ends = []
    results = {}
    tidy = hidden_dev % 128 == 0 and (heads_dev * DH) % 128 == 0
    shapes = [
        [jax.ShapeDtypeStruct(item.shape, F32) for item in group]
        for group in (
            (query_weight, key_weight, value_weight),
            (gate_weight, up_weight),
            (mixing_weight,),
            (down_weight,),
        )
    ]
    layers = []
    for layer in range(LAYERS):
        qkv = paired(query_weight[layer], key_weight[layer], value_weight[layer])
        gu = paired(gate_weight[layer], up_weight[layer])
        table = lax.dynamic_slice_in_dim(relative_bias[layer], head_start, heads_dev, 1)
        layers.append(
            dict(
                qkv_half=halves(qkv, 1, core),
                gu_half=halves(gu, 1, core),
                mix_half=halves(mixing_weight[layer], 0, core),
                down_half=halves(down_weight[layer], 0, core),
                bias=jnp.einsum("dcb,bh->hdc", ahead, table, precision=HIGH),
                gain1=lax.dynamic_slice_in_dim(attention_gain[layer], col_start, col_count),
                gain2=lax.dynamic_slice_in_dim(dense_gain[layer], col_start, col_count),
            )
        )
    acc = [dict() for _ in range(LAYERS)]

    def add(layer, name, value):
        have = acc[layer].get(name)
        acc[layer][name] = value if have is None else have + value

    def batch_flow(layer, name, kept, start):
        axis = 0 if name in ("down", "mix") else 1
        rows = kept.shape[0]
        for bits, mine in steps:
            (kept,) = order.enter(kept)
            send = take_half(kept, 1 - mine)
            order.leave(send)
            come = link_swap(send, bits)
            yield
            come, kept = order.enter(come, kept)
            kept = (take_half(kept, mine).astype(F32) + come.astype(F32)).astype(BF)
            order.leave(kept)
        for bits, mine in reversed(steps[1:]):
            come = link_swap(kept, bits)
            yield
            come, kept = order.enter(come, kept)
            kept = stack_half(kept, come, mine)
            order.leave(kept)
        bits, mine = steps[0]
        come = link_swap(kept, bits)
        yield
        come, kept = order.enter(come, kept)
        if tidy:
            group = ("qkv", "gu", "mix", "down").index(name)
            flag = (mine ^ core) if axis == 0 else mine
            base = start // (rows // 2)
            targets = results.get(name, [])
            results[name] = settle(
                kept, come, flag, core, layer, base, axis == 1, targets, shapes[group]
            )
            order.leave(results[name][0])
        else:
            kept = stack_half(kept, come, mine).astype(F32)
            order.leave(kept)
            results.setdefault((layer, name), []).append(kept)

    def small_flow():
        gain = jnp.stack([acc[n][name] for name in ("gain1", "gain2") for n in range(LAYERS)])
        gain = lax.dynamic_update_slice_in_dim(jnp.zeros((2 * LAYERS, D), F32), gain, col_start, 1)
        bias = jnp.stack([acc[n]["bias"][:, :NEAR] for n in range(LAYERS)])
        bias = jnp.einsum("lhdc,dcb->lbh", bias, behind, precision=HIGH)
        bias = lax.dynamic_update_slice_in_dim(
            jnp.zeros((LAYERS, NB, H), F32), bias, head_start, 2
        )
        total = jnp.concatenate((gain.reshape(-1, 128), bias.reshape(-1, 128)), 0)
        for axis in ("gx", "gy", "dp"):
            (total,) = order.enter(total)
            total = axis_sum(total, axis)
            yield
            (total,) = order.enter(total)
            order.leave(total)
        split = gain.size // 128
        summed.append(total[:split].reshape(gain.shape))
        summed.append(total[split:].reshape(bias.shape))

    def weight_grads():
        for layer, name, left, right in later:
            last = name in acc[layer]
            have = acc[layer].get(name, (None, None))
            left = order.enter(*left)
            right = order.enter(*right)
            both = [dot(a, b, TN) for a in left for b in right]
            if last:
                both = [a + b for a, b in zip(have, both)]
            acc[layer][name] = both
            order.leave(both[1])
            if last:
                axis = 0 if name in ("down", "mix") else 1
                total = jnp.concatenate([item.astype(BF) for item in both], axis)
                order.leave(total)
                flow = batch_flow(layer, name, total, 0)
                next(flow)
                flows.append(flow)
        later.clear()

    def run_later():
        for flow in list(flows):
            if next(flow, "end") == "end":
                flows.remove(flow)
        weight_grads()

    def forward(micro):
        seg_all = segments[micro]
        row_segs = lax.dynamic_slice_in_dim(seg_all, block * row_count, row_count)
        keep = (row_segs != 0).astype(F32)[:, None]
        views = segment_views(seg_all)
        hidden = inputs[micro].astype(F32)
        saved = []
        for layer in range(LAYERS):
            w = layers[layer]
            scale1 = row_norm(hidden)
            normed = (hidden * scale1[:, None] * w["gain1"]).astype(BF)
            order.leave(normed)
            normed = token_gather(normed)
            yield
            (normed,) = order.enter(normed)
            come = core_swap(rows_dot([normed], w["qkv_half"][1:], NN))
            qkv = rows_dot([normed], w["qkv_half"][:1], NN, add_rounded, [come])
            own, lse = attend(qkv, *views, w["bias"])
            mixed = [own, core_swap(own)]
            branch = rows_dot(mixed, w["mix_half"], NN)
            order.leave(branch)
            branch = token_reduce(branch)
            yield
            (branch,) = order.enter(branch)
            middle = hidden + branch
            scale2 = row_norm(middle)
            dense = (middle * scale2[:, None] * w["gain2"]).astype(BF)
            order.leave(dense)
            dense = token_gather(dense)
            yield
            (dense,) = order.enter(dense)
            come = core_swap(rows_dot([dense], w["gu_half"][1:], NN))
            gate_up, active = rows_dot(
                [dense],
                w["gu_half"][:1],
                NN,
                gate_rounded,
                [come],
                (2 * hidden_dev, hidden_dev),
            )
            active = [active, core_swap(active)]
            out = rows_dot(active, w["down_half"], NN)
            order.leave(out)
            saved.append(
                (hidden, scale1, normed, qkv, lse, mixed, middle, scale2, dense)
                + (gate_up, active)
            )
            if layer == LAYERS - 1:
                break
            out = token_reduce(out)
            yield
            (out,) = order.enter(out)
            hidden = middle + out
        ends.append((middle, out, keep))
        grad = cotangent[micro].astype(F32) * keep
        for layer in reversed(range(LAYERS)):
            w = layers[layer]
            hidden, scale1, normed, qkv, lse, mixed = saved[layer][:6]
            middle, scale2, dense, gate_up, active = saved[layer][6:]
            grad_out = grad.astype(BF)
            order.leave(grad_out)
            grad_out = token_gather(grad_out)
            yield
            (grad_out,) = order.enter(grad_out)
            come = core_swap(rows_dot([grad_out], w["down_half"][1:], NT))
            pair = rows_dot(
                [grad_out],
                w["down_half"][:1],
                NT,
                gate_back_rounded,
                [come, gate_up],
                (2 * hidden_dev,),
            )
            pair = [pair, core_swap(pair)]
            grad_dense = rows_dot(pair, w["gu_half"], NT)
            order.leave(grad_dense)
            grad_dense = token_reduce(grad_dense)
            later.append((layer, "down", active, [grad_out]))
            later.append((layer, "gu", [dense], pair))
            yield
            (grad_dense,) = order.enter(grad_dense)
            grad_norm, gain_part = norm_back(grad_dense, middle, scale2, w["gain2"])
            add(layer, "gain2", gain_part)
            grad_mid = grad + grad_norm
            grad_out = grad_mid.astype(BF)
            order.leave(grad_out)
            grad_out = token_gather(grad_out)
            yield
            (grad_out,) = order.enter(grad_out)
            come = core_swap(rows_dot([grad_out], w["mix_half"][1:], NT))
            grad_mixed = rows_dot([grad_out], w["mix_half"][:1], NT, add_rounded, [come])
            if layer == 0 and micro == MICRO - 1:
                order.leave(grad_mixed)
                later.append((layer, "mix", mixed, [grad_out]))
                weight_grads()
                (grad_mixed,) = order.enter(grad_mixed)
            gq, gk, gv, gb = attend_back(qkv, *views, w["bias"], mixed[0], lse, grad_mixed)
            add(layer, "bias", gb)
            triple = jnp.concatenate((gq, gk, gv), 1)
            triple = [triple, core_swap(triple)]
            grad_normed = rows_dot(triple, w["qkv_half"], NT)
            order.leave(grad_normed)
            grad_normed = token_reduce(grad_normed)
            if layer == 0 and micro == MICRO - 1:
                for n, (middle, out, keep) in enumerate(ends):
                    (out,) = order.enter(out)
                    outputs[n] = (middle + token_reduce(out)) * keep
            if layer > 0 or micro < MICRO - 1:
                later.append((layer, "mix", mixed, [grad_out]))
            later.append((layer, "qkv", [normed], triple))
            yield
            (grad_normed,) = order.enter(grad_normed)
            grad_norm, gain_part = norm_back(grad_normed, hidden, scale1, w["gain1"])
            add(layer, "gain1", gain_part)
            grad = grad_mid + grad_norm
        grads[micro] = grad

    outputs = [None] * MICRO
    grads = [None] * MICRO
    micro_flows = [forward(micro) for micro in range(MICRO)]
    live = list(micro_flows)
    while live:
        for flow in list(live):
            if next(flow, "end") == "end":
                live.remove(flow)
        run_later()
    flow = small_flow()
    next(flow)
    flows.append(flow)
    while flows:
        run_later()
    gain, bias = summed
    if not tidy:
        for name, count in (("qkv", 3), ("gu", 2), ("mix", 1), ("down", 1)):
            axis = 0 if count == 1 else 1
            whole = []
            for layer in range(LAYERS):
                both = jnp.split(jnp.concatenate(results[layer, name], 0), 2, axis)
                ordered = in_order(*both, core, axis)
                whole.append([ordered] if count == 1 else unpaired(ordered, count))
            results[name] = [
                jnp.stack([whole[layer][n] for layer in range(LAYERS)]) for n in range(count)
            ]
    grad_query, grad_key, grad_value = results["qkv"]
    grad_gate, grad_up = results["gu"]
    (grad_mixing,) = results["mix"]
    (grad_down,) = results["down"]
    return (
        jnp.stack(outputs),
        jnp.stack(grads),
        gain[:LAYERS],
        grad_query,
        grad_key,
        grad_value,
        grad_mixing,
        bias,
        gain[LAYERS:],
        grad_gate,
        grad_up,
        grad_down,
    )


def solution(mesh):
    tokens = P(None, ("dp", "gy"), "gx")
    wide = P(None, "gx", "gy")
    tall = P(None, "gy", "gx")
    return jax.shard_map(
        body,
        mesh=mesh,
        in_specs=(tokens, tokens, P(None, "dp"), P())
        + (wide, wide, wide, tall, P(), P(), wide, wide, tall),
        out_specs=(tokens, tokens, P(), wide, wide, wide, tall, P(), P(), wide, wide, tall),
        check_vma=False,
    )
```

time: 1900 us -> 1690 us (0.89)
  matrix products: 309 us -> 92 us
  Pallas kernels: 217 us -> 378 us
  local copies, waits for them, and re-layouts: 91.6 us -> 217 us
  starting transfers between devices: 169 us -> 52 us
  waiting for transfers between devices: 891 us -> 794 us
  other arithmetic: 197 us -> 122 us
    dot_general x97 -> x33, matrix products: 309 us -> 91.3 us  [the longest x32 91.1 us: dot(): lax.dot_general(left, right, (dims, ((), ())), preferred_element_type=F32)]
    pallas_call x8 -> x64, Pallas kernels: 217 us -> 378 us  [the longest x48 184 us: rows_dot(): pl.pallas_call(functools.partial(rows_kernel, dims, len(parts), len(extra...]
    unnamed x553 -> x549, local copies, waits for them, and re-layouts: 29.3 us -> 144 us
    ppermute x133 -> x39, starting transfers between devices: 156 us -> 42.5 us  [the longest x32 34.3 us: link_swap(): return lax.ppermute(values, ('dp', 'gx'), pairs)]
    all_gather x16, waiting for transfers between devices: 396 us -> 304 us  [token_gather(): return lax.all_gather(values, 'gy', axis=0, tiled=True)]
    reduce_scatter x16, waiting for transfers between devices: 229 us -> 169 us  [token_reduce(): lax.psum_scatter(values, 'gy', scatter_dimension=0, tiled=True).astype(F32)]
    select_n x78 -> x8, other arithmetic: 68.7 us -> 21.8 us  [stack_half(): jnp.where(which == 0, jnp.concatenate((own, other), 0), jnp.concatenate((...]
    ppermute x48, waiting for transfers between devices: 30.8 us -> 72.6 us  [core_swap(): return lax.ppermute(values, 'gx', [(0, 1), (1, 0)])]
  transfers between devices with their start and end apart: 213 -> 119, of which waited for: 123 -> 71; matrix products, arithmetic and copies ran while one was open for 28% -> 17% of each run, Pallas kernels for 10% -> 22%
where the time goes in v2:
time: 1690 us; the launch traced here: 1670 us
  waiting for transfers between devices  794 us (47%)
  Pallas kernels  378 us (22%)
  local copies, waits for them, and re-layouts  217 us (13%)
  other arithmetic  122 us (7%)
  matrix products  92 us (5%)
  starting transfers between devices  52 us (3%)
  between operations  17.8 us (1%)
    all_gather x16, waiting for transfers between devices, token_gather(): return lax.all_gather(values, 'gy', axis=0, tiled=True)  304 us
    ppermute x32, waiting for transfers between devices, link_swap(): return lax.ppermute(values, ('dp', 'gx'), pairs)  238 us
    pallas_call x48, Pallas kernels, rows_dot(): pl.pallas_call(functools.partial(rows_kernel, dims, len(parts), len(extra...  184 us
    reduce_scatter x16, waiting for transfers between devices, token_reduce(): lax.psum_scatter(values, 'gy', scatter_dimension=0, tiled=True).astype(F32)  169 us
    unnamed x549, local copies, waits for them, and re-layouts  144 us
    dot_general x32, matrix products, dot(): lax.dot_general(left, right, (dims, ((), ())), preferred_element_type=F32)  91.1 us
    pallas_call x4, Pallas kernels, attend_back(): pl.pallas_call(functools.partial(bwd_kernel, heads), grid_spec=grid, out_...  81.7 us
    pallas_call x4, Pallas kernels, attend(): pl.pallas_call(functools.partial(fwd_kernel, heads), grid_spec=grid, out_...  74.9 us
  transfers between devices with their start and end apart: 119, of which 71 were waited for; matrix products, arithmetic and copies ran while one was open for 17% of the time, Pallas kernels for 22%

profile of v2, /device:TPU:0, one launch (start us, length us, event | category | flops | bytes accessed | tf_op | source)
XLA Modules:
  0.0 1672.6 jit_solution(15685967408821750766)
XLA Ops:
  27.0 35.2 %all-gather.17.cloned.1.call-done.refs_0_ = bf16[1024,1024]{1,0:T(8,128)(2,1)} async-done(((bf16[256,1024]{1,0:T(8,128)(2,1)}), bf16[1024,1024]{1,0:T(8,128)(2,1)}) %all-gather.17.cloned.1.call-update) | async-done | bytes 2097168 | tf_op jit(solution)/shard_map/all_gather | solution.py:309
  76.3 19.2 %shard_map.222 = (bf16[1024,256]{1,0:T(8,128)(2,1)}, f32[8,1024]{1,0:T(8,128)S(1)}) custom-call(s32[2,4]{1,0:T(2,128)S(1)} %pad_add_fusion.span, s32[1,1024]{1,0:T(1,128)S(1)} %get-tuple-element.505.segr, s32[1024,1]{1,0:T(8,128)S(1)} %compare_select_fusion.1.segc, bf16[1024,768]{1,0:T(8,128)(2,1)S(1)} %shard_map.221.q_ref.k_ref.v_ref, ...), custom_call_target="tpu_custom_call" | custom-call | tf_op jit(solution)/shard_map/pallas_call | solution.py:236
  170.4 30.1 %reduce-scatter.19.cloned.1.call-done = bf16[256,1024]{1,0:T(8,128)(2,1)} async-done(((bf16[1024,1024]{1,0:T(8,128)(2,1)}), bf16[256,1024]{1,0:T(8,128)(2,1)}) %reduce-scatter.19.cloned.1.call-update) | async-done | bytes 524304 | tf_op jit(solution)/shard_map/reduce_scatter | solution.py:313
  207.7 40.0 %all-gather.21.cloned.1.call-done.refs_0_ = bf16[1024,1024]{1,0:T(8,128)(2,1)} async-done(((bf16[256,1024]{1,0:T(8,128)(2,1)}), bf16[1024,1024]{1,0:T(8,128)(2,1)}) %all-gather.21.cloned.1.call-update) | async-done | bytes 2097168 | tf_op jit(solution)/shard_map/all_gather | solution.py:309
  323.6 20.4 %reduce-scatter.21.cloned.1.call-done = bf16[256,1024]{1,0:T(8,128)(2,1)} async-done(((bf16[1024,1024]{1,0:T(8,128)(2,1)}), bf16[256,1024]{1,0:T(8,128)(2,1)}) %reduce-scatter.21.cloned.1.call-update) | async-done | bytes 524304 | tf_op jit(solution)/shard_map/reduce_scatter | solution.py:313
  347.7 42.6 %reduce-scatter.23.cloned.1.call-done = bf16[256,1024]{1,0:T(8,128)(2,1)} async-done(((bf16[1024,1024]{1,0:T(8,128)(2,1)}), bf16[256,1024]{1,0:T(8,128)(2,1)}) %reduce-scatter.23.cloned.1.call-update) | async-done | bytes 524304 | tf_op jit(solution)/shard_map/reduce_scatter | solution.py:313
  399.2 38.5 %all-gather.25.cloned.1.call-done.refs_0_ = bf16[1024,1024]{1,0:T(8,128)(2,1)} async-done(((bf16[256,1024]{1,0:T(8,128)(2,1)}), bf16[1024,1024]{1,0:T(8,128)(2,1)}) %all-gather.25.cloned.1.call-update) | async-done | bytes 2097168 | tf_op jit(solution)/shard_map/all_gather | solution.py:309
  494.2 18.5 %shard_map.240 = (bf16[1024,256]{1,0:T(8,128)(2,1)S(1)}, f32[8,1024]{1,0:T(8,128)S(1)}) custom-call(s32[2,4]{1,0:T(2,128)S(1)} %pad_add_fusion.1.span, s32[1,1024]{1,0:T(1,128)S(1)} %get-tuple-element.509.segr, s32[1024,1]{1,0:T(8,128)S(1)} %copy-done.65, bf16[1024,768]{1,0:T(8,128)(2,1)S(1)} %shard_map.239.q_ref.k_ref.v_ref, ...), custom_call_target="tpu_custom_call" | custom-call | tf_op jit(solution)/shard_map/pallas_call | solution.py:236
  536.2 39.7 %reduce-scatter.27.cloned.1.call-done = bf16[256,1024]{1,0:T(8,128)(2,1)} async-done(((bf16[1024,1024]{1,0:T(8,128)(2,1)}), bf16[256,1024]{1,0:T(8,128)(2,1)}) %reduce-scatter.27.cloned.1.call-update) | async-done | bytes 524304 | tf_op jit(solution)/shard_map/reduce_scatter | solution.py:313
  585.7 37.7 %all-gather.29.cloned.1.call-done.refs_0_ = bf16[1024,1024]{1,0:T(8,128)(2,1)} async-done(((bf16[256,1024]{1,0:T(8,128)(2,1)}), bf16[1024,1024]{1,0:T(8,128)(2,1)}) %all-gather.29.cloned.1.call-update) | async-done | bytes 2097168 | tf_op jit(solution)/shard_map/all_gather | solution.py:309
  632.7 36.7 %all-gather.33.cloned.1.call-done.refs_0_ = bf16[1024,1024]{1,0:T(8,128)(2,1)} async-done(((bf16[256,1024]{1,0:T(8,128)(2,1)}), bf16[1024,1024]{1,0:T(8,128)(2,1)}) %all-gather.33.cloned.1.call-update) | async-done | bytes 2097168 | tf_op jit(solution)/shard_map/all_gather | solution.py:309
  691.9 24.2 %all-gather.35.cloned.1.call-done.refs_0_ = bf16[1024,1024]{1,0:T(8,128)(2,1)} async-done(((bf16[256,1024]{1,0:T(8,128)(2,1)}), bf16[1024,1024]{1,0:T(8,128)(2,1)}) %all-gather.35.cloned.1.call-update) | async-done | bytes 2097168 | tf_op jit(solution)/shard_map/all_gather | solution.py:309
  732.6 29.5 %all-gather.31.cloned.1.call-done.refs_0_ = bf16[1024,1024]{1,0:T(8,128)(2,1)} async-done(((bf16[256,1024]{1,0:T(8,128)(2,1)}), bf16[1024,1024]{1,0:T(8,128)(2,1)}) %all-gather.31.cloned.1.call-update) | async-done | bytes 2097168 | tf_op jit(solution)/shard_map/all_gather | solution.py:309
  860.2 27.8 %collective-permute-done.31 = bf16[640,1024]{1,0:T(8,128)(2,1)} collective-permute-done((bf16[640,1024]{1,0:T(8,128)(2,1)}, bf16[640,1024]{1,0:T(8,128)(2,1)}, u32[]{:S(2)}, u32[]{:S(2)}) %collective-permute-start.31) | collective-permute-done | bytes 1310752 | tf_op jit(solution)/shard_map/ppermute | solution.py:454
  908.8 20.2 %shard_map.255 = (bf16[1024,256]{1,0:T(8,128)(2,1)S(1)}, bf16[1024,256]{1,0:T(8,128)(2,1)S(1)}, bf16[1024,256]{1,0:T(8,128)(2,1)S(1)}, f32[4,8,512]{2,1,0:T(8,128)S(1)}) custom-call(s32[2,4]{1,0:T(2,128)S(1)} %pad_add_fusion.span, s32[1,1024]{1,0:T(1,128)S(1)} %get-tuple-element.505.segr, s32[1024,1]{1,0:T(8,128)S(1)} %copy-done.70, ...), custom_call_target="tpu_custom_call" | custom-call | tf_op jit(solution)/shard_map/pallas_call | solution.py:265
  960.6 20.2 %shard_map.259 = (bf16[1024,256]{1,0:T(8,128)(2,1)S(1)}, bf16[1024,256]{1,0:T(8,128)(2,1)S(1)}, bf16[1024,256]{1,0:T(8,128)(2,1)S(1)}, f32[4,8,512]{2,1,0:T(8,128)S(1)}) custom-call(s32[2,4]{1,0:T(2,128)S(1)} %pad_add_fusion.1.span, s32[1,1024]{1,0:T(1,128)S(1)} %get-tuple-element.509.segr, s32[1024,1]{1,0:T(8,128)S(1)} %copy-done.66, ...), custom_call_target="tpu_custom_call" | custom-call | tf_op jit(solution)/shard_map/pallas_call | solution.py:265
  1070.9 23.2 %collective-permute-done.43 = bf16[320,1024]{1,0:T(8,128)(2,1)} collective-permute-done((bf16[320,1024]{1,0:T(8,128)(2,1)}, bf16[320,1024]{1,0:T(8,128)(2,1)}, u32[]{:S(2)}, u32[]{:S(2)}) %collective-permute-start.43) | collective-permute-done | bytes 655392 | tf_op jit(solution)/shard_map/ppermute | solution.py:454
  1193.7 41.5 %collective-permute-done.51.other_ref = bf16[640,1024]{1,0:T(8,128)(2,1)} collective-permute-done((bf16[640,1024]{1,0:T(8,128)(2,1)}, bf16[640,1024]{1,0:T(8,128)(2,1)}, u32[]{:S(2)}, u32[]{:S(2)}) %collective-permute-start.51) | collective-permute-done | bytes 1310752 | tf_op jit(solution)/shard_map/ppermute | solution.py:454
  1297.9 20.7 %collective-permute-done.57 = bf16[128,1024]{1,0:T(8,128)(2,1)} collective-permute-done((bf16[128,1024]{1,0:T(8,128)(2,1)}, bf16[128,1024]{1,0:T(8,128)(2,1)}, u32[]{:S(2)}, u32[]{:S(2)}) %collective-permute-start.57) | collective-permute-done | bytes 262176 | tf_op jit(solution)/shard_map/ppermute | solution.py:454
  1324.3 23.1 %collective-permute-done.55 = bf16[640,1024]{1,0:T(8,128)(2,1)} collective-permute-done((bf16[640,1024]{1,0:T(8,128)(2,1)}, bf16[640,1024]{1,0:T(8,128)(2,1)}, u32[]{:S(2)}, u32[]{:S(2)}) %collective-permute-start.55) | collective-permute-done | bytes 1310752 | tf_op jit(solution)/shard_map/ppermute | solution.py:454
  1361.8 21.0 %shard_map.271 = (bf16[1024,256]{1,0:T(8,128)(2,1)S(1)}, bf16[1024,256]{1,0:T(8,128)(2,1)S(1)}, bf16[1024,256]{1,0:T(8,128)(2,1)S(1)}, f32[4,8,512]{2,1,0:T(8,128)S(1)}) custom-call(s32[2,4]{1,0:T(2,128)S(1)} %pad_add_fusion.span, s32[1,1024]{1,0:T(1,128)S(1)} %get-tuple-element.505.segr, s32[1024,1]{1,0:T(8,128)S(1)} %copy-done.71, ...), custom_call_target="tpu_custom_call" | custom-call | tf_op jit(solution)/shard_map/pallas_call | solution.py:265
  1419.4 20.2 %shard_map.275 = (bf16[1024,256]{1,0:T(8,128)(2,1)S(1)}, bf16[1024,256]{1,0:T(8,128)(2,1)S(1)}, bf16[1024,256]{1,0:T(8,128)(2,1)S(1)}, f32[4,8,512]{2,1,0:T(8,128)S(1)}) custom-call(s32[2,4]{1,0:T(2,128)S(1)} %pad_add_fusion.1.span, s32[1,1024]{1,0:T(1,128)S(1)} %get-tuple-element.509.segr, s32[1024,1]{1,0:T(8,128)S(1)} %copy-done.67, ...), custom_call_target="tpu_custom_call" | custom-call | tf_op jit(solution)/shard_map/pallas_call | solution.py:265
  1475.2 23.3 %collective-permute-done.66.other_ref = bf16[256,1024]{1,0:T(8,128)(2,1)} collective-permute-done((bf16[256,1024]{1,0:T(8,128)(2,1)S(1)}, bf16[256,1024]{1,0:T(8,128)(2,1)}, u32[]{:S(2)}, u32[]{:S(2)}) %collective-permute-start.66) | collective-permute-done | bytes 524320 | tf_op jit(solution)/shard_map/ppermute | solution.py:454
  1560.9 43.2 %collective-permute-done.77.other_ref = bf16[640,1024]{1,0:T(8,128)(2,1)} collective-permute-done((bf16[640,1024]{1,0:T(8,128)(2,1)}, bf16[640,1024]{1,0:T(8,128)(2,1)}, u32[]{:S(2)}, u32[]{:S(2)}) %collective-permute-start.77) | collective-permute-done | bytes 1310752 | tf_op jit(solution)/shard_map/ppermute | solution.py:454
  (1089 shorter events, 958.2 us)
Async XLA Ops:
  22.2 132.2 %reduce-scatter.17.cloned.1.call-start = ((), (), s32[]{:S(2)}) async-start(), calls=%async_computation.17 | async-start | bytes 2621440 | tf_op jit(solution)/shard_map/reduce_scatter | solution.py:313
  158.0 140.6 %all-gather.23.cloned.1.call-start = ((), (), s32[]{:S(2)}) async-start(), calls=%async_computation.22 | async-start | bytes 2621440 | tf_op jit(solution)/shard_map/all_gather | solution.py:309
  283.3 106.9 %reduce-scatter.23.cloned.1.call-start = ((), (), s32[]{:S(2)}) async-start(), calls=%async_computation.24 | async-start | bytes 2621440 | tf_op jit(solution)/shard_map/reduce_scatter | solution.py:313
  323.6 114.1 %all-gather.25.cloned.1.call-start = ((), (), s32[]{:S(2)}) async-start(), calls=%async_computation.23 | async-start | bytes 2621440 | tf_op jit(solution)/shard_map/all_gather | solution.py:309
  347.6 136.7 %all-gather.27.cloned.1.call-start = ((), (), s32[]{:S(2)}) async-start(), calls=%async_computation.26 | async-start | bytes 2621440 | tf_op jit(solution)/shard_map/all_gather | solution.py:309
  393.8 136.0 %reduce-scatter.25.cloned.1.call-start = ((), (), s32[]{:S(2)}) async-start(), calls=%async_computation.25 | async-start | bytes 2621440 | tf_op jit(solution)/shard_map/reduce_scatter | solution.py:313
  533.6 135.8 %all-gather.33.cloned.1.call-start = ((), (), s32[]{:S(2)}) async-start(), calls=%async_computation.30 | async-start | bytes 2621440 | tf_op jit(solution)/shard_map/all_gather | solution.py:309
  536.2 179.9 %all-gather.35.cloned.1.call-start = ((), (), s32[]{:S(2)}) async-start(), calls=%async_computation.31 | async-start | bytes 2621440 | tf_op jit(solution)/shard_map/all_gather | solution.py:309
  579.7 182.4 %all-gather.31.cloned.1.call-start = ((), (), s32[]{:S(2)}) async-start(), calls=%async_computation.29 | async-start | bytes 2621440 | tf_op jit(solution)/shard_map/all_gather | solution.py:309
  675.7 161.1 %reduce-scatter.31.cloned.1.call-start = ((), (), s32[]{:S(2)}) async-start(), calls=%async_computation.33 | async-start | bytes 2621440 | tf_op jit(solution)/shard_map/reduce_scatter | solution.py:313
  732.6 120.9 %reduce-scatter.29.cloned.1.call-start = ((), (), s32[]{:S(2)}) async-start(), calls=%async_computation.32 | async-start | bytes 2621440 | tf_op jit(solution)/shard_map/reduce_scatter | solution.py:313
  796.2 104.8 %all-gather.39.cloned.1.call-start = ((), (), s32[]{:S(2)}) async-start(), calls=%async_computation.35 | async-start | bytes 2621440 | tf_op jit(solution)/shard_map/all_gather | solution.py:309
  841.8 105.8 %all-gather.37.cloned.1.call-start = ((), (), s32[]{:S(2)}) async-start(), calls=%async_computation.34 | async-start | bytes 2621440 | tf_op jit(solution)/shard_map/all_gather | solution.py:309
  891.3 152.6 %reduce-scatter.35.cloned.1.call-start = ((), (), s32[]{:S(2)}) async-start(), calls=%async_computation.37 | async-start | bytes 2621440 | tf_op jit(solution)/shard_map/reduce_scatter | solution.py:313
  952.6 113.7 %reduce-scatter.33.cloned.1.call-start = ((), (), s32[]{:S(2)}) async-start(), calls=%async_computation.36 | async-start | bytes 2621440 | tf_op jit(solution)/shard_map/reduce_scatter | solution.py:313
  1048.2 114.7 %all-gather.41.cloned.1.call-start = ((), (), s32[]{:S(2)}) async-start(), calls=%async_computation.38 | async-start | bytes 2621440 | tf_op jit(solution)/shard_map/all_gather | solution.py:309
  1117.9 167.7 %reduce-scatter.39.cloned.1.call-start = ((), (), s32[]{:S(2)}) async-start(), calls=%async_computation.41 | async-start | bytes 2621440 | tf_op jit(solution)/shard_map/reduce_scatter | solution.py:313
  1147.7 146.1 %reduce-scatter.37.cloned.1.call-start = ((), (), s32[]{:S(2)}) async-start(), calls=%async_computation.40 | async-start | bytes 2621440 | tf_op jit(solution)/shard_map/reduce_scatter | solution.py:313
  1235.3 119.6 %all-gather.47.cloned.1.call-start = ((), (), s32[]{:S(2)}) async-start(), calls=%async_computation.43 | async-start | bytes 2621440 | tf_op jit(solution)/shard_map/all_gather | solution.py:309
  1290.0 104.9 %all-gather.45.cloned.1.call-start = ((), (), s32[]{:S(2)}) async-start(), calls=%async_computation.42 | async-start | bytes 2621440 | tf_op jit(solution)/shard_map/all_gather | solution.py:309
  1349.3 209.5 %reduce-scatter.45.cloned.1.call-start = ((), (), s32[]{:S(2)}) async-start(), calls=%async_computation.46 | async-start | bytes 2621440 | tf_op jit(solution)/shard_map/reduce_scatter | solution.py:313
  1399.9 222.6 %reduce-scatter.47.cloned.1.call-start = ((), (), s32[]{:S(2)}) async-start(), calls=%async_computation.47 | async-start | bytes 2621440 | tf_op jit(solution)/shard_map/reduce_scatter | solution.py:313
  1451.0 176.0 %reduce-scatter.41.cloned.1.call-start = ((), (), s32[]{:S(2)}) async-start(), calls=%async_computation.44 | async-start | bytes 2621440 | tf_op jit(solution)/shard_map/reduce_scatter | solution.py:313
  1463.1 166.0 %reduce-scatter.43.cloned.1.call-start = ((), (), s32[]{:S(2)}) async-start(), calls=%async_computation.45 | async-start | bytes 2621440 | tf_op jit(solution)/shard_map/reduce_scatter | solution.py:313
  (361 other events, 4813.1 us)
Sparse Core Ops, SparseCore 0:
  13.5 48.6 all-gather.16
  64.3 44.6 all-gather.18
  157.2 43.1 reduce-scatter.18
  202.4 45.2 all-gather.20
  253.7 44.7 all-gather.22
  347.0 43.1 reduce-scatter.22
  392.4 45.2 all-gather.24
  439.7 44.6 all-gather.26
  532.7 43.1 reduce-scatter.26
  578.0 45.2 all-gather.28
  624.8 44.6 all-gather.32
  671.5 44.5 all-gather.34
  717.5 44.6 all-gather.30
  810.3 43.1 reduce-scatter.28
  855.7 45.2 all-gather.38
  902.9 44.6 all-gather.36
  952.7 42.7 reduce-scatter.34
  1068.4 45.2 all-gather.42
  1118.0 44.7 all-gather.40
  1235.4 42.8 reduce-scatter.36
  1290.1 45.2 all-gather.46
  1349.4 45.4 all-gather.44
  1496.3 43.2 reduce-scatter.40
  1542.6 43.1 reduce-scatter.42
  (8 shorter events, 339.8 us)

commit v3 on v2

--- a/solution.py
+++ b/solution.py
@@ -245,7 +245,11 @@
     )(span, segr, segc, *parts, w)
 
 
-def attend_back(qkv, span, segr, segc, w, o, lse, go):
+def bwd_waiting(heads, waits, *refs):
+    bwd_kernel(heads, *refs[:10], *refs[10 + waits :])
+
+
+def attend_back(qkv, span, segr, segc, w, o, lse, go, after):
     heads = w.shape[0]
     width = heads * DH
     specs, parts = seen_specs(qkv, heads)
@@ -255,7 +259,7 @@
     grid = pltpu.PrefetchScalarGridSpec(
         num_scalar_prefetch=1,
         grid=(LEN // TILE,),
-        in_specs=specs + [tile, sums, tile],
+        in_specs=specs + [tile, sums, tile] + [pl.BlockSpec(memory_space=pl.ANY)] * len(after),
         out_specs=[tile, whole, whole, pl.BlockSpec((heads, 8, 2 * TILE), lambda i, s: (0, 0, 0))],
         scratch_shapes=[pltpu.VMEM((heads, NEAR, TILE, TILE), jnp.float32)] * 2
         + [pltpu.VMEM((LEN, width), jnp.float32)] * 2
@@ -263,12 +267,12 @@
     )
     flat = jax.ShapeDtypeStruct((LEN, width), jnp.bfloat16)
     return pl.pallas_call(
-        functools.partial(bwd_kernel, heads),
+        functools.partial(bwd_waiting, heads, len(after)),
         grid_spec=grid,
         out_shape=[flat, flat, flat, jax.ShapeDtypeStruct((heads, 8, 2 * TILE), jnp.float32)],
         compiler_params=pltpu.CompilerParams(vmem_limit_bytes=40 * 1024 * 1024),
         cost_estimate=pl.CostEstimate(flops=0, bytes_accessed=0, transcendentals=0),
-    )(span, segr, segc, *parts, w, o, lse, go)
+    )(span, segr, segc, *parts, w, o, lse, go, *after)
 
 
 THRESHOLDS = (12, 16, 23, 32, 46, 64, 91)
@@ -322,13 +326,13 @@
     return lax.dot_general(left, right, (dims, ((), ())), preferred_element_type=F32)
 
 
-def rows_kernel(dims, count, extras, finish, *refs):
+def rows_kernel(dims, count, extras, waits, finish, *refs):
     total = None
     for n in range(count):
         part = dot(refs[n][...], refs[count + n][...], dims)
         total = part if total is None else total + part
     inner = 2 * count + extras
-    finish(total, [ref[...] for ref in refs[2 * count : inner]], refs[inner:])
+    finish(total, [ref[...] for ref in refs[2 * count : inner]], refs[inner + waits :])
 
 
 def keep_rounded(total, extras, outs):
@@ -364,7 +368,7 @@
     outs[0][:, width:] = (grad * value).astype(BF)
 
 
-def rows_dot(parts, weights, dims, finish=keep_rounded, extras=(), widths=None):
+def rows_dot(parts, weights, dims, finish=keep_rounded, extras=(), widths=None, after=()):
     rows = parts[0].shape[0]
     if widths is None:
         widths = (weights[0].shape[1 - dims[1][0]],)
@@ -380,17 +384,212 @@
         return pl.BlockSpec(item.shape, lambda i: (0, 0))
 
     result = pl.pallas_call(
-        functools.partial(rows_kernel, dims, len(parts), len(extras), finish),
+        functools.partial(rows_kernel, dims, len(parts), len(extras), len(after), finish),
         grid=(rows // tall,),
         in_specs=[sliced(item) for item in parts]
         + [whole(item) for item in weights]
-        + [sliced(item) for item in extras],
+        + [sliced(item) for item in extras]
+        + [pl.BlockSpec(memory_space=pl.ANY)] * len(after),
         out_specs=[sliced(item) for item in outs],
         out_shape=outs,
         compiler_params=pltpu.CompilerParams(vmem_limit_bytes=40 * 1024 * 1024),
         cost_estimate=pl.CostEstimate(flops=0, bytes_accessed=0, transcendentals=0),
-    )(*parts, *weights, *extras)
+    )(*parts, *weights, *extras, *after)
     return result[0] if len(outs) == 1 else result
+
+
+def join_kernel(count, waits, *refs):
+    width = refs[0].shape[1]
+    for n in range(count):
+        refs[count + waits][:, n * width : (n + 1) * width] = refs[n][...]
+
+
+def rows_join(parts, after):
+    rows, width = parts[0].shape
+    count = len(parts)
+    if width % 128:
+        return jnp.concatenate(parts, 1)
+    tall = min(rows, ROWS)
+    return pl.pallas_call(
+        functools.partial(join_kernel, count, len(after)),
+        grid=(rows // tall,),
+        in_specs=[pl.BlockSpec((tall, width), lambda i: (i, 0))] * count
+        + [pl.BlockSpec(memory_space=pl.ANY)] * len(after),
+        out_specs=pl.BlockSpec((tall, count * width), lambda i: (i, 0)),
+        out_shape=jax.ShapeDtypeStruct((rows, count * width), BF),
+        compiler_params=pltpu.CompilerParams(vmem_limit_bytes=40 * 1024 * 1024),
+        cost_estimate=pl.CostEstimate(flops=0, bytes_accessed=0, transcendentals=0),
+    )(*parts, *after)
+
+
+def grads_kernel(groups, micros, waits, blocks, mine, *refs):
+    kept, sent = refs[-2:]
+    ours = (pl.program_id(0) // blocks) == mine[0]
+    rights = sum(groups)
+    each = len(groups) + rights
+    column = 0
+    for g, size in enumerate(groups):
+        turned = [refs[n * each + g][...].T for n in range(micros)]
+        first = len(groups) + sum(groups[:g])
+        for j in range(first, first + size):
+            total = sum(dot(turned[n], refs[n * each + j][...], NN) for n in range(micros))
+            total = total.astype(BF)
+            place = slice(column, column + total.shape[1])
+            column = place.stop
+
+            @pl.when(ours)
+            def _():
+                kept[:, place] = total
+
+            @pl.when(jnp.logical_not(ours))
+            def _():
+                sent[:, place] = total
+
+
+def half_spec(rows, width, blocks, ours):
+    def index(i, s):
+        which = s[0] if ours else 1 - s[0]
+        return jnp.clip(i - which * blocks, 0, blocks - 1), 0
+
+    return pl.BlockSpec((rows, width), index)
+
+
+def local_call(kernel, scalar, grid, in_specs, out_specs, out_shape, arrays, after):
+    spec = pltpu.PrefetchScalarGridSpec(
+        num_scalar_prefetch=1,
+        grid=grid,
+        in_specs=in_specs + [pl.BlockSpec(memory_space=pl.ANY)] * len(after),
+        out_specs=out_specs,
+    )
+    return pl.pallas_call(
+        kernel,
+        grid_spec=spec,
+        out_shape=out_shape,
+        compiler_params=pltpu.CompilerParams(vmem_limit_bytes=56 * 1024 * 1024),
+        cost_estimate=pl.CostEstimate(flops=0, bytes_accessed=0, transcendentals=0),
+    )(scalar.astype(jnp.int32).reshape(1), *arrays, *after)
+
+
+def packed_grads(items, mine, after):
+    groups = [len(rights) for _, rights in items[0]]
+    depth = items[0][0][0].shape[1]
+    if any(right.shape[1] % 128 for _, rights in items[0] for right in rights):
+        result = []
+        for g, size in enumerate(groups):
+            for j in range(size):
+                parts = [dot(item[g][0], item[g][1][j], TN) for item in items]
+                result.append(sum(parts).astype(BF))
+        total = jnp.concatenate(result, 1)
+        return take_half(total, mine), take_half(total, 1 - mine)
+    arrays, specs = [], []
+    for item in items:
+        for left, _ in item:
+            arrays.append(left)
+            specs.append(pl.BlockSpec((left.shape[0], ROWS), lambda i, s: (0, i)))
+        for _, rights in item:
+            arrays.extend(rights)
+            specs.extend(pl.BlockSpec(right.shape, lambda i, s: (0, 0)) for right in rights)
+    width = sum(right.shape[1] for _, rights in items[0] for right in rights)
+    blocks = depth // ROWS // 2
+    return local_call(
+        functools.partial(grads_kernel, groups, len(items), len(after), blocks),
+        mine,
+        (2 * blocks,),
+        specs,
+        [half_spec(ROWS, width, blocks, ours) for ours in (True, False)],
+        [jax.ShapeDtypeStruct((depth // 2, width), BF)] * 2,
+        arrays,
+        after,
+    )
+
+
+def halve_kernel(waits, blocks, mine, have, come, *refs):
+    kept, sent = refs[waits:]
+    total = (have[...].astype(F32) + come[...].astype(F32)).astype(BF)
+    ours = (pl.program_id(0) // blocks) == mine[0]
+
+    @pl.when(ours)
+    def _():
+        kept[...] = total
+
+    @pl.when(jnp.logical_not(ours))
+    def _():
+        sent[...] = total
+
+
+def halve(have, come, mine, after):
+    rows, width = have.shape
+    if width % 128 or rows % 64:
+        total = (have.astype(F32) + come.astype(F32)).astype(BF)
+        return take_half(total, mine), take_half(total, 1 - mine)
+    tall = rows // 4
+    return local_call(
+        functools.partial(halve_kernel, len(after), 2),
+        mine,
+        (4,),
+        [pl.BlockSpec((tall, width), lambda i, s: (i, 0))] * 2,
+        [half_spec(tall, width, 2, ours) for ours in (True, False)],
+        [jax.ShapeDtypeStruct((rows // 2, width), BF)] * 2,
+        [have, come],
+        after,
+    )
+
+
+def total_kernel(waits, mine, have, come, *refs):
+    refs[waits][...] = (have[...].astype(F32) + come[...].astype(F32)).astype(BF)
+
+
+def double_kernel(waits, blocks, mine, own, come, *refs):
+    ours = (pl.program_id(0) // blocks) == mine[0]
+
+    @pl.when(ours)
+    def _():
+        refs[waits][...] = own[...]
+
+    @pl.when(jnp.logical_not(ours))
+    def _():
+        refs[waits][...] = come[...]
+
+
+def arrive_kernel(*refs):
+    refs[-1][...] = jnp.zeros_like(refs[-1])
+
+
+def arrived(come, after):
+    return pl.pallas_call(
+        arrive_kernel,
+        in_specs=[pl.BlockSpec(memory_space=pl.ANY)] * (1 + len(after)),
+        out_shape=jax.ShapeDtypeStruct((8, 128), F32),
+        cost_estimate=pl.CostEstimate(flops=0, bytes_accessed=0, transcendentals=0),
+    )(come, *after)
+
+
+def total_of(have, come, mine, after):
+    rows, width = have.shape
+    if width % 128 or rows % 32:
+        return (have.astype(F32) + come.astype(F32)).astype(BF)
+    tall = rows // 2
+    spec = pl.BlockSpec((tall, width), lambda i, s: (i, 0))
+    shape = jax.ShapeDtypeStruct((rows, width), BF)
+    kernel = functools.partial(total_kernel, len(after))
+    return local_call(kernel, mine, (2,), [spec] * 2, spec, shape, [have, come], after)
+
+
+def double(own, come, mine, after):
+    rows, width = own.shape
+    if width % 128 or rows % 32:
+        return stack_half(own, come, mine)
+    tall = rows // 2
+    return local_call(
+        functools.partial(double_kernel, len(after), 2),
+        mine,
+        (4,),
+        [half_spec(tall, width, 2, ours) for ours in (True, False)],
+        pl.BlockSpec((tall, width), lambda i, s: (i, 0)),
+        jax.ShapeDtypeStruct((2 * rows, width), BF),
+        [own, come],
+        after,
+    )
 
 
 class Holder:
@@ -443,11 +642,6 @@
     return jnp.concatenate([item[n] for n in range(2) for item in cut], 1)
 
 
-def unpaired(values, count):
-    cut = jnp.split(values, 2 * count, axis=1)
-    return [jnp.concatenate((cut[n], cut[count + n]), 1) for n in range(count)]
-
-
 def link_swap(values, bits):
     size = lax.axis_size("dp")
     pairs = [(n * 2 + c, (n ^ bits[c]) * 2 + c) for n in range(size) for c in range(2)]
@@ -477,51 +671,70 @@
     return steps
 
 
-def settle_kernel(core_cut, count, place, own_ref, other_ref, *refs):
-    outs = refs[-count:]
-    half = pl.program_id(0)
+def settle_kernel(count, waits, blocks, place, own_ref, other_ref, *refs):
+    outs = refs[waits:]
+    half = pl.program_id(0) // blocks
 
     def store(values, core):
-        width = values.shape[1] // (2 * count)
-        for n in range(count):
-            for part in range(2):
+        width = outs[0].shape[2] // 2
+        tall = outs[count].shape[1] // 2
+        for part in range(2):
+            spot = part ^ core
+            for n in range(count):
                 start = (part * count + n) * width
-                spot = (part ^ core) * width
-                outs[n][0, :, spot : spot + width] = values[:, start : start + width].astype(F32)
+                cut = values[:, start : start + width].astype(F32)
+                outs[n][0, :, spot * width : (spot + 1) * width] = cut
+            start = 2 * count * width + part * tall
+            cut = values[:, start : start + tall].astype(F32)
+            outs[count][0, spot * tall : (spot + 1) * tall, :] = cut.T
 
     for source, ref in enumerate((own_ref, other_ref)):
-
-        @pl.when((half ^ place[0]) == source)
-        def _():
-            if not core_cut:
-                outs[0][0] = ref[...].astype(F32)
-            for core in range(2 if core_cut else 0):
-
-                @pl.when(place[1] == core)
-                def _():
-                    store(ref[...], core)
-
-
-def settle(own, other, flag, core, layer, base, core_cut, targets, shapes):
-    rows, width = own.shape
-    whole = pl.BlockSpec((rows, width), lambda i, s: (0, 0))
+        for core in range(2):
+
+            @pl.when(((half ^ place[0]) == source) & (place[1] == core))
+            def _():
+                store(ref[...], core)
+
+
+def settle(own, other, flag, core, layer, targets, shapes, after):
+    rows = 128
+    blocks = own.shape[0] // rows
+
+    def block(source):
+        def index(i, s):
+            return jnp.where(((i // blocks) ^ s[0]) == source, i % blocks, 0), 0
+
+        return pl.BlockSpec((rows, own.shape[1]), index)
+
+    count = len(shapes) - 1
     grid = pltpu.PrefetchScalarGridSpec(
         num_scalar_prefetch=1,
-        grid=(2,),
-        in_specs=[whole, whole] + [pl.BlockSpec(memory_space=pl.ANY)] * len(targets),
+        grid=(2 * blocks,),
+        in_specs=[block(0), block(1)]
+        + [pl.BlockSpec(memory_space=pl.ANY)] * (len(targets) + len(after)),
         out_specs=[
-            pl.BlockSpec((1, rows, item.shape[2]), lambda i, s: (layer, base + i, 0))
-            for item in shapes
-        ],
+            pl.BlockSpec((1, rows, item.shape[2]), lambda i, s: (layer, i, 0))
+            for item in shapes[:count]
+        ]
+        + [pl.BlockSpec((1, shapes[count].shape[1], rows), lambda i, s: (layer, 0, i))],
     )
     return pl.pallas_call(
-        functools.partial(settle_kernel, core_cut, len(shapes)),
+        functools.partial(settle_kernel, count, len(targets) + len(after), blocks),
         grid_spec=grid,
         out_shape=shapes,
         input_output_aliases={3 + n: n for n in range(len(targets))},
         compiler_params=pltpu.CompilerParams(vmem_limit_bytes=40 * 1024 * 1024),
         cost_estimate=pl.CostEstimate(flops=0, bytes_accessed=0, transcendentals=0),
-    )(jnp.stack((flag, core)).astype(jnp.int32), own, other, *targets)
+    )(jnp.stack((flag, core)).astype(jnp.int32), own, other, *targets, *after)
+
+
+def plain_settle(values, core, shapes):
+    count = len(shapes) - 1
+    width = shapes[0].shape[2] // 2
+    cut = [values[:, n * width : (n + 1) * width] for n in range(2 * count)]
+    done = [in_order(cut[n], cut[count + n], core, 1) for n in range(count)]
+    own, other = jnp.split(values[:, 2 * count * width :].T, 2, 0)
+    return done + [in_order(own, other, core, 0)]
 
 
 def axis_sum(values, axis):
@@ -540,9 +753,15 @@
     return values
 
 
+GROUPS = ("ffn", "attn")
+
+
 class Order:
     def __init__(self):
         self.last = None
+        self.dues = []
+        self.slow = []
+        self.gate = []
 
     def enter(self, *values):
         if self.last is None:
@@ -551,6 +770,17 @@
 
     def leave(self, value):
         self.last = value
+
+    def due(self, value):
+        self.dues.append(value)
+
+    def take(self):
+        dues, self.dues = self.dues, []
+        return dues
+
+    def take_slow(self):
+        dues, self.slow = self.slow, []
+        return dues
 
 
 def body(
@@ -581,21 +811,19 @@
     behind = near_table(True)
     steps = batch_steps(place, core)
     order = Order()
-    later = []
-    flows = []
+    later = {}
+    flows = {}
     summed = []
     ends = []
     results = {}
     tidy = hidden_dev % 128 == 0 and (heads_dev * DH) % 128 == 0
-    shapes = [
-        [jax.ShapeDtypeStruct(item.shape, F32) for item in group]
-        for group in (
-            (query_weight, key_weight, value_weight),
-            (gate_weight, up_weight),
-            (mixing_weight,),
-            (down_weight,),
+    shapes = {
+        kind: [jax.ShapeDtypeStruct(item.shape, F32) for item in group]
+        for kind, group in (
+            ("attn", (query_weight, key_weight, value_weight, mixing_weight)),
+            ("ffn", (gate_weight, up_weight, down_weight)),
         )
-    ]
+    }
     layers = []
     for layer in range(LAYERS):
         qkv = paired(query_weight[layer], key_weight[layer], value_weight[layer])
@@ -618,41 +846,33 @@
         have = acc[layer].get(name)
         acc[layer][name] = value if have is None else have + value
 
-    def batch_flow(layer, name, kept, start):
-        axis = 0 if name in ("down", "mix") else 1
-        rows = kept.shape[0]
-        for bits, mine in steps:
-            (kept,) = order.enter(kept)
-            send = take_half(kept, 1 - mine)
-            order.leave(send)
-            come = link_swap(send, bits)
-            yield
-            come, kept = order.enter(come, kept)
-            kept = (take_half(kept, mine).astype(F32) + come.astype(F32)).astype(BF)
-            order.leave(kept)
-        for bits, mine in reversed(steps[1:]):
-            come = link_swap(kept, bits)
-            yield
-            come, kept = order.enter(come, kept)
-            kept = stack_half(kept, come, mine)
-            order.leave(kept)
-        bits, mine = steps[0]
-        come = link_swap(kept, bits)
+    def batch_flow(layer, kind, kept, sent):
+        (bits1, mine1), (bits2, mine2) = steps
+        come = link_swap(sent, bits1)
         yield
-        come, kept = order.enter(come, kept)
+        kept, sent = halve(kept, come, mine2, order.gate)
+        order.due(kept)
+        come = link_swap(sent, bits2)
+        yield
+        kept = total_of(kept, come, mine2, order.gate)
+        order.due(kept)
+        come = link_swap(kept, bits2)
+        yield
+        kept = double(kept, come, mine2, order.gate)
+        order.due(kept)
+        come = link_swap(kept, bits1)
+        yield
+        order.due(arrived(come, order.gate))
+        yield
         if tidy:
-            group = ("qkv", "gu", "mix", "down").index(name)
-            flag = (mine ^ core) if axis == 0 else mine
-            base = start // (rows // 2)
-            targets = results.get(name, [])
-            results[name] = settle(
-                kept, come, flag, core, layer, base, axis == 1, targets, shapes[group]
+            targets = results.get(kind, [])
+            results[kind] = settle(
+                kept, come, mine1, core, layer, targets, shapes[kind], order.gate
             )
-            order.leave(results[name][0])
+            order.slow.append(results[kind][0])
         else:
-            kept = stack_half(kept, come, mine).astype(F32)
-            order.leave(kept)
-            results.setdefault((layer, name), []).append(kept)
+            kept = stack_half(kept, come, mine1).astype(F32)
+            results[layer, kind] = plain_settle(kept, core, shapes[kind])
 
     def small_flow():
         gain = jnp.stack([acc[n][name] for name in ("gain1", "gain2") for n in range(LAYERS)])
@@ -664,40 +884,29 @@
         )
         total = jnp.concatenate((gain.reshape(-1, 128), bias.reshape(-1, 128)), 0)
         for axis in ("gx", "gy", "dp"):
-            (total,) = order.enter(total)
             total = axis_sum(total, axis)
             yield
-            (total,) = order.enter(total)
-            order.leave(total)
         split = gain.size // 128
         summed.append(total[:split].reshape(gain.shape))
         summed.append(total[split:].reshape(bias.shape))
 
     def weight_grads():
-        for layer, name, left, right in later:
-            last = name in acc[layer]
-            have = acc[layer].get(name, (None, None))
-            left = order.enter(*left)
-            right = order.enter(*right)
-            both = [dot(a, b, TN) for a in left for b in right]
-            if last:
-                both = [a + b for a, b in zip(have, both)]
-            acc[layer][name] = both
-            order.leave(both[1])
-            if last:
-                axis = 0 if name in ("down", "mix") else 1
-                total = jnp.concatenate([item.astype(BF) for item in both], axis)
-                order.leave(total)
-                flow = batch_flow(layer, name, total, 0)
+        for (layer, kind), items in list(later.items()):
+            if len(items) == MICRO:
+                before = order.last
+                if kind == "ffn":
+                    advance("attn", layer + 1)
+                kept, sent = packed_grads(items, steps[0][1], [before, *order.take()])
+                order.leave(kept)
+                flow = batch_flow(layer, kind, kept, sent)
                 next(flow)
-                flows.append(flow)
-        later.clear()
-
-    def run_later():
-        for flow in list(flows):
-            if next(flow, "end") == "end":
-                flows.remove(flow)
-        weight_grads()
+                flows[kind, layer] = flow
+                del later[layer, kind]
+
+    def advance(kind, layer, gate=None):
+        order.gate = [order.last if gate is None else gate]
+        if (kind, layer) in flows and next(flows[kind, layer], "end") == "end":
+            del flows[kind, layer]
 
     def forward(micro):
         seg_all = segments[micro]
@@ -740,19 +949,19 @@
                 (2 * hidden_dev, hidden_dev),
             )
             active = [active, core_swap(active)]
-            out = rows_dot(active, w["down_half"], NN)
-            order.leave(out)
             saved.append(
                 (hidden, scale1, normed, qkv, lse, mixed, middle, scale2, dense)
                 + (gate_up, active)
             )
             if layer == LAYERS - 1:
                 break
+            out = rows_dot(active, w["down_half"], NN)
+            order.leave(out)
             out = token_reduce(out)
             yield
             (out,) = order.enter(out)
             hidden = middle + out
-        ends.append((middle, out, keep))
+        ends.append((middle, active, w["down_half"], keep))
         grad = cotangent[micro].astype(F32) * keep
         for layer in reversed(range(LAYERS)):
             w = layers[layer]
@@ -763,7 +972,11 @@
             grad_out = token_gather(grad_out)
             yield
             (grad_out,) = order.enter(grad_out)
-            come = core_swap(rows_dot([grad_out], w["down_half"][1:], NT))
+            if micro == 0:
+                advance("ffn", layer + 1)
+            advance("attn", layer + 1)
+            dues = order.take()
+            come = core_swap(rows_dot([grad_out], w["down_half"][1:], NT, after=dues))
             pair = rows_dot(
                 [grad_out],
                 w["down_half"][:1],
@@ -773,11 +986,11 @@
                 (2 * hidden_dev,),
             )
             pair = [pair, core_swap(pair)]
-            grad_dense = rows_dot(pair, w["gu_half"], NT)
+            grad_dense = rows_dot(pair, w["gu_half"], NT, after=order.take())
             order.leave(grad_dense)
             grad_dense = token_reduce(grad_dense)
-            later.append((layer, "down", active, [grad_out]))
-            later.append((layer, "gu", [dense], pair))
+            item = [(dense, pair), (grad_out, active)]
+            later.setdefault((layer, "ffn"), []).append(item)
             yield
             (grad_dense,) = order.enter(grad_dense)
             grad_norm, gain_part = norm_back(grad_dense, middle, scale2, w["gain2"])
@@ -788,27 +1001,23 @@
             grad_out = token_gather(grad_out)
             yield
             (grad_out,) = order.enter(grad_out)
-            come = core_swap(rows_dot([grad_out], w["mix_half"][1:], NT))
+            if micro == 0:
+                advance("ffn", layer)
+            dues = order.take()
+            come = core_swap(rows_dot([grad_out], w["mix_half"][1:], NT, after=dues))
             grad_mixed = rows_dot([grad_out], w["mix_half"][:1], NT, add_rounded, [come])
-            if layer == 0 and micro == MICRO - 1:
-                order.leave(grad_mixed)
-                later.append((layer, "mix", mixed, [grad_out]))
-                weight_grads()
-                (grad_mixed,) = order.enter(grad_mixed)
-            gq, gk, gv, gb = attend_back(qkv, *views, w["bias"], mixed[0], lse, grad_mixed)
+            gq, gk, gv, gb = attend_back(
+                qkv, *views, w["bias"], mixed[0], lse, grad_mixed, order.take()
+            )
             add(layer, "bias", gb)
-            triple = jnp.concatenate((gq, gk, gv), 1)
+            advance("ffn", layer, gq)
+            triple = rows_join((gq, gk, gv), order.take())
             triple = [triple, core_swap(triple)]
             grad_normed = rows_dot(triple, w["qkv_half"], NT)
             order.leave(grad_normed)
             grad_normed = token_reduce(grad_normed)
-            if layer == 0 and micro == MICRO - 1:
-                for n, (middle, out, keep) in enumerate(ends):
-                    (out,) = order.enter(out)
-                    outputs[n] = (middle + token_reduce(out)) * keep
-            if layer > 0 or micro < MICRO - 1:
-                later.append((layer, "mix", mixed, [grad_out]))
-            later.append((layer, "qkv", [normed], triple))
+            item = [(normed, triple), (grad_out, mixed)]
+            later.setdefault((layer, "attn"), []).append(item)
             yield
             (grad_normed,) = order.enter(grad_normed)
             grad_norm, gain_part = norm_back(grad_normed, hidden, scale1, w["gain1"])
@@ -824,28 +1033,38 @@
         for flow in list(live):
             if next(flow, "end") == "end":
                 live.remove(flow)
-        run_later()
-    flow = small_flow()
-    next(flow)
-    flows.append(flow)
-    while flows:
-        run_later()
+        weight_grads()
+    advance("ffn", 0)
+    after = [order.last, *order.take()]
+    last = [rows_dot(active, down, NN, after=after) for _, active, down, _ in ends]
+    after = last[-1]
+    last = jnp.split(token_reduce(jnp.concatenate(last, 1)), MICRO, 1)
+    for n, (middle, _, _, keep) in enumerate(ends):
+        outputs[n] = (middle + last[n]) * keep
+    small = small_flow()
+    next(small)
+    for kind, layer in (("ffn", 1), ("ffn", 0), (None, 0)):
+        advance("attn", 0, after)
+        after = order.take()[-1]
+        next(small, None)
+        if kind is not None:
+            advance(kind, layer, after)
+            after = (order.take_slow() or [after])[-1]
+    advance("attn", 1, after)
+    order.take()
+    advance("attn", 1, after)
+    after = (order.take_slow() or [after])[-1]
+    advance("attn", 0, after)
+    after = order.take()[-1]
+    advance("attn", 0, after)
+    next(small, None)
     gain, bias = summed
     if not tidy:
-        for name, count in (("qkv", 3), ("gu", 2), ("mix", 1), ("down", 1)):
-            axis = 0 if count == 1 else 1
-            whole = []
-            for layer in range(LAYERS):
-                both = jnp.split(jnp.concatenate(results[layer, name], 0), 2, axis)
-                ordered = in_order(*both, core, axis)
-                whole.append([ordered] if count == 1 else unpaired(ordered, count))
-            results[name] = [
-                jnp.stack([whole[layer][n] for layer in range(LAYERS)]) for n in range(count)
-            ]
-    grad_query, grad_key, grad_value = results["qkv"]
-    grad_gate, grad_up = results["gu"]
-    (grad_mixing,) = results["mix"]
-    (grad_down,) = results["down"]
+        for kind in GROUPS:
+            both = [results[layer, kind] for layer in range(LAYERS)]
+            results[kind] = [jnp.stack(item) for item in zip(*both)]
+    grad_query, grad_key, grad_value, grad_mixing = results["attn"]
+    grad_gate, grad_up, grad_down = results["ffn"]
     return (
         jnp.stack(outputs),
         jnp.stack(grads),

time: 1690 us -> 1580 us (0.935)
  Pallas kernels: 378 us -> 523 us
  matrix products: 92 us -> 0.91 us
  waiting for transfers between devices: 794 us -> 739 us
  other arithmetic: 122 us -> 69 us
  local copies, waits for them, and re-layouts: 217 us -> 182 us
  starting transfers between devices: 52 us -> 32.2 us
    pallas_call x12 -> x31, Pallas kernels: 119 us -> 282 us  [the longest x16 161 us: local_call(): pl.pallas_call(kernel, grid_spec=spec, out_shape=out_shape, compiler_para...]
    ppermute x32 -> x16, waiting for transfers between devices: 238 us -> 135 us  [link_swap(): return lax.ppermute(values, ('dp', 'gx'), pairs)]
    dot_general x32 -> x0, matrix products: 91.1 us -> none  [dot(): lax.dot_general(left, right, (dims, ((), ())), preferred_element_type=F32)]
    convert_element_type x18 -> x0, other arithmetic: 34.5 us -> none  [the longest x16 33.5 us: batch_flow(): kept = (take_half(kept, mine).astype(F32) + come.astype(F32)).astype(BF)]
    select_n x8 -> x0, other arithmetic: 21.8 us -> none  [stack_half(): jnp.where(which == 0, jnp.concatenate((own, other), 0), jnp.concatenate((...]
    all_gather x16, waiting for transfers between devices: 304 us -> 326 us  [token_gather(): return lax.all_gather(values, 'gy', axis=0, tiled=True)]
    ppermute x32 -> x16, starting transfers between devices: 34.3 us -> 14.1 us  [link_swap(): return lax.ppermute(values, ('dp', 'gx'), pairs)]
    dynamic_slice x16 -> x0, local copies, waits for them, and re-layouts: 18.6 us -> none  [take_half(): return lax.dynamic_slice_in_dim(values, which * rows, rows, 0)]
  transfers between devices with their start and end apart: 119 -> 102, of which waited for: 71 -> 74; matrix products, arithmetic and copies ran while one was open for 17% -> 7% of each run, Pallas kernels for 22% -> 33%
where the time goes in v3:
time: 1580 us; the launch traced here: 1560 us
  waiting for transfers between devices  739 us (47%)
  Pallas kernels  523 us (33%)
  local copies, waits for them, and re-layouts  182 us (12%)
  other arithmetic  69 us (4%)
  starting transfers between devices  32.2 us (2%)
  between operations  17.4 us (1%)
    all_gather x16, waiting for transfers between devices, token_gather(): return lax.all_gather(values, 'gy', axis=0, tiled=True)  326 us
    reduce_scatter x15, waiting for transfers between devices, token_reduce(): lax.psum_scatter(values, 'gy', scatter_dimension=0, tiled=True).astype(F32)  177 us
    pallas_call x48, Pallas kernels, rows_dot(): pl.pallas_call(functools.partial(rows_kernel, dims, len(parts), len(extra...  167 us
    pallas_call x16, Pallas kernels, local_call(): pl.pallas_call(kernel, grid_spec=spec, out_shape=out_shape, compiler_para...  161 us
    unnamed x464, local copies, waits for them, and re-layouts  137 us
    ppermute x16, waiting for transfers between devices, link_swap(): return lax.ppermute(values, ('dp', 'gx'), pairs)  135 us
    ppermute x48, waiting for transfers between devices, core_swap(): return lax.ppermute(values, 'gx', [(0, 1), (1, 0)])  85.7 us
    pallas_call x4, Pallas kernels, attend_back(): pl.pallas_call(functools.partial(bwd_waiting, heads, len(after)), grid_sp...  81.7 us
  transfers between devices with their start and end apart: 102, of which 74 were waited for; matrix products, arithmetic and copies ran while one was open for 7% of the time, Pallas kernels for 33%

profile of v3, /device:TPU:0, one launch (start us, length us, event | category | flops | bytes accessed | tf_op | source)
XLA Modules:
  0.0 1564.1 jit_solution(16077846001646505487)
XLA Ops:
  28.1 34.0 %all-gather.17.cloned.1.call-done.refs_0_ = bf16[1024,1024]{1,0:T(8,128)(2,1)} async-done(((bf16[256,1024]{1,0:T(8,128)(2,1)}), bf16[1024,1024]{1,0:T(8,128)(2,1)}) %all-gather.17.cloned.1.call-update) | async-done | bytes 2097168 | tf_op jit(solution)/shard_map/all_gather | solution.py:313
  71.9 19.2 %shard_map.222 = (bf16[1024,256]{1,0:T(8,128)(2,1)}, f32[8,1024]{1,0:T(8,128)S(1)}) custom-call(s32[2,4]{1,0:T(2,128)S(1)} %pad_add_fusion.span.refs_0_, s32[1,1024]{1,0:T(1,128)S(1)} %get-tuple-element.305.segr.refs_1_, s32[1024,1]{1,0:T(8,128)S(1)} %compare_select_fusion.1.segc.refs_2_, ...), custom_call_target="tpu_custom_call" | custom-call | tf_op jit(solution)/shard_map/pallas_call | solution.py:236
  170.3 30.2 %reduce-scatter.18.cloned.1.call-done = bf16[256,1024]{1,0:T(8,128)(2,1)} async-done(((bf16[1024,1024]{1,0:T(8,128)(2,1)}), bf16[256,1024]{1,0:T(8,128)(2,1)}) %reduce-scatter.18.cloned.1.call-update) | async-done | bytes 524304 | tf_op jit(solution)/shard_map/reduce_scatter | solution.py:317
  207.7 40.0 %all-gather.21.cloned.1.call-done.refs_0_ = bf16[1024,1024]{1,0:T(8,128)(2,1)} async-done(((bf16[256,1024]{1,0:T(8,128)(2,1)}), bf16[1024,1024]{1,0:T(8,128)(2,1)}) %all-gather.21.cloned.1.call-update) | async-done | bytes 2097168 | tf_op jit(solution)/shard_map/all_gather | solution.py:313
  323.7 20.4 %reduce-scatter.20.cloned.1.call-done = bf16[256,1024]{1,0:T(8,128)(2,1)} async-done(((bf16[1024,1024]{1,0:T(8,128)(2,1)}), bf16[256,1024]{1,0:T(8,128)(2,1)}) %reduce-scatter.20.cloned.1.call-update) | async-done | bytes 524304 | tf_op jit(solution)/shard_map/reduce_scatter | solution.py:317
  347.7 42.6 %reduce-scatter.22.cloned.1.call-done = bf16[256,1024]{1,0:T(8,128)(2,1)} async-done(((bf16[1024,1024]{1,0:T(8,128)(2,1)}), bf16[256,1024]{1,0:T(8,128)(2,1)}) %reduce-scatter.22.cloned.1.call-update) | async-done | bytes 524304 | tf_op jit(solution)/shard_map/reduce_scatter | solution.py:317
  400.1 37.6 %all-gather.25.cloned.1.call-done.refs_0_ = bf16[1024,1024]{1,0:T(8,128)(2,1)} async-done(((bf16[256,1024]{1,0:T(8,128)(2,1)}), bf16[1024,1024]{1,0:T(8,128)(2,1)}) %all-gather.25.cloned.1.call-update) | async-done | bytes 2097168 | tf_op jit(solution)/shard_map/all_gather | solution.py:313
  494.2 18.5 %shard_map.240 = (bf16[1024,256]{1,0:T(8,128)(2,1)S(1)}, f32[8,1024]{1,0:T(8,128)S(1)}) custom-call(s32[2,4]{1,0:T(2,128)S(1)} %pad_add_fusion.1.span.refs_0_, s32[1,1024]{1,0:T(1,128)S(1)} %get-tuple-element.309.segr.refs_1_, s32[1024,1]{1,0:T(8,128)S(1)} %copy-done.91, bf16[1024,768]{1,0:T(8,128)(2,1)S(1)} %shard_map.239.q_ref.k_ref.v_ref.refs_3_.refs_4_.refs_5_, ...), custom_call_target="tpu_custom_call" | custom-call | tf_op jit(solution)/shard_map/pallas_call | solution.py:236
  537.2 38.6 %reduce-scatter.26.cloned.1.call-done = bf16[256,1024]{1,0:T(8,128)(2,1)} async-done(((bf16[1024,1024]{1,0:T(8,128)(2,1)}), bf16[256,1024]{1,0:T(8,128)(2,1)}) %reduce-scatter.26.cloned.1.call-update) | async-done | bytes 524304 | tf_op jit(solution)/shard_map/reduce_scatter | solution.py:317
  586.6 36.6 %all-gather.29.cloned.1.call-done.refs_0_ = bf16[1024,1024]{1,0:T(8,128)(2,1)} async-done(((bf16[256,1024]{1,0:T(8,128)(2,1)}), bf16[1024,1024]{1,0:T(8,128)(2,1)}) %all-gather.29.cloned.1.call-update) | async-done | bytes 2097168 | tf_op jit(solution)/shard_map/all_gather | solution.py:313
  632.6 37.4 %all-gather.31.cloned.1.call-done.refs_0_.refs_1_ = bf16[1024,1024]{1,0:T(8,128)(2,1)} async-done(((bf16[256,1024]{1,0:T(8,128)(2,1)}), bf16[1024,1024]{1,0:T(8,128)(2,1)}) %all-gather.31.cloned.1.call-update) | async-done | bytes 2097168 | tf_op jit(solution)/shard_map/all_gather | solution.py:313
  691.9 24.7 %all-gather.33.cloned.1.call-done.refs_0_.refs_6_ = bf16[1024,1024]{1,0:T(8,128)(2,1)} async-done(((bf16[256,1024]{1,0:T(8,128)(2,1)}), bf16[1024,1024]{1,0:T(8,128)(2,1)}) %all-gather.33.cloned.1.call-update) | async-done | bytes 2097168 | tf_op jit(solution)/shard_map/all_gather | solution.py:313
  733.2 29.5 %all-gather.35.cloned.1.call-done.refs_0_.refs_7_ = bf16[1024,1024]{1,0:T(8,128)(2,1)} async-done(((bf16[256,1024]{1,0:T(8,128)(2,1)}), bf16[1024,1024]{1,0:T(8,128)(2,1)}) %all-gather.35.cloned.1.call-update) | async-done | bytes 2097168 | tf_op jit(solution)/shard_map/all_gather | solution.py:313
  799.9 31.8 %shard_map.252 = (bf16[512,3840]{1,0:T(8,128)(2,1)}, bf16[512,3840]{1,0:T(8,128)(2,1)}) custom-call(s32[1]{0:T(128)} %bitcast.40.mine, bf16[1024,1024]{1,0:T(8,128)(2,1)} %all-gather.29.cloned.1.call-done.refs_0_, bf16[1024,1024]{1,0:T(8,128)(2,1)} %all-gather.31.cloned.1.call-done.refs_0_.refs_1_, bf16[1024,1280]{1,0:T(8,128)(2,1)} %shard_map.245.refs_0_.refs_2_, ...), custom_call_target="tpu_custom_call" | custom-call | tf_op jit(solution)/shard_map/pallas_call | solution.py:464
  910.4 20.2 %shard_map.256 = (bf16[1024,256]{1,0:T(8,128)(2,1)S(1)}, bf16[1024,256]{1,0:T(8,128)(2,1)S(1)}, bf16[1024,256]{1,0:T(8,128)(2,1)S(1)}, f32[4,8,512]{2,1,0:T(8,128)S(1)}) custom-call(s32[2,4]{1,0:T(2,128)S(1)} %pad_add_fusion.span.refs_0_, s32[1,1024]{1,0:T(1,128)S(1)} %get-tuple-element.305.segr.refs_1_, s32[1024,1]{1,0:T(8,128)S(1)} %copy-done.88, ...), custom_call_target="tpu_custom_call" | custom-call | tf_op jit(solution)/shard_map/pallas_call | solution.py:269
  957.0 20.2 %shard_map.262 = (bf16[1024,256]{1,0:T(8,128)(2,1)S(1)}, bf16[1024,256]{1,0:T(8,128)(2,1)S(1)}, bf16[1024,256]{1,0:T(8,128)(2,1)S(1)}, f32[4,8,512]{2,1,0:T(8,128)S(1)}) custom-call(s32[2,4]{1,0:T(2,128)S(1)} %pad_add_fusion.1.span.refs_0_, s32[1,1024]{1,0:T(1,128)S(1)} %get-tuple-element.309.segr.refs_1_, s32[1024,1]{1,0:T(8,128)S(1)} %copy-done.92, ...), custom_call_target="tpu_custom_call" | custom-call | tf_op jit(solution)/shard_map/pallas_call | solution.py:269
  995.7 21.9 %shard_map.266 = (bf16[512,2048]{1,0:T(8,128)(2,1)}, bf16[512,2048]{1,0:T(8,128)(2,1)}) custom-call(s32[1]{0:T(128)} %bitcast.40.mine, bf16[1024,1024]{1,0:T(8,128)(2,1)} %all-gather.25.cloned.1.call-done.refs_0_, bf16[1024,1024]{1,0:T(8,128)(2,1)} %all-gather.37.cloned.1.call-done.refs_0_.refs_1_, bf16[1024,768]{1,0:T(8,128)(2,1)} %copy-done.85, ...), custom_call_target="tpu_custom_call" | custom-call | tf_op jit(solution)/shard_map/pallas_call | solution.py:464
  1044.5 19.7 %collective-permute-done.40.come = bf16[512,2048]{1,0:T(8,128)(2,1)} collective-permute-done((bf16[512,2048]{1,0:T(8,128)(2,1)}, bf16[512,2048]{1,0:T(8,128)(2,1)}, u32[]{:S(2)}, u32[]{:S(2)}) %collective-permute-start.40) | collective-permute-done | bytes 2097184 | tf_op jit(solution)/shard_map/ppermute | solution.py:648
  1186.9 32.2 %shard_map.277 = (bf16[512,3840]{1,0:T(8,128)(2,1)}, bf16[512,3840]{1,0:T(8,128)(2,1)}) custom-call(s32[1]{0:T(128)} %bitcast.40.mine, bf16[1024,1024]{1,0:T(8,128)(2,1)} %all-gather.21.cloned.1.call-done.refs_0_, bf16[1024,1024]{1,0:T(8,128)(2,1)} %all-gather.41.cloned.1.call-done.refs_0_.refs_1_, bf16[1024,1280]{1,0:T(8,128)(2,1)} %copy-done.44, ...), custom_call_target="tpu_custom_call" | custom-call | tf_op jit(solution)/shard_map/pallas_call | solution.py:464
  1233.3 31.8 %collective-permute-done.49.come = bf16[512,3840]{1,0:T(8,128)(2,1)} collective-permute-done((bf16[512,3840]{1,0:T(8,128)(2,1)}, bf16[512,3840]{1,0:T(8,128)(2,1)}, u32[]{:S(2)}, u32[]{:S(2)}) %collective-permute-start.49) | collective-permute-done | bytes 3932192 | tf_op jit(solution)/shard_map/ppermute | solution.py:648
  1283.7 21.0 %shard_map.281 = (bf16[1024,256]{1,0:T(8,128)(2,1)S(1)}, bf16[1024,256]{1,0:T(8,128)(2,1)S(1)}, bf16[1024,256]{1,0:T(8,128)(2,1)S(1)}, f32[4,8,512]{2,1,0:T(8,128)S(1)}) custom-call(s32[2,4]{1,0:T(2,128)S(1)} %pad_add_fusion.span.refs_0_, s32[1,1024]{1,0:T(1,128)S(1)} %get-tuple-element.305.segr.refs_1_, s32[1024,1]{1,0:T(8,128)S(1)} %copy-done.89, ...), custom_call_target="tpu_custom_call" | custom-call | tf_op jit(solution)/shard_map/pallas_call | solution.py:269
  1332.5 20.2 %shard_map.287 = (bf16[1024,256]{1,0:T(8,128)(2,1)S(1)}, bf16[1024,256]{1,0:T(8,128)(2,1)S(1)}, bf16[1024,256]{1,0:T(8,128)(2,1)S(1)}, f32[4,8,512]{2,1,0:T(8,128)S(1)}) custom-call(s32[2,4]{1,0:T(2,128)S(1)} %pad_add_fusion.1.span.refs_0_, s32[1,1024]{1,0:T(1,128)S(1)} %get-tuple-element.309.segr.refs_1_, s32[1024,1]{1,0:T(8,128)S(1)} %copy-done.93, ...), custom_call_target="tpu_custom_call" | custom-call | tf_op jit(solution)/shard_map/pallas_call | solution.py:269
  1370.4 21.9 %shard_map.291 = (bf16[512,2048]{1,0:T(8,128)(2,1)}, bf16[512,2048]{1,0:T(8,128)(2,1)}) custom-call(s32[1]{0:T(128)} %bitcast.40.mine, bf16[1024,1024]{1,0:T(8,128)(2,1)} %all-gather.17.cloned.1.call-done.refs_0_, bf16[1024,1024]{1,0:T(8,128)(2,1)} %all-gather.45.cloned.1.call-done.refs_0_.refs_1_, bf16[1024,768]{1,0:T(8,128)(2,1)} %copy-done.84, ...), custom_call_target="tpu_custom_call" | custom-call | tf_op jit(solution)/shard_map/pallas_call | solution.py:464
  1424.7 26.0 %collective-permute-done.66.come = bf16[512,2048]{1,0:T(8,128)(2,1)S(1)} collective-permute-done((bf16[512,2048]{1,0:T(8,128)(2,1)S(1)}, bf16[512,2048]{1,0:T(8,128)(2,1)S(1)}, u32[]{:S(2)}, u32[]{:S(2)}) %collective-permute-start.66) | collective-permute-done | bytes 2097184 | tf_op jit(solution)/shard_map/ppermute | solution.py:648
  (900 shorter events, 870.5 us)
Async XLA Ops:
  23.4 131.0 %reduce-scatter.16.cloned.1.call-start = ((), (), s32[]{:S(2)}) async-start(), calls=%async_computation.16 | async-start | bytes 2621440 | tf_op jit(solution)/shard_map/reduce_scatter | solution.py:317
  146.5 101.2 %all-gather.21.cloned.1.call-start = ((), (), s32[]{:S(2)}) async-start(), calls=%async_computation.18 | async-start | bytes 2621440 | tf_op jit(solution)/shard_map/all_gather | solution.py:313
  158.0 140.6 %all-gather.23.cloned.1.call-start = ((), (), s32[]{:S(2)}) async-start(), calls=%async_computation.21 | async-start | bytes 2621440 | tf_op jit(solution)/shard_map/all_gather | solution.py:313
  283.3 106.9 %reduce-scatter.22.cloned.1.call-start = ((), (), s32[]{:S(2)}) async-start(), calls=%async_computation.23 | async-start | bytes 2621440 | tf_op jit(solution)/shard_map/reduce_scatter | solution.py:317
  323.6 114.1 %all-gather.25.cloned.1.call-start = ((), (), s32[]{:S(2)}) async-start(), calls=%async_computation.22 | async-start | bytes 2621440 | tf_op jit(solution)/shard_map/all_gather | solution.py:313
  347.6 136.8 %all-gather.27.cloned.1.call-start = ((), (), s32[]{:S(2)}) async-start(), calls=%async_computation.25 | async-start | bytes 2621440 | tf_op jit(solution)/shard_map/all_gather | solution.py:313
  393.8 135.9 %reduce-scatter.24.cloned.1.call-start = ((), (), s32[]{:S(2)}) async-start(), calls=%async_computation.24 | async-start | bytes 2621440 | tf_op jit(solution)/shard_map/reduce_scatter | solution.py:317
  473.6 102.2 %reduce-scatter.26.cloned.1.call-start = ((), (), s32[]{:S(2)}) async-start(), calls=%async_computation.27 | async-start | bytes 2621440 | tf_op jit(solution)/shard_map/reduce_scatter | solution.py:317
  519.5 103.7 %all-gather.29.cloned.1.call-start = ((), (), s32[]{:S(2)}) async-start(), calls=%async_computation.26 | async-start | bytes 2621440 | tf_op jit(solution)/shard_map/all_gather | solution.py:313
  534.6 135.4 %all-gather.31.cloned.1.call-start = ((), (), s32[]{:S(2)}) async-start(), calls=%async_computation.28 | async-start | bytes 2621440 | tf_op jit(solution)/shard_map/all_gather | solution.py:313
  537.1 179.5 %all-gather.33.cloned.1.call-start = ((), (), s32[]{:S(2)}) async-start(), calls=%async_computation.30 | async-start | bytes 2621440 | tf_op jit(solution)/shard_map/all_gather | solution.py:313
  580.6 182.1 %all-gather.35.cloned.1.call-start = ((), (), s32[]{:S(2)}) async-start(), calls=%async_computation.31 | async-start | bytes 2621440 | tf_op jit(solution)/shard_map/all_gather | solution.py:313
  676.2 156.9 %reduce-scatter.28.cloned.1.call-start = ((), (), s32[]{:S(2)}) async-start(), calls=%async_computation.29 | async-start | bytes 2621440 | tf_op jit(solution)/shard_map/reduce_scatter | solution.py:317
  733.2 120.9 %reduce-scatter.30.cloned.1.call-start = ((), (), s32[]{:S(2)}) async-start(), calls=%async_computation.33 | async-start | bytes 2621440 | tf_op jit(solution)/shard_map/reduce_scatter | solution.py:317
  794.0 107.4 %all-gather.37.cloned.1.call-start = ((), (), s32[]{:S(2)}) async-start(), calls=%async_computation.32 | async-start | bytes 2621440 | tf_op jit(solution)/shard_map/all_gather | solution.py:313
  838.7 111.0 %all-gather.39.cloned.1.call-start = ((), (), s32[]{:S(2)}) async-start(), calls=%async_computation.35 | async-start | bytes 2621440 | tf_op jit(solution)/shard_map/all_gather | solution.py:313
  885.5 132.1 %reduce-scatter.32.cloned.1.call-start = ((), (), s32[]{:S(2)}) async-start(), calls=%async_computation.34 | async-start | bytes 2621440 | tf_op jit(solution)/shard_map/reduce_scatter | solution.py:317
  1022.0 115.1 %all-gather.43.cloned.1.call-start = ((), (), s32[]{:S(2)}) async-start(), calls=%async_computation.39 | async-start | bytes 2621440 | tf_op jit(solution)/shard_map/all_gather | solution.py:313
  1092.1 128.4 %reduce-scatter.36.cloned.1.call-start = ((), (), s32[]{:S(2)}) async-start(), calls=%async_computation.38 | async-start | bytes 2621440 | tf_op jit(solution)/shard_map/reduce_scatter | solution.py:317
  1121.8 106.7 %reduce-scatter.38.cloned.1.call-start = ((), (), s32[]{:S(2)}) async-start(), calls=%async_computation.41 | async-start | bytes 2621440 | tf_op jit(solution)/shard_map/reduce_scatter | solution.py:317
  1166.2 109.6 %all-gather.45.cloned.1.call-start = ((), (), s32[]{:S(2)}) async-start(), calls=%async_computation.40 | async-start | bytes 2621440 | tf_op jit(solution)/shard_map/all_gather | solution.py:313
  1273.0 203.4 %reduce-scatter.42.cloned.1.call-start = ((), (), s32[]{:S(2)}) async-start(), calls=%async_computation.44 | async-start | bytes 2621440 | tf_op jit(solution)/shard_map/reduce_scatter | solution.py:317
  1323.2 165.6 %reduce-scatter.44.cloned.1.call-start = ((), (), s32[]{:S(2)}) async-start(), calls=%async_computation.45 | async-start | bytes 2621440 | tf_op jit(solution)/shard_map/reduce_scatter | solution.py:317
  1370.1 183.2 %reduce-scatter.40.cloned.1.call-start = ((), (), s32[]{:S(2)}) async-start(), calls=%async_computation.43 | async-start | bytes 5242880 | tf_op jit(solution)/shard_map/reduce_scatter | solution.py:317
  (305 other events, 3450.0 us)
Sparse Core Ops, SparseCore 0:
  13.5 48.6 all-gather.16
  64.3 44.6 all-gather.18
  157.2 43.1 reduce-scatter.17
  202.4 45.2 all-gather.20
  253.8 44.7 all-gather.22
  347.0 43.1 reduce-scatter.21
  392.4 45.2 all-gather.24
  439.7 44.6 all-gather.26
  532.6 43.1 reduce-scatter.25
  577.9 45.2 all-gather.28
  625.2 44.6 all-gather.30
  671.9 44.6 all-gather.32
  718.0 44.6 all-gather.34
  810.8 43.1 reduce-scatter.29
  856.2 45.2 all-gather.36
  902.9 44.6 all-gather.38
  995.7 43.4 reduce-scatter.33
  1041.3 45.3 all-gather.40
  1092.2 44.7 all-gather.42
  1185.4 43.1 reduce-scatter.37
  1230.6 45.2 all-gather.44
  1278.0 44.6 all-gather.46
  1370.9 43.2 reduce-scatter.43
  1423.3 73.7 reduce-scatter.39
  (7 shorter events, 297.0 us)

commit v4 on v3

--- a/solution.py
+++ b/solution.py
@@ -1003,6 +1003,8 @@
             (grad_out,) = order.enter(grad_out)
             if micro == 0:
                 advance("ffn", layer)
+            elif layer == 0:
+                advance("ffn", layer, grad_out)
             dues = order.take()
             come = core_swap(rows_dot([grad_out], w["mix_half"][1:], NT, after=dues))
             grad_mixed = rows_dot([grad_out], w["mix_half"][:1], NT, add_rounded, [come])
@@ -1034,7 +1036,6 @@
             if next(flow, "end") == "end":
                 live.remove(flow)
         weight_grads()
-    advance("ffn", 0)
     after = [order.last, *order.take()]
     last = [rows_dot(active, down, NN, after=after) for _, active, down, _ in ends]
     after = last[-1]

time: 1580 us -> 1590 us (level)
    unnamed x464 -> x474, local copies, waits for them, and re-layouts: 137 us -> 143 us
  transfers between devices with their start and end apart: 102 -> 102, of which waited for: 74 -> 72; matrix products, arithmetic and copies ran while one was open for 7% -> 7% of each run, Pallas kernels for 33% -> 32%
where the time goes in v4:
time: 1590 us; the launch traced here: 1570 us
  waiting for transfers between devices  747 us (47%)
  Pallas kernels  513 us (32%)
  local copies, waits for them, and re-layouts  188 us (12%)
  other arithmetic  66.6 us (4%)
  starting transfers between devices  41.9 us (3%)
  between operations  17.5 us (1%)
    all_gather x16, waiting for transfers between devices, token_gather(): return lax.all_gather(values, 'gy', axis=0, tiled=True)  326 us
    reduce_scatter x15, waiting for transfers between devices, token_reduce(): lax.psum_scatter(values, 'gy', scatter_dimension=0, tiled=True).astype(F32)  183 us
    pallas_call x48, Pallas kernels, rows_dot(): pl.pallas_call(functools.partial(rows_kernel, dims, len(parts), len(extra...  167 us
    pallas_call x16, Pallas kernels, local_call(): pl.pallas_call(kernel, grid_spec=spec, out_shape=out_shape, compiler_para...  161 us
    ppermute x16, waiting for transfers between devices, link_swap(): return lax.ppermute(values, ('dp', 'gx'), pairs)  144 us
    unnamed x474, local copies, waits for them, and re-layouts  143 us
    ppermute x48, waiting for transfers between devices, core_swap(): return lax.ppermute(values, 'gx', [(0, 1), (1, 0)])  85.4 us
    pallas_call x4, Pallas kernels, attend_back(): pl.pallas_call(functools.partial(bwd_waiting, heads, len(after)), grid_sp...  77.1 us
  transfers between devices with their start and end apart: 102, of which 72 were waited for; matrix products, arithmetic and copies ran while one was open for 7% of the time, Pallas kernels for 32%

profile of v4, /device:TPU:0, one launch (start us, length us, event | category | flops | bytes accessed | tf_op | source)
XLA Modules:
  0.0 1574.6 jit_solution(2380387326435251279)
XLA Ops:
  28.1 34.0 %all-gather.17.cloned.1.call-done.refs_0_ = bf16[1024,1024]{1,0:T(8,128)(2,1)} async-done(((bf16[256,1024]{1,0:T(8,128)(2,1)}), bf16[1024,1024]{1,0:T(8,128)(2,1)}) %all-gather.17.cloned.1.call-update) | async-done | bytes 2097168 | tf_op jit(solution)/shard_map/all_gather | solution.py:313
  71.9 19.2 %shard_map.222 = (bf16[1024,256]{1,0:T(8,128)(2,1)}, f32[8,1024]{1,0:T(8,128)S(1)}) custom-call(s32[2,4]{1,0:T(2,128)S(1)} %pad_add_fusion.span.refs_0_, s32[1,1024]{1,0:T(1,128)S(1)} %get-tuple-element.305.segr.refs_1_, s32[1024,1]{1,0:T(8,128)S(1)} %compare_select_fusion.1.segc.refs_2_, ...), custom_call_target="tpu_custom_call" | custom-call | tf_op jit(solution)/shard_map/pallas_call | solution.py:236
  170.4 30.1 %reduce-scatter.18.cloned.1.call-done = bf16[256,1024]{1,0:T(8,128)(2,1)} async-done(((bf16[1024,1024]{1,0:T(8,128)(2,1)}), bf16[256,1024]{1,0:T(8,128)(2,1)}) %reduce-scatter.18.cloned.1.call-update) | async-done | bytes 524304 | tf_op jit(solution)/shard_map/reduce_scatter | solution.py:317
  207.8 40.0 %all-gather.21.cloned.1.call-done.refs_0_ = bf16[1024,1024]{1,0:T(8,128)(2,1)} async-done(((bf16[256,1024]{1,0:T(8,128)(2,1)}), bf16[1024,1024]{1,0:T(8,128)(2,1)}) %all-gather.21.cloned.1.call-update) | async-done | bytes 2097168 | tf_op jit(solution)/shard_map/all_gather | solution.py:313
  323.7 20.4 %reduce-scatter.20.cloned.1.call-done = bf16[256,1024]{1,0:T(8,128)(2,1)} async-done(((bf16[1024,1024]{1,0:T(8,128)(2,1)}), bf16[256,1024]{1,0:T(8,128)(2,1)}) %reduce-scatter.20.cloned.1.call-update) | async-done | bytes 524304 | tf_op jit(solution)/shard_map/reduce_scatter | solution.py:317
  347.7 42.6 %reduce-scatter.22.cloned.1.call-done = bf16[256,1024]{1,0:T(8,128)(2,1)} async-done(((bf16[1024,1024]{1,0:T(8,128)(2,1)}), bf16[256,1024]{1,0:T(8,128)(2,1)}) %reduce-scatter.22.cloned.1.call-update) | async-done | bytes 524304 | tf_op jit(solution)/shard_map/reduce_scatter | solution.py:317
  400.2 37.6 %all-gather.25.cloned.1.call-done.refs_0_ = bf16[1024,1024]{1,0:T(8,128)(2,1)} async-done(((bf16[256,1024]{1,0:T(8,128)(2,1)}), bf16[1024,1024]{1,0:T(8,128)(2,1)}) %all-gather.25.cloned.1.call-update) | async-done | bytes 2097168 | tf_op jit(solution)/shard_map/all_gather | solution.py:313
  447.5 18.5 %shard_map.236 = (bf16[1024,256]{1,0:T(8,128)(2,1)S(1)}, f32[8,1024]{1,0:T(8,128)S(1)}) custom-call(s32[2,4]{1,0:T(2,128)S(1)} %pad_add_fusion.span.refs_0_, s32[1,1024]{1,0:T(1,128)S(1)} %get-tuple-element.305.segr.refs_1_, s32[1024,1]{1,0:T(8,128)S(1)} %copy-done.93, bf16[1024,768]{1,0:T(8,128)(2,1)S(1)} %shard_map.235.q_ref.k_ref.v_ref.refs_3_.refs_4_.refs_5_, ...), custom_call_target="tpu_custom_call" | custom-call | tf_op jit(solution)/shard_map/pallas_call | solution.py:236
  537.2 38.7 %reduce-scatter.26.cloned.1.call-done = bf16[256,1024]{1,0:T(8,128)(2,1)} async-done(((bf16[1024,1024]{1,0:T(8,128)(2,1)}), bf16[256,1024]{1,0:T(8,128)(2,1)}) %reduce-scatter.26.cloned.1.call-update) | async-done | bytes 524304 | tf_op jit(solution)/shard_map/reduce_scatter | solution.py:317
  586.7 36.7 %all-gather.29.cloned.1.call-done.refs_0_ = bf16[1024,1024]{1,0:T(8,128)(2,1)} async-done(((bf16[256,1024]{1,0:T(8,128)(2,1)}), bf16[1024,1024]{1,0:T(8,128)(2,1)}) %all-gather.29.cloned.1.call-update) | async-done | bytes 2097168 | tf_op jit(solution)/shard_map/all_gather | solution.py:313
  632.6 37.4 %all-gather.31.cloned.1.call-done.refs_0_.refs_1_ = bf16[1024,1024]{1,0:T(8,128)(2,1)} async-done(((bf16[256,1024]{1,0:T(8,128)(2,1)}), bf16[1024,1024]{1,0:T(8,128)(2,1)}) %all-gather.31.cloned.1.call-update) | async-done | bytes 2097168 | tf_op jit(solution)/shard_map/all_gather | solution.py:313
  692.0 24.7 %all-gather.33.cloned.1.call-done.refs_0_.refs_6_ = bf16[1024,1024]{1,0:T(8,128)(2,1)} async-done(((bf16[256,1024]{1,0:T(8,128)(2,1)}), bf16[1024,1024]{1,0:T(8,128)(2,1)}) %all-gather.33.cloned.1.call-update) | async-done | bytes 2097168 | tf_op jit(solution)/shard_map/all_gather | solution.py:313
  733.3 29.5 %all-gather.35.cloned.1.call-done.refs_0_.refs_7_ = bf16[1024,1024]{1,0:T(8,128)(2,1)} async-done(((bf16[256,1024]{1,0:T(8,128)(2,1)}), bf16[1024,1024]{1,0:T(8,128)(2,1)}) %all-gather.35.cloned.1.call-update) | async-done | bytes 2097168 | tf_op jit(solution)/shard_map/all_gather | solution.py:313
  800.0 31.8 %shard_map.252 = (bf16[512,3840]{1,0:T(8,128)(2,1)}, bf16[512,3840]{1,0:T(8,128)(2,1)}) custom-call(s32[1]{0:T(128)} %bitcast.40.mine, bf16[1024,1024]{1,0:T(8,128)(2,1)} %all-gather.29.cloned.1.call-done.refs_0_, bf16[1024,1024]{1,0:T(8,128)(2,1)} %all-gather.31.cloned.1.call-done.refs_0_.refs_1_, bf16[1024,1280]{1,0:T(8,128)(2,1)} %shard_map.245.refs_0_.refs_2_, ...), custom_call_target="tpu_custom_call" | custom-call | tf_op jit(solution)/shard_map/pallas_call | solution.py:464
  910.5 20.2 %shard_map.256 = (bf16[1024,256]{1,0:T(8,128)(2,1)S(1)}, bf16[1024,256]{1,0:T(8,128)(2,1)S(1)}, bf16[1024,256]{1,0:T(8,128)(2,1)S(1)}, f32[4,8,512]{2,1,0:T(8,128)S(1)}) custom-call(s32[2,4]{1,0:T(2,128)S(1)} %pad_add_fusion.span.refs_0_, s32[1,1024]{1,0:T(1,128)S(1)} %get-tuple-element.305.segr.refs_1_, s32[1024,1]{1,0:T(8,128)S(1)} %copy-done.94, ...), custom_call_target="tpu_custom_call" | custom-call | tf_op jit(solution)/shard_map/pallas_call | solution.py:269
  957.1 17.9 %shard_map.262 = (bf16[1024,256]{1,0:T(8,128)(2,1)S(1)}, bf16[1024,256]{1,0:T(8,128)(2,1)S(1)}, bf16[1024,256]{1,0:T(8,128)(2,1)S(1)}, f32[4,8,512]{2,1,0:T(8,128)S(1)}) custom-call(s32[2,4]{1,0:T(2,128)S(1)} %pad_add_fusion.1.span.refs_0_, s32[1,1024]{1,0:T(1,128)S(1)} %get-tuple-element.309.segr.refs_1_, s32[1024,1]{1,0:T(8,128)S(1)} %copy-done.90, ...), custom_call_target="tpu_custom_call" | custom-call | tf_op jit(solution)/shard_map/pallas_call | solution.py:269
  997.3 21.9 %shard_map.266 = (bf16[512,2048]{1,0:T(8,128)(2,1)}, bf16[512,2048]{1,0:T(8,128)(2,1)}) custom-call(s32[1]{0:T(128)} %bitcast.40.mine, bf16[1024,1024]{1,0:T(8,128)(2,1)} %all-gather.25.cloned.1.call-done.refs_0_, bf16[1024,1024]{1,0:T(8,128)(2,1)} %all-gather.37.cloned.1.call-done.refs_0_.refs_1_, bf16[1024,768]{1,0:T(8,128)(2,1)} %copy-done.86, ...), custom_call_target="tpu_custom_call" | custom-call | tf_op jit(solution)/shard_map/pallas_call | solution.py:464
  1044.1 19.7 %collective-permute-done.40.come = bf16[512,2048]{1,0:T(8,128)(2,1)} collective-permute-done((bf16[512,2048]{1,0:T(8,128)(2,1)}, bf16[512,2048]{1,0:T(8,128)(2,1)}, u32[]{:S(2)}, u32[]{:S(2)}) %collective-permute-start.40) | collective-permute-done | bytes 2097184 | tf_op jit(solution)/shard_map/ppermute | solution.py:648
  1186.6 32.1 %shard_map.277 = (bf16[512,3840]{1,0:T(8,128)(2,1)}, bf16[512,3840]{1,0:T(8,128)(2,1)}) custom-call(s32[1]{0:T(128)} %bitcast.40.mine, bf16[1024,1024]{1,0:T(8,128)(2,1)} %all-gather.21.cloned.1.call-done.refs_0_, bf16[1024,1024]{1,0:T(8,128)(2,1)} %all-gather.41.cloned.1.call-done.refs_0_.refs_1_, bf16[1024,1280]{1,0:T(8,128)(2,1)} %copy-done.47, ...), custom_call_target="tpu_custom_call" | custom-call | tf_op jit(solution)/shard_map/pallas_call | solution.py:464
  1232.4 32.3 %collective-permute-done.49.come = bf16[512,3840]{1,0:T(8,128)(2,1)} collective-permute-done((bf16[512,3840]{1,0:T(8,128)(2,1)}, bf16[512,3840]{1,0:T(8,128)(2,1)}, u32[]{:S(2)}, u32[]{:S(2)}) %collective-permute-start.49) | collective-permute-done | bytes 3932192 | tf_op jit(solution)/shard_map/ppermute | solution.py:648
  1283.4 21.0 %shard_map.281 = (bf16[1024,256]{1,0:T(8,128)(2,1)S(1)}, bf16[1024,256]{1,0:T(8,128)(2,1)S(1)}, bf16[1024,256]{1,0:T(8,128)(2,1)S(1)}, f32[4,8,512]{2,1,0:T(8,128)S(1)}) custom-call(s32[2,4]{1,0:T(2,128)S(1)} %pad_add_fusion.span.refs_0_, s32[1,1024]{1,0:T(1,128)S(1)} %get-tuple-element.305.segr.refs_1_, s32[1024,1]{1,0:T(8,128)S(1)} %copy-done.95, ...), custom_call_target="tpu_custom_call" | custom-call | tf_op jit(solution)/shard_map/pallas_call | solution.py:269
  1351.2 17.9 %shard_map.288 = (bf16[1024,256]{1,0:T(8,128)(2,1)S(1)}, bf16[1024,256]{1,0:T(8,128)(2,1)S(1)}, bf16[1024,256]{1,0:T(8,128)(2,1)S(1)}, f32[4,8,512]{2,1,0:T(8,128)S(1)}) custom-call(s32[2,4]{1,0:T(2,128)S(1)} %pad_add_fusion.1.span.refs_0_, s32[1,1024]{1,0:T(1,128)S(1)} %get-tuple-element.309.segr.refs_1_, s32[1024,1]{1,0:T(8,128)S(1)} %copy-done.91, ...), custom_call_target="tpu_custom_call" | custom-call | tf_op jit(solution)/shard_map/pallas_call | solution.py:269
  1401.9 22.0 %shard_map.292 = (bf16[512,2048]{1,0:T(8,128)(2,1)}, bf16[512,2048]{1,0:T(8,128)(2,1)}) custom-call(s32[1]{0:T(128)} %bitcast.40.mine, bf16[1024,1024]{1,0:T(8,128)(2,1)} %all-gather.17.cloned.1.call-done.refs_0_, bf16[1024,1024]{1,0:T(8,128)(2,1)} %all-gather.45.cloned.1.call-done.refs_0_.refs_1_, bf16[1024,768]{1,0:T(8,128)(2,1)} %copy-done.85, ...), custom_call_target="tpu_custom_call" | custom-call | tf_op jit(solution)/shard_map/pallas_call | solution.py:464
  1440.0 24.8 %collective-permute-done.66.come = bf16[512,2048]{1,0:T(8,128)(2,1)S(1)} collective-permute-done((bf16[512,2048]{1,0:T(8,128)(2,1)}, bf16[512,2048]{1,0:T(8,128)(2,1)S(1)}, u32[]{:S(2)}, u32[]{:S(2)}) %collective-permute-start.66) | collective-permute-done | bytes 2097184 | tf_op jit(solution)/shard_map/ppermute | solution.py:648
  (910 shorter events, 886.0 us)
Async XLA Ops:
  23.4 131.1 %reduce-scatter.16.cloned.1.call-start = ((), (), s32[]{:S(2)}) async-start(), calls=%async_computation.16 | async-start | bytes 2621440 | tf_op jit(solution)/shard_map/reduce_scatter | solution.py:317
  143.8 104.0 %all-gather.21.cloned.1.call-start = ((), (), s32[]{:S(2)}) async-start(), calls=%async_computation.18 | async-start | bytes 2621440 | tf_op jit(solution)/shard_map/all_gather | solution.py:313
  158.1 140.6 %all-gather.23.cloned.1.call-start = ((), (), s32[]{:S(2)}) async-start(), calls=%async_computation.21 | async-start | bytes 2621440 | tf_op jit(solution)/shard_map/all_gather | solution.py:313
  283.3 107.0 %reduce-scatter.22.cloned.1.call-start = ((), (), s32[]{:S(2)}) async-start(), calls=%async_computation.23 | async-start | bytes 2621440 | tf_op jit(solution)/shard_map/reduce_scatter | solution.py:317
  323.6 114.1 %all-gather.25.cloned.1.call-start = ((), (), s32[]{:S(2)}) async-start(), calls=%async_computation.22 | async-start | bytes 2621440 | tf_op jit(solution)/shard_map/all_gather | solution.py:313
  347.7 136.8 %all-gather.27.cloned.1.call-start = ((), (), s32[]{:S(2)}) async-start(), calls=%async_computation.25 | async-start | bytes 2621440 | tf_op jit(solution)/shard_map/all_gather | solution.py:313
  393.9 135.9 %reduce-scatter.24.cloned.1.call-start = ((), (), s32[]{:S(2)}) async-start(), calls=%async_computation.24 | async-start | bytes 2621440 | tf_op jit(solution)/shard_map/reduce_scatter | solution.py:317
  473.7 102.2 %reduce-scatter.26.cloned.1.call-start = ((), (), s32[]{:S(2)}) async-start(), calls=%async_computation.27 | async-start | bytes 2621440 | tf_op jit(solution)/shard_map/reduce_scatter | solution.py:317
  516.9 106.4 %all-gather.29.cloned.1.call-start = ((), (), s32[]{:S(2)}) async-start(), calls=%async_computation.26 | async-start | bytes 2621440 | tf_op jit(solution)/shard_map/all_gather | solution.py:313
  534.6 135.4 %all-gather.31.cloned.1.call-start = ((), (), s32[]{:S(2)}) async-start(), calls=%async_computation.28 | async-start | bytes 2621440 | tf_op jit(solution)/shard_map/all_gather | solution.py:313
  537.2 179.5 %all-gather.33.cloned.1.call-start = ((), (), s32[]{:S(2)}) async-start(), calls=%async_computation.30 | async-start | bytes 2621440 | tf_op jit(solution)/shard_map/all_gather | solution.py:313
  580.7 182.1 %all-gather.35.cloned.1.call-start = ((), (), s32[]{:S(2)}) async-start(), calls=%async_computation.31 | async-start | bytes 2621440 | tf_op jit(solution)/shard_map/all_gather | solution.py:313
  676.2 157.0 %reduce-scatter.28.cloned.1.call-start = ((), (), s32[]{:S(2)}) async-start(), calls=%async_computation.29 | async-start | bytes 2621440 | tf_op jit(solution)/shard_map/reduce_scatter | solution.py:317
  733.2 120.8 %reduce-scatter.30.cloned.1.call-start = ((), (), s32[]{:S(2)}) async-start(), calls=%async_computation.33 | async-start | bytes 2621440 | tf_op jit(solution)/shard_map/reduce_scatter | solution.py:317
  794.1 107.4 %all-gather.37.cloned.1.call-start = ((), (), s32[]{:S(2)}) async-start(), calls=%async_computation.32 | async-start | bytes 2621440 | tf_op jit(solution)/shard_map/all_gather | solution.py:313
  838.8 110.9 %all-gather.39.cloned.1.call-start = ((), (), s32[]{:S(2)}) async-start(), calls=%async_computation.35 | async-start | bytes 2621440 | tf_op jit(solution)/shard_map/all_gather | solution.py:313
  885.7 133.6 %reduce-scatter.32.cloned.1.call-start = ((), (), s32[]{:S(2)}) async-start(), calls=%async_computation.34 | async-start | bytes 2621440 | tf_op jit(solution)/shard_map/reduce_scatter | solution.py:317
  1023.5 113.2 %all-gather.43.cloned.1.call-start = ((), (), s32[]{:S(2)}) async-start(), calls=%async_computation.39 | async-start | bytes 2621440 | tf_op jit(solution)/shard_map/all_gather | solution.py:313
  1091.8 128.4 %reduce-scatter.36.cloned.1.call-start = ((), (), s32[]{:S(2)}) async-start(), calls=%async_computation.38 | async-start | bytes 2621440 | tf_op jit(solution)/shard_map/reduce_scatter | solution.py:317
  1121.5 106.7 %reduce-scatter.38.cloned.1.call-start = ((), (), s32[]{:S(2)}) async-start(), calls=%async_computation.41 | async-start | bytes 2621440 | tf_op jit(solution)/shard_map/reduce_scatter | solution.py:317
  1165.9 109.6 %all-gather.45.cloned.1.call-start = ((), (), s32[]{:S(2)}) async-start(), calls=%async_computation.40 | async-start | bytes 2621440 | tf_op jit(solution)/shard_map/all_gather | solution.py:313
  1272.7 230.2 %reduce-scatter.42.cloned.1.call-start = ((), (), s32[]{:S(2)}) async-start(), calls=%async_computation.44 | async-start | bytes 2621440 | tf_op jit(solution)/shard_map/reduce_scatter | solution.py:317
  1341.3 175.9 %reduce-scatter.44.cloned.1.call-start = ((), (), s32[]{:S(2)}) async-start(), calls=%async_computation.45 | async-start | bytes 2621440 | tf_op jit(solution)/shard_map/reduce_scatter | solution.py:317
  1401.6 162.1 %reduce-scatter.40.cloned.1.call-start = ((), (), s32[]{:S(2)}) async-start(), calls=%async_computation.43 | async-start | bytes 5242880 | tf_op jit(solution)/shard_map/reduce_scatter | solution.py:317
  (310 other events, 3530.0 us)
Sparse Core Ops, SparseCore 0:
  13.5 48.6 all-gather.16
  64.3 44.6 all-gather.18
  157.3 43.1 reduce-scatter.17
  202.5 45.2 all-gather.20
  253.8 44.7 all-gather.22
  347.1 43.1 reduce-scatter.21
  392.5 45.2 all-gather.24
  439.7 44.6 all-gather.26
  532.7 43.1 reduce-scatter.25
  578.0 45.2 all-gather.28
  625.3 44.6 all-gather.30
  672.0 44.6 all-gather.32
  718.1 44.6 all-gather.34
  810.9 43.1 reduce-scatter.29
  856.2 45.3 all-gather.36
  903.0 44.6 all-gather.38
  996.1 43.1 reduce-scatter.33
  1041.4 44.8 all-gather.40
  1091.9 44.7 all-gather.42
  1139.6 42.5 reduce-scatter.35
  1185.0 43.1 reduce-scatter.37
  1230.2 45.2 all-gather.44
  1277.6 44.6 all-gather.46
  1446.6 76.0 reduce-scatter.39
  (7 shorter events, 296.2 us)
